TPU v7x, 32 devices: a whole 2x2x4 slice. The times are simulated.
32 devices in a mesh: role: 4 (over y, core), seq: 2 (over x), mp: 4 (over z).
Axes of the slice: x: 2, y: 2, z: 4, core: 2. Of those that a mesh axis runs over, the one named last changes fastest.
Arguments:
- gen_heads: bfloat16 [128, 4096], P(None, 'seq'), may hold values from -6 to 6
- gen_resid: bfloat16 [128, 5120], P('seq', 'mp'), may hold values from -6 to 6
- gen_out_w: bfloat16 [4096, 5120], P('seq', 'mp'), may hold values from -0.09375 to 0.09375
- gen_time_w: bfloat16 [256, 5120], P(None, 'mp'), may hold values from -0.375 to 0.375
- noise: bfloat16 [128, 5120], P('seq', 'mp'), may hold values from -6 to 6
- steps: int32 [3], replicated, may hold values from 20 to 979
- teacher_qkv: bfloat16 [5120, 3, 4096], P('mp', None, 'seq'), may hold values from -0.078125 to 0.078125
- teacher_out: bfloat16 [4096, 5120], P('seq', 'mp'), may hold values from -0.09375 to 0.09375
- teacher_time: bfloat16 [256, 3, 5120], P(None, None, 'mp'), may hold values from -0.375 to 0.375
- teacher_norm: float32 [2, 4096], P(None, 'seq'), may hold values from 0.5 to 1.5
- critic_qkv: bfloat16 [5120, 3, 4096], P('mp', None, 'seq'), may hold values from -0.078125 to 0.078125
- critic_out: bfloat16 [4096, 5120], P('seq', 'mp'), may hold values from -0.09375 to 0.09375
- critic_time: bfloat16 [256, 3, 5120], P(None, None, 'mp'), may hold values from -0.375 to 0.375
- critic_norm: float32 [2, 4096], P(None, 'seq'), may hold values from 0.5 to 1.5
Outputs:
- latent: bfloat16 [128, 5120], P('seq', 'mp')
- weight_grad: bfloat16 [4096, 5120], P('seq', 'mp')
All inputs are finite; a program needn't handle non-finite values.
Results may differ from a plain program's by a relative error of at most 0.012.
Values may be sent and summed in bfloat16 or wider, within the bound.
No kernel may reach another device: no remote copies, remote signals or barrier semaphores. Data moves between devices by JAX's collectives and lax.ppermute only.
A program may use at most 128 MiB of HBM per device.

v0:
```python
import math

import jax
import jax.numpy as jnp
from jax import lax
from jax.sharding import PartitionSpec as P

D = 5120
HEAD_DIM = 128


def time_embed(step_value, width):
    half_width = width // 2
    positions = jnp.arange(half_width, dtype=jnp.float32)
    frequencies = jnp.exp(positions * (-math.log(10000.0) / half_width))
    angles = step_value.astype(jnp.float32) * frequencies
    return jnp.concatenate([jnp.cos(angles), jnp.sin(angles)]).astype(jnp.bfloat16)


def head_norm(values, gains):
    factor = lax.rsqrt(jnp.mean(values * values, axis=-1, keepdims=True) + 1e-06)
    return (values * factor * gains).astype(jnp.bfloat16)


def attend(query_norm, key_norm, value_rows):
    full_length, heads_here, head_width = query_norm.shape
    query_blocks = query_norm.reshape(
        full_length // full_length, full_length, heads_here, head_width
    )

    def one_block(query_block):
        logits = jnp.einsum(
            "qhd,khd->hqk", query_block, key_norm, preferred_element_type=jnp.float32
        ) * (1.0 / math.sqrt(head_width))
        expanded = jnp.exp(logits)
        probs = (expanded / jnp.sum(expanded, axis=2, keepdims=True)).astype(jnp.bfloat16)
        return jnp.einsum(
            "hqk,khd->qhd", probs, value_rows, preferred_element_type=jnp.float32
        ).astype(jnp.bfloat16)

    head_out = lax.map(one_block, query_blocks)
    return head_out.reshape(full_length, heads_here * head_width)


def on_device(
    gen_heads,
    gen_resid,
    gen_out_w,
    gen_time_w,
    noise,
    steps,
    teacher_qkv,
    teacher_out,
    teacher_time,
    teacher_norm,
    critic_qkv,
    critic_out,
    critic_time,
    critic_norm,
):
    full_length = gen_heads.shape[0]
    head_cols = gen_heads.shape[1]
    embed_width = gen_time_w.shape[0]
    gen_gate = jnp.dot(
        time_embed(steps[0], embed_width)[None, :], gen_time_w, preferred_element_type=jnp.float32
    )[0]
    block = gen_heads
    gen_proj = lax.psum_scatter(
        jnp.dot(block, gen_out_w, preferred_element_type=jnp.float32),
        "seq",
        scatter_dimension=0,
        tiled=True,
    )
    latent = (gen_resid.astype(jnp.float32) + gen_gate * gen_proj).astype(jnp.bfloat16)
    role_index = lax.axis_index("role")
    level = steps[1 + role_index // 2]
    use_critic = role_index % 2 == 1
    w_qkv = jnp.where(use_critic, critic_qkv, teacher_qkv)
    w_out = jnp.where(use_critic, critic_out, teacher_out)
    w_time = jnp.where(use_critic, critic_time, teacher_time)
    w_norm = jnp.where(use_critic, critic_norm, teacher_norm)
    noise_level = level.astype(jnp.float32) / 1000.0
    noisy = (
        (1.0 - noise_level) * latent.astype(jnp.float32) + noise_level * noise.astype(jnp.float32)
    ).astype(jnp.bfloat16)
    modulation = jnp.einsum(
        "f,fkd->kd", time_embed(level, embed_width), w_time, preferred_element_type=jnp.float32
    )
    shift_vec = modulation[0]
    scale_vec = modulation[1]
    gate_vec = modulation[2]
    gathered = lax.all_gather(noisy, "seq", axis=0, tiled=True)
    partial_squares = jnp.sum(jnp.square(gathered.astype(jnp.float32)), axis=1)
    scaled = (gathered.astype(jnp.float32) * (1.0 + scale_vec)).astype(jnp.bfloat16)
    flat_w = w_qkv.reshape(w_qkv.shape[0], 3 * head_cols)
    projected = jnp.dot(scaled, flat_w, preferred_element_type=jnp.float32)
    shift_proj = jnp.dot(
        shift_vec.astype(jnp.bfloat16)[None, :], flat_w, preferred_element_type=jnp.float32
    )[0]
    projected, squares, shift_proj = lax.psum((projected, partial_squares, shift_proj), "mp")
    mixed = projected * lax.rsqrt(squares / D + 1e-06)[:, None] + shift_proj
    heads_here = head_cols // HEAD_DIM
    mixed = mixed.reshape(full_length, 3, heads_here, HEAD_DIM)
    gains = w_norm.reshape(2, heads_here, HEAD_DIM)
    query_norm = head_norm(mixed[:, 0], gains[0])
    key_norm = head_norm(mixed[:, 1], gains[1])
    value_rows = mixed[:, 2].astype(jnp.bfloat16)
    head_out = attend(query_norm, key_norm, value_rows)
    weight_sign = jnp.where(use_critic, 0.5, -0.5)
    block = head_out
    summed_rows = lax.psum_scatter(
        weight_sign * (gate_vec * jnp.dot(block, w_out, preferred_element_type=jnp.float32)),
        ("role", "seq"),
        scatter_dimension=0,
        tiled=True,
    )
    grad_rows = lax.all_gather(
        (gen_gate * summed_rows).astype(jnp.bfloat16), ("role", "seq"), axis=0, tiled=True
    )
    weight_grad = lax.dot_general(
        gen_heads, grad_rows, (((0,), (0,)), ((), ())), preferred_element_type=jnp.float32
    )
    return (latent, weight_grad.astype(jnp.bfloat16))


def solution(mesh):
    in_specs = (
        P(None, "seq"),
        P("seq", "mp"),
        P("seq", "mp"),
        P(None, "mp"),
        P("seq", "mp"),
        P(),
        P("mp", None, "seq"),
        P("seq", "mp"),
        P(None, None, "mp"),
        P(None, "seq"),
        P("mp", None, "seq"),
        P("seq", "mp"),
        P(None, None, "mp"),
        P(None, "seq"),
    )
    out_specs = (P("seq", "mp"), P("seq", "mp"))
    return jax.shard_map(
        on_device, mesh=mesh, in_specs=in_specs, out_specs=out_specs, check_vma=False
    )
```

profile of v0, /device:TPU:1, one launch (start us, length us, event | category | flops | bytes accessed | tf_op | source)
XLA Modules:
  0.0 298.8 jit_solution(10533154245719186183)
XLA Ops:
  7.2 0.0 copy-start
  7.2 0.0 reduce-scatter.3.cloned.1.call-start
  7.2 4.4 %fusion.37 = f32[128,1280]{1,0:T(8,128)} fusion(bf16[128,2048]{1,0:T(8,128)(2,1)} %param.14, bf16[2048,1280]{1,0:T(8,128)(2,1)} %param.16), kind=kOutput, calls=%fused_computation.63 | convolution fusion | flops 671088640 | bytes 6422528 | tf_op jit(solution)/shard_map/dot_general | solution.py:69
  11.6 0.0 reduce-scatter.3.cloned.1.call-update
  11.6 0.0 all-reduce.3.cloned.1.call-start
  11.7 20.9 %copy.21 = bf16[1280,3,2048]{0,2,1:T(8,128)(2,1)} copy(bf16[1280,3,2048]{2,0,1:T(8,128)(2,1)} %param.24) | data formatting | bytes 31457280 | tf_op args[10]
  32.7 21.0 %copy.22 = bf16[1280,3,2048]{0,2,1:T(8,128)(2,1)} copy(bf16[1280,3,2048]{2,0,1:T(8,128)(2,1)} %param.20) | data formatting | bytes 31457280 | tf_op args[6]
  53.6 0.0 copy-start.8
  53.6 0.0 copy-start.3
  53.6 0.0 copy-start.4
  53.6 0.0 copy-start.5
  53.6 13.7 %broadcast_select_fusion = bf16[1280,3,2048]{0,2,1:T(8,128)(2,1)} fusion(bf16[1280,3,2048]{0,2,1:T(8,128)(2,1)} %copy.21, bf16[1280,3,2048]{0,2,1:T(8,128)(2,1)} %copy.22, pred[]{:T(512)S(6)} %eq.5), kind=kLoop, calls=%fused_computation | loop fusion | flops 7864320 | bytes 47185920 | tf_op jit(solution)/shard_map/jit(_where)/select_n | solution.py:78
  67.3 0.0 copy-done.8
  67.3 0.7 fusion.36
  68.7 0.1 sine_convert_fusion.1
  69.4 0.1 sine_convert_fusion
  69.5 0.0 copy-done.3
  69.5 0.6 fusion.10
  70.1 0.0 copy-done
  70.2 0.2 convolution_reduce_fusion
  70.4 0.0 reduce-scatter.3.cloned.1.call-done
  70.4 0.0 copy-done.4
  70.4 0.0 copy-done.5
  70.4 1.7 add_convert_fusion
  72.2 5.4 %all_gather.6 = bf16[128,1280]{1,0:T(8,128)(2,1)S(1)} all-gather(bf16[64,1280]{1,0:T(8,128)(2,1)S(1)} %get-tuple-element.25), channel_id=1, replica_groups=mesh['role'=4,'seq'=2,'mp'=4] {'seq'}, dimensions={0}, use_global_device_ids=true | all-gather | bytes 491520 | tf_op jit(solution)/shard_map/all_gather | solution.py:92
  77.5 0.0 copy-start.6
  77.5 0.0 copy-start.7
  77.5 12.3 %fusion.24 = f32[128,6144]{1,0:T(8,128)} fusion(bf16[1280,6144]{0,1:T(8,128)(2,1)} %bitcast.49, bf16[128,1280]{1,0:T(8,128)(2,1)S(1)} %all_gather.6, f32[1280]{0:T(1024)S(1)} %get-tuple-element.22), kind=kOutput, calls=%fused_computation.34 | convolution fusion | flops 2013757440 | bytes 19207168 | tf_op jit(solution)/shard_map/dot_general | solution.py:96
  89.8 0.0 all-reduce.3.cloned.1.call-update
  89.9 0.0 reduce-scatter.5.cloned.1.call-start
  89.9 0.0 copy-done.6
  89.9 0.0 copy-done.7
  90.0 9.6 %fusion.28 = f32[1,6144]{1,0:T(1,128)S(1)} fusion(bf16[1280,6144]{0,1:T(8,128)(2,1)} %bitcast.50, f32[3,1280]{1,0:T(4,128)S(1)} %bitcast.54), kind=kOutput, calls=%fused_computation.45 | convolution fusion | flops 15728640 | bytes 15758336 | tf_op jit(solution)/shard_map/dot_general | solution.py:97
  99.6 0.2 fusion.15
  99.7 18.1 %all-reduce = (f32[6144]{0:T(1024)S(1)}, f32[128]{0:T(128)S(1)}) all-reduce(f32[6144]{0:T(1024)S(1)} %bitcast.55, f32[128]{0:T(128)S(1)} %fusion.15), channel_id=1, replica_groups=mesh['role'=4,'seq'=2,'mp'=4] {'mp'}, use_global_device_ids=true, to_apply=%region_4.5 | all-reduce | flops 6272 | bytes 50176 | tf_op jit(solution)/shard_map/psum | solution.py:100
  117.8 97.4 %all-reduce.3.cloned.1.call-done = f32[128,6144]{1,0:T(8,128)} async-done(((f32[128,6144]{1,0:T(8,128)}), f32[128,6144]{1,0:T(8,128)}) %all-reduce.3.cloned.1.call-update) | async-done | bytes 3145744 | tf_op jit(solution)/shard_map/psum | solution.py:100
  215.3 2.3 add_bitcast_fusion
  217.6 0.5 copy.33
  218.1 0.1 fusion.34
  218.3 0.1 slice.43
  218.3 0.4 multiply_reduce_fusion
  218.7 0.4 multiply_reduce_fusion.1
  219.1 0.5 copy.32
  219.6 2.3 fusion.13
  221.8 2.0 convolution_convert_fusion.1
  223.8 0.0 copy-start.2
  223.8 4.5 %fusion.7 = f32[128,1280]{1,0:T(8,128)} fusion(bf16[128,2048]{0,1:T(8,128)(2,1)S(1)} %bitcast.58, bf16[2048,1280]{1,0:T(8,128)(2,1)} %param.25, bf16[2048,1280]{1,0:T(8,128)(2,1)} %param.21, pred[]{:T(512)S(6)} %eq.5, f32[1280]{0:T(1024)S(1)} %get-tuple-element.21, f32[]{:T(128)S(6)} %select_n.51), kind=kOutput, calls=%fused_computation.8 | convolution fusion | flops 674037760 | bytes 11670533 | tf_op jit(solution)/shard_map/dot_general | solution.py:112
  228.4 0.0 reduce-scatter.5.cloned.1.call-update
  228.4 33.3 %reduce-scatter.5.cloned.1.call-done = f32[16,1280]{1,0:T(8,128)} async-done(((f32[128,1280]{1,0:T(8,128)}), f32[16,1280]{1,0:T(8,128)}) %reduce-scatter.5.cloned.1.call-update) | async-done | bytes 81936 | tf_op jit(solution)/shard_map/reduce_scatter | solution.py:111
  261.7 0.9 multiply_convert_fusion.4
  262.6 17.9 %all_gather.7 = bf16[128,1280]{1,0:T(8,128)(2,1)S(1)} all-gather(bf16[16,1280]{1,0:T(8,128)(2,1)S(1)} %multiply_convert_fusion.4), channel_id=1, replica_groups=mesh['role'=4,'seq'=2,'mp'=4] {'role','seq'}, dimensions={0}, use_global_device_ids=true | all-gather | bytes 368640 | tf_op jit(solution)/shard_map/all_gather | solution.py:117
  280.5 0.0 copy-done.2
  280.5 0.0 copy-start.1
  280.5 3.9 %fusion = bf16[2048,1280]{0,1:T(8,128)(2,1)} fusion(bf16[128,1280]{1,0:T(8,128)(2,1)S(1)} %all_gather.7, bf16[128,2048]{1,0:T(8,128)(2,1)S(1)} %copy-done.2), kind=kOutput, calls=%fused_computation.2 | convolution fusion | flops 673710080 | bytes 6094848 | tf_op jit(solution)/shard_map/dot_general | solution.py:120
  284.4 7.9 %copy.27 = bf16[2048,1280]{1,0:T(8,128)(2,1)} copy(bf16[2048,1280]{0,1:T(8,128)(2,1)} %fusion) | data formatting | bytes 10485760
  292.2 0.0 copy-done.1
  (11 shorter events, 0.1 us)
Async XLA Ops:
  7.2 63.0 %copy-start = (bf16[256,1280]{1,0:T(8,128)(2,1)S(1)}, bf16[256,1280]{1,0:T(8,128)(2,1)}, u32[]{:S(2)}) copy-start(bf16[256,1280]{1,0:T(8,128)(2,1)} %param.17) | copy-start | bytes 1966084
  7.2 63.2 %reduce-scatter.3.cloned.1.call-start = ((), (), s32[]{:S(2)}) async-start(), calls=%async_computation.2 | async-start | bytes 983040 | tf_op jit(solution)/shard_map/reduce_scatter | solution.py:68
  11.6 203.6 %all-reduce.3.cloned.1.call-start = ((), (), s32[]{:S(2)}) async-start(), calls=%async_computation.3 | async-start | bytes 6291456 | tf_op jit(solution)/shard_map/psum | solution.py:100
  53.6 13.7 %copy-start.8 = (s32[3]{0:T(128)S(1)}, s32[3]{0:T(128)}, u32[]{:S(2)}) copy-start(s32[3]{0:T(128)} %param.19) | copy-start | bytes 40
  53.6 15.9 %copy-start.3 = (bf16[256,3,1280]{2,0,1:T(8,128)(2,1)S(1)}, bf16[256,3,1280]{2,0,1:T(8,128)(2,1)}, u32[]{:S(2)}) copy-start(bf16[256,3,1280]{2,0,1:T(8,128)(2,1)} %param.26) | copy-start | bytes 5898244
  53.6 16.8 %copy-start.4 = (bf16[64,1280]{1,0:T(8,128)(2,1)S(1)}, bf16[64,1280]{1,0:T(8,128)(2,1)}, u32[]{:S(2)}) copy-start(bf16[64,1280]{1,0:T(8,128)(2,1)} %param.18) | copy-start | bytes 491524
  53.6 16.8 %copy-start.5 = (bf16[64,1280]{1,0:T(8,128)(2,1)S(1)}, bf16[64,1280]{1,0:T(8,128)(2,1)}, u32[]{:S(2)}) copy-start(bf16[64,1280]{1,0:T(8,128)(2,1)} %param.15) | copy-start | bytes 491524
  77.5 12.4 %copy-start.6 = (f32[2,2048]{1,0:T(2,128)S(1)}, f32[2,2048]{1,0:T(2,128)}, u32[]{:S(2)}) copy-start(f32[2,2048]{1,0:T(2,128)} %param.27) | copy-start | bytes 49156
  77.5 12.4 %copy-start.7 = (f32[2,2048]{1,0:T(2,128)S(1)}, f32[2,2048]{1,0:T(2,128)}, u32[]{:S(2)}) copy-start(f32[2,2048]{1,0:T(2,128)} %param.23) | copy-start | bytes 49156
  89.9 171.9 %reduce-scatter.5.cloned.1.call-start = ((), (), s32[]{:S(2)}) async-start(), calls=%async_computation.4 | async-start | bytes 737280 | tf_op jit(solution)/shard_map/reduce_scatter | solution.py:111
  223.8 56.7 %copy-start.2 = (bf16[128,2048]{1,0:T(8,128)(2,1)S(1)}, bf16[128,2048]{1,0:T(8,128)(2,1)}, u32[]{:S(2)}) copy-start(bf16[128,2048]{1,0:T(8,128)(2,1)} %param.14) | copy-start | bytes 1572868
  280.5 11.7 %copy-start.1 = (bf16[256,1280]{1,0:T(8,128)(2,1)S(1)}, bf16[256,1280]{1,0:T(8,128)(2,1)}, u32[]{:S(2)}) copy-start(bf16[256,1280]{1,0:T(8,128)(2,1)} %param.17) | copy-start | bytes 1966084
Sparse Core Ops, SparseCore 0:
  11.8 18.0 reduce-scatter.2
  90.0 125.2 all-reduce.2
  228.5 33.1 reduce-scatter.4
where the time goes:
time: 300 us; the launch traced here: 299 us
  waiting for transfers between devices  131 us (44%)
  local copies, waits for them, and re-layouts  51.7 us (17%)
  blocking collectives  41.3 us (14%)
  matrix products  39.7 us (13%)
  other arithmetic  19.7 us (7%)
  between operations  15.3 us (5%)
    psum x1, waiting for transfers between devices, on_device(): lax.psum((projected, partial_squares, shift_proj), 'mp')  97.4 us
    unnamed x23, local copies, waits for them, and re-layouts  50.8 us
    reduce_scatter x1, waiting for transfers between devices, on_device(): lax.psum_scatter(weight_sign * (gate_vec * jnp.dot(block, w_out, preferre...  33.3 us
    psum x1, blocking collectives, on_device(): lax.psum((projected, partial_squares, shift_proj), 'mp')  18.1 us
    all_gather x1, blocking collectives, on_device(): lax.all_gather((gen_gate * summed_rows).astype(jnp.bfloat16), ('role', 's...  17.9 us
    select_n x1, other arithmetic, on_device(): w_qkv = jnp.where(use_critic, critic_qkv, teacher_qkv)  13.7 us
    dot_general x1, matrix products, on_device(): projected = jnp.dot(scaled, flat_w, preferred_element_type=jnp.float32)  12.3 us
    dot_general x1, matrix products, on_device(): jnp.dot(shift_vec.astype(jnp.bfloat16)[None, :], flat_w, preferred_elemen...  9.61 us
  transfers between devices with their start and end apart: 3, of which 2 were waited for; matrix products, arithmetic and copies ran while one was open for 22% of the time, Pallas kernels for 0%

commit v1 on v0

--- a/solution.py
+++ b/solution.py
@@ -3,6 +3,8 @@
 import jax
 import jax.numpy as jnp
 from jax import lax
+from jax.experimental import pallas as pl
+from jax.experimental.pallas import tpu as pltpu
 from jax.sharding import PartitionSpec as P
 
 D = 5120
@@ -42,7 +44,7 @@
     return head_out.reshape(full_length, heads_here * head_width)
 
 
-def on_device(
+def pass_per_role(
     gen_heads,
     gen_resid,
     gen_out_w,
@@ -122,6 +124,403 @@
     )
     return (latent, weight_grad.astype(jnp.bfloat16))
 
+MIB = 1024 * 1024
+EXTRA_ROWS = 16
+
+
+def vmem_spec():
+    return pl.BlockSpec(memory_space=pltpu.VMEM)
+
+
+def smem_spec():
+    return pl.BlockSpec(memory_space=pltpu.SMEM)
+
+
+def params(mebibytes):
+    return pltpu.CompilerParams(vmem_limit_bytes=mebibytes * MIB)
+
+
+def dot32(a, b):
+    return jnp.dot(a, b, preferred_element_type=jnp.float32)
+
+
+def at_block(index, size):
+    return pl.ds(pl.multiple_of(index * size, size), size)
+
+
+def gen_kernel(where, heads, weight, time_w, embed, resid, noise, full, sent):
+    step = pl.program_id(0)
+    length = full.shape[0]
+    own = resid.shape[0]
+
+    @pl.when(step == 0)
+    def _():
+        full[...] = jnp.zeros_like(full)
+
+    full[...] += dot32(heads[...], weight[...])
+
+    @pl.when(step == pl.num_programs(0) - 1)
+    def _():
+        full[...] = full[...] * dot32(embed[...], time_w[...])[0:1]
+        at = at_block(where[0], own)
+        full[at, :] = full[at, :] + resid[...].astype(jnp.float32)
+        sent[pl.ds(0, length), :] = full[...].astype(jnp.bfloat16)
+        sent[pl.ds(length, own), :] = noise[...]
+
+
+def gen_part(where, heads, weight, time_w, embed, resid, noise, steps):
+    length, depth = heads.shape
+    width = weight.shape[1] // 2
+    freq = time_w.shape[0]
+    own = resid.shape[0]
+    tile = depth // steps
+    grid_spec = pltpu.PrefetchScalarGridSpec(
+        num_scalar_prefetch=1,
+        grid=(steps,),
+        in_specs=[
+            pl.BlockSpec((length, tile), lambda n, w: (0, n)),
+            pl.BlockSpec((tile, width), lambda n, w: (n, w[1])),
+            pl.BlockSpec((freq, width), lambda n, w: (0, w[1])),
+            pl.BlockSpec((8, freq), lambda n, w: (0, 0)),
+            pl.BlockSpec((own, width), lambda n, w: (0, w[1])),
+            pl.BlockSpec((own, width), lambda n, w: (0, w[1])),
+        ],
+        out_specs=[
+            pl.BlockSpec((length, width), lambda n, w: (0, 0)),
+            pl.BlockSpec((length + own, width), lambda n, w: (0, 0)),
+        ],
+    )
+    return pl.pallas_call(
+        gen_kernel,
+        grid_spec=grid_spec,
+        out_shape=[
+            jax.ShapeDtypeStruct((length, width), jnp.float32),
+            jax.ShapeDtypeStruct((length + own, width), jnp.bfloat16),
+        ],
+        compiler_params=params(56),
+        name="gen_part",
+    )(where, heads, weight, time_w, embed, resid, noise)
+
+
+def mod_kernel(embed, time_a, time_b, time_w, mods, gate):
+    gate[...] = dot32(embed[...], time_w[...])
+    for k in range(3):
+        mods[0, k] = dot32(embed[...], time_a[k])
+        mods[1, k] = dot32(embed[...], time_b[k])
+
+
+def mod_part(embed, time_a, time_b, time_w):
+    width = time_a.shape[2]
+    return pl.pallas_call(
+        mod_kernel,
+        in_specs=[vmem_spec()] * 4,
+        out_specs=[vmem_spec()] * 2,
+        out_shape=[
+            jax.ShapeDtypeStruct((2, 3, 8, width), jnp.float32),
+            jax.ShapeDtypeStruct((8, width), jnp.float32),
+        ],
+        compiler_params=params(16),
+        name="mod_part",
+    )(embed, time_a, time_b, time_w)
+
+
+def project(index, mine, noisy, squares, mods, weight, kept, sent, result):
+    tokens = noisy.shape[0]
+    length = tokens // 2
+    unit = squares.shape[1] // 2
+    groups = weight.shape[2] // unit
+    scale = mods[index, 1]
+    shift = mods[index, 0]
+    spread = noisy.astype(jnp.float32)
+    top = spread[:length] * (1.0 + scale[1:2])
+    low = spread[length:] * (1.0 + scale[2:3])
+    extra = jnp.concatenate([shift[1:3], jnp.zeros((EXTRA_ROWS - 2, shift.shape[1]), jnp.float32)], axis=0)
+    rows = jnp.concatenate([top, low, extra], axis=0).astype(jnp.bfloat16)
+    row_id = lax.broadcasted_iota(jnp.int32, (EXTRA_ROWS, unit), 0)
+    for part in range(3):
+        result[...] = dot32(rows, weight[part])
+        cols = pl.ds(part * unit, unit)
+        for slot in range(groups):
+            at = at_block(jnp.bitwise_xor(mine, slot), unit)
+            goal = sent if slot % 2 else kept
+            for level in range(2):
+                goal[level][slot // 2, pl.ds(0, length), cols] = result[pl.ds(level * length, length), at].astype(
+                    jnp.bfloat16
+                )
+                tail = jnp.where(row_id == 0, result[pl.ds(tokens + level, 1), at], 0.0)
+                tail = jnp.where(row_id == 1, squares[0:1, level * length : (level + 1) * length], tail)
+                goal[level][slot // 2, pl.ds(length, EXTRA_ROWS), cols] = tail.astype(jnp.bfloat16)
+
+
+def first_kernel(where, levels, half, swapped, arrived, noise, mods, weight, *refs):
+    latent, noisy, squares, kept_a, kept_b, sent_a, sent_b, values, noises, result = refs
+    length, cols = half.shape
+    own = latent.shape[0]
+    tokens = 2 * length
+    seq, core, mine = where[0], where[1], where[2]
+    values[:, at_block(core, cols)] = half[...]
+    values[:, at_block(1 - core, cols)] = swapped[pl.ds(0, length), :]
+    latent[...] = values[at_block(seq, own), :]
+    noises[at_block(seq, own), :] = noise[...]
+    theirs = at_block(1 - seq, own)
+    noises[theirs, at_block(core, cols)] = arrived[pl.ds(length, own), :]
+    noises[theirs, at_block(1 - core, cols)] = swapped[pl.ds(length, own), :]
+    spread = values[...].astype(jnp.float32)
+    noise_rows = noises[...].astype(jnp.float32)
+    mixed = jnp.concatenate(
+        [(1.0 - levels[level]) * spread + levels[level] * noise_rows for level in range(2)], axis=0
+    ).astype(jnp.bfloat16)
+    noisy[...] = mixed
+    wide = mixed.astype(jnp.float32)
+    sums = jnp.sum(wide * wide, axis=1, keepdims=True)
+    sums = jnp.broadcast_to(sums, (tokens, length)).T[0:8]
+    squares[...] = sums
+    project(0, mine, mixed, sums, mods, weight, (kept_a, kept_b), (sent_a, sent_b), result)
+
+
+def second_kernel(where, noisy, squares, mods, weight, kept_a, kept_b, sent_a, sent_b, result):
+    project(1, where[2], noisy[...], squares[...], mods, weight, (kept_a, kept_b), (sent_a, sent_b), result)
+
+
+def chunk_shapes(length, weight):
+    unit = length
+    groups = weight.shape[2] // unit
+    return [jax.ShapeDtypeStruct((groups // 2, length + EXTRA_ROWS, 3 * unit), jnp.bfloat16)] * 4
+
+
+def first_part(where, levels, half, swapped, arrived, noise, mods, weight):
+    length, cols = half.shape
+    own, width = noise.shape
+    tokens = 2 * length
+    return pl.pallas_call(
+        first_kernel,
+        in_specs=[smem_spec(), smem_spec()] + [vmem_spec()] * 6,
+        out_specs=[vmem_spec()] * 7,
+        out_shape=[
+            jax.ShapeDtypeStruct((own, width), jnp.bfloat16),
+            jax.ShapeDtypeStruct((tokens, width), jnp.bfloat16),
+            jax.ShapeDtypeStruct((8, tokens), jnp.float32),
+        ]
+        + chunk_shapes(length, weight),
+        scratch_shapes=[
+            pltpu.VMEM((length, width), jnp.bfloat16),
+            pltpu.VMEM((length, width), jnp.bfloat16),
+            pltpu.VMEM((tokens + EXTRA_ROWS, weight.shape[2]), jnp.float32),
+        ],
+        compiler_params=params(24),
+        name="first_part",
+    )(where, levels, half, swapped, arrived, noise, mods, weight)
+
+
+def second_part(where, noisy, squares, mods, weight):
+    tokens = noisy.shape[0]
+    return pl.pallas_call(
+        second_kernel,
+        in_specs=[smem_spec()] + [vmem_spec()] * 4,
+        out_specs=[vmem_spec()] * 4,
+        out_shape=chunk_shapes(tokens // 2, weight),
+        scratch_shapes=[pltpu.VMEM((tokens + EXTRA_ROWS, weight.shape[2]), jnp.float32)],
+        compiler_params=params(24),
+        name="second_part",
+    )(where, noisy, squares, mods, weight)
+
+
+def attend_kernel(width, kept_a, other_a, kept_b, other_b, gains, out):
+    _, length, unit = out.shape
+    for level, (kept, other) in enumerate(((kept_a, other_a), (kept_b, other_b))):
+        mixed = kept[...] + other[...].astype(jnp.float32)
+        squares = jnp.broadcast_to(mixed[length + 1 : length + 2, :unit], (unit, unit)).T
+        factor = lax.rsqrt(squares * (1.0 / width) + 1e-06)
+
+        def pick(part):
+            cols = slice(part * unit, (part + 1) * unit)
+            return mixed[:length, cols] * factor + mixed[length : length + 1, cols]
+
+        def normed(part):
+            rows = pick(part)
+            mean = jnp.mean(rows * rows, axis=1, keepdims=True)
+            return (rows * lax.rsqrt(mean + 1e-06) * gains[part : part + 1, :]).astype(jnp.bfloat16)
+
+        query, key = normed(0), normed(1)
+        value = pick(2).astype(jnp.bfloat16)
+        logits = lax.dot_general(
+            query, key, (((1,), (1,)), ((), ())), preferred_element_type=jnp.float32
+        ) * (1.0 / math.sqrt(unit))
+        expanded = jnp.exp(logits)
+        probs = (expanded / jnp.sum(expanded, axis=1, keepdims=True)).astype(jnp.bfloat16)
+        out[level] = dot32(probs, value).astype(jnp.bfloat16)
+
+
+def attend_part(chunks, gains, width):
+    kept_a, kept_b = chunks[0][0], chunks[1][0]
+    unit = kept_a.shape[1] // 3
+    length = kept_a.shape[0] - EXTRA_ROWS
+    return pl.pallas_call(
+        lambda *refs: attend_kernel(width, *refs),
+        in_specs=[vmem_spec()] * 5,
+        out_specs=vmem_spec(),
+        out_shape=jax.ShapeDtypeStruct((2, length, unit), jnp.bfloat16),
+        compiler_params=params(8),
+        name="attend_part",
+    )(kept_a, chunks[0][1], kept_b, chunks[1][1], gains)
+
+
+def out_kernel(where, *refs):
+    heads_a, heads_b = refs[0:4], refs[4:8]
+    weight_a, weight_b, mods, kept, sent, rows, total = refs[8:]
+    _, length, unit = heads_a[0].shape
+    core, mine = where[1], where[2]
+    for index, (heads, weight) in enumerate(((heads_a, weight_a), (heads_b, weight_b))):
+        for slot, head in enumerate(heads):
+            at = at_block(jnp.bitwise_xor(mine, slot), unit)
+            for level in range(2):
+                rows[pl.ds(level * length, length), at] = head[level]
+        result = dot32(rows[...], weight[...])
+        gates = mods[index, 2]
+        signed = gates[1:2] * result[:length] + gates[2:3] * result[length:]
+        if index == 0:
+            total[...] = -0.5 * signed
+        else:
+            total[...] = total[...] + 0.5 * signed
+    cols = kept.shape[1]
+    kept[...] = total[:, at_block(core, cols)]
+    sent[...] = total[:, at_block(1 - core, cols)].astype(jnp.bfloat16)
+
+
+def out_part(where, heads_a, heads_b, weight_a, weight_b, mods):
+    _, length, unit = heads_a[0].shape
+    depth, width = weight_a.shape
+    return pl.pallas_call(
+        out_kernel,
+        in_specs=[smem_spec()] + [vmem_spec()] * 11,
+        out_specs=[vmem_spec()] * 2,
+        out_shape=[
+            jax.ShapeDtypeStruct((length, width // 2), jnp.float32),
+            jax.ShapeDtypeStruct((length, width // 2), jnp.bfloat16),
+        ],
+        scratch_shapes=[
+            pltpu.VMEM((2 * length, depth), jnp.bfloat16),
+            pltpu.VMEM((length, width), jnp.float32),
+        ],
+        compiler_params=params(16),
+        name="out_part",
+    )(where, *heads_a, *heads_b, weight_a, weight_b, mods)
+
+
+def grad_kernel(where, heads_t, mine, theirs, out, rows):
+    cols = mine.shape[1]
+
+    @pl.when(pl.program_id(0) == 0)
+    def _():
+        rows[:, at_block(where[1], cols)] = mine[...]
+        rows[:, at_block(1 - where[1], cols)] = theirs[...]
+
+    out[...] = dot32(heads_t[...], rows[...]).astype(jnp.bfloat16)
+
+
+def grad_part(where, heads_t, mine, theirs, steps):
+    depth, length = heads_t.shape
+    cols = mine.shape[1]
+    tile = depth // steps
+    grid_spec = pltpu.PrefetchScalarGridSpec(
+        num_scalar_prefetch=1,
+        grid=(steps,),
+        in_specs=[
+            pl.BlockSpec((tile, length), lambda n, w: (n, 0)),
+            pl.BlockSpec((length, cols), lambda n, w: (0, 0)),
+            pl.BlockSpec((length, cols), lambda n, w: (0, 0)),
+        ],
+        out_specs=pl.BlockSpec((tile, 2 * cols), lambda n, w: (n, 0)),
+        scratch_shapes=[pltpu.VMEM((length, 2 * cols), jnp.bfloat16)],
+    )
+    return pl.pallas_call(
+        grad_kernel,
+        grid_spec=grid_spec,
+        out_shape=jax.ShapeDtypeStruct((depth, 2 * cols), jnp.bfloat16),
+        compiler_params=params(24),
+        name="grad_part",
+    )(where, heads_t, mine, theirs)
+
+
+def exchange(array, axis, bit):
+    return lax.ppermute(array, axis, [(i, i ^ bit) for i in range(lax.axis_size(axis))])
+
+
+def both(mine, theirs):
+    return mine.astype(jnp.float32) + theirs.astype(jnp.float32)
+
+
+def heads_per_role(
+    gen_heads,
+    gen_resid,
+    gen_out_w,
+    gen_time_w,
+    noise,
+    steps,
+    teacher_qkv,
+    teacher_out,
+    teacher_time,
+    teacher_norm,
+    critic_qkv,
+    critic_out,
+    critic_time,
+    critic_norm,
+):
+    length = gen_heads.shape[0]
+    roles, groups = lax.axis_size("role"), lax.axis_size("mp")
+    role, seq, mp = lax.axis_index("role"), lax.axis_index("seq"), lax.axis_index("mp")
+    part_cols = gen_heads.shape[1] // roles
+    freq = gen_time_w.shape[0]
+    core = role % 2
+    where = jnp.stack([seq, core, mp]).astype(jnp.int32)
+    half_cols = gen_resid.shape[1] // 2
+
+    embed = jax.vmap(lambda t: time_embed(t, freq))(steps)
+    embed = jnp.concatenate([embed, jnp.zeros((5, freq), jnp.bfloat16)], axis=0)
+    levels = steps[1:3].astype(jnp.float32) / 1000.0
+    full, sent = gen_part(where, gen_heads, gen_out_w, gen_time_w, embed, gen_resid, noise, 4)
+    arrived = exchange(sent, "seq", 1)
+
+    start = role * part_cols
+    weight_a = lax.dynamic_slice_in_dim(teacher_qkv.transpose(1, 0, 2), start, part_cols, axis=2)
+    weight_b = lax.dynamic_slice_in_dim(critic_qkv.transpose(1, 0, 2), start, part_cols, axis=2)
+    mods, gate = mod_part(embed, teacher_time.transpose(1, 0, 2), critic_time.transpose(1, 0, 2), gen_time_w)
+
+    half = both(full, arrived[:length]).astype(jnp.bfloat16)
+    swapped = exchange(jnp.concatenate([half, arrived[length:]], axis=0), "role", 1)
+    first = first_part(where, levels, half, swapped, arrived, noise, mods, weight_a)
+    latent, noisy, squares = first[:3]
+    second = second_part(where, noisy, squares, mods, weight_b)
+
+    out_a = lax.dynamic_slice_in_dim(teacher_out, start, part_cols, axis=0)
+    out_b = lax.dynamic_slice_in_dim(critic_out, start, part_cols, axis=0)
+    unit = part_cols // groups
+    gathered = []
+    for chunks, gains in ((first[3:], teacher_norm), (second, critic_norm)):
+        kept, sends = chunks[:2], chunks[2:]
+        pieces = []
+        for level in range(2):
+            summed = both(kept[level], exchange(sends[level], "mp", 1))
+            pieces.append((summed[0], exchange(summed[1].astype(jnp.bfloat16), "mp", 2)))
+        gains = lax.dynamic_slice_in_dim(gains, start + mp * unit, unit, axis=1)
+        head_out = attend_part(pieces, gains, D)
+        near = exchange(head_out, "mp", 1)
+        far = exchange(head_out, "mp", 2)
+        gathered.append((head_out, near, far, exchange(far, "mp", 1)))
+
+    kept, sent = out_part(where, *gathered, out_a, out_b, mods)
+    total = both(kept, exchange(sent, "role", 1)).astype(jnp.bfloat16)
+    middle = length // 2
+    top, low = total[:middle], total[middle:]
+    top = both(top, exchange(top, "seq", 1)).astype(jnp.bfloat16)
+    low = both(low, exchange(low, "role", 2)).astype(jnp.bfloat16)
+    top = both(top, exchange(top, "role", 2))
+    low = both(low, exchange(low, "seq", 1))
+    gate_row = lax.dynamic_slice_in_dim(gate, core * half_cols, half_cols, axis=1)[0:1]
+    rows = (gate_row * jnp.concatenate([top, low], axis=0)).astype(jnp.bfloat16)
+    weight_grad = grad_part(where, gen_heads.T, rows, exchange(rows, "role", 1), 4)
+    return latent, weight_grad
+
 
 def solution(mesh):
     in_specs = (
@@ -141,6 +540,14 @@
         P(None, "seq"),
     )
     out_specs = (P("seq", "mp"), P("seq", "mp"))
+    roles, seqs, groups = mesh.shape["role"], mesh.shape["seq"], mesh.shape["mp"]
+
+    def on_device(*arrays):
+        heads_here = arrays[0].shape[1] // HEAD_DIM
+        length = arrays[0].shape[0]
+        fits = (roles, seqs, groups) == (4, 2, 4) and heads_here == roles * groups and length == HEAD_DIM
+        return heads_per_role(*arrays) if fits else pass_per_role(*arrays)
+
     return jax.shard_map(
         on_device, mesh=mesh, in_specs=in_specs, out_specs=out_specs, check_vma=False
     )

time: 300 us -> 108 us (0.36)
  waiting for transfers between devices: 131 us -> 45.8 us
  blocking collectives: 41.3 us -> 0 us
  matrix products: 39.7 us -> 0 us
  local copies, waits for them, and re-layouts: 51.7 us -> 14.3 us
  starting transfers between devices: 0.12 us -> 24.1 us
  Pallas kernels: 0 us -> 18.2 us
  other arithmetic: 19.7 us -> 4.24 us
  between operations: 15.3 us -> 0.91 us
    psum x1 -> x0, waiting for transfers between devices: 97.4 us -> none  [on_device(): lax.psum((projected, partial_squares, shift_proj), 'mp')]
    unnamed x23, local copies, waits for them, and re-layouts: 50.8 us -> 4.11 us
    ppermute x0 -> x22, waiting for transfers between devices: none -> 45.8 us  [exchange(): lax.ppermute(array, axis, [(i, i ^ bit) for i in range(lax.axis_size(axis...]
    dot_general x9 -> x0, matrix products: 39.7 us -> none  [the longest x1 12.3 us: on_device(): projected = jnp.dot(scaled, flat_w, preferred_element_type=jnp.float32)]
    reduce_scatter x2 -> x0, waiting for transfers between devices: 33.4 us -> none  [the longest x1 33.3 us: on_device(): lax.psum_scatter(weight_sign * (gate_vec * jnp.dot(block, w_out, preferre...]
    ppermute x0 -> x22, starting transfers between devices: none -> 24.1 us  [exchange(): lax.ppermute(array, axis, [(i, i ^ bit) for i in range(lax.axis_size(axis...]
    all_gather x2 -> x0, blocking collectives: 23.3 us -> none  [the longest x1 17.9 us: on_device(): lax.all_gather((gen_gate * summed_rows).astype(jnp.bfloat16), ('role', 's...]
    pallas_call x0 -> x8, Pallas kernels: none -> 18.2 us  [the longest x1 5.08 us: gen_part(): pl.pallas_call(gen_kernel, grid_spec=grid_spec, out_shape=[jax.ShapeDtype...]
  transfers between devices with their start and end apart: 3 -> 22, of which waited for: 2 -> 17; matrix products, arithmetic and copies ran while one was open for 22% -> 10% of each run, Pallas kernels for 0% -> 2%
where the time goes in v1:
time: 108 us
  waiting for transfers between devices  45.8 us (42%)
  starting transfers between devices  24.1 us (22%)
  Pallas kernels  18.2 us (17%)
  local copies, waits for them, and re-layouts  14.3 us (13%)
  other arithmetic  4.24 us (4%)
    ppermute x22, waiting for transfers between devices, exchange(): lax.ppermute(array, axis, [(i, i ^ bit) for i in range(lax.axis_size(axis...  45.8 us
    ppermute x22, starting transfers between devices, exchange(): lax.ppermute(array, axis, [(i, i ^ bit) for i in range(lax.axis_size(axis...  24.1 us
    dynamic_slice x1, local copies, waits for them, and re-layouts, heads_per_role(): lax.dynamic_slice_in_dim(critic_qkv.transpose(1, 0, 2), start, part_cols,...  7.48 us
    pallas_call x1, Pallas kernels, gen_part(): pl.pallas_call(gen_kernel, grid_spec=grid_spec, out_shape=[jax.ShapeDtype...  5.08 us
    pallas_call x1, Pallas kernels, grad_part(): pl.pallas_call(grad_kernel, grid_spec=grid_spec, out_shape=jax.ShapeDtype...  4.19 us
    unnamed x23, local copies, waits for them, and re-layouts  4.11 us
    pallas_call x1, Pallas kernels, first_part(): pl.pallas_call(first_kernel, in_specs=[smem_spec(), smem_spec()] + [vmem_...  3.13 us
  transfers between devices with their start and end apart: 22, of which 17 were waited for; matrix products, arithmetic and copies ran while one was open for 10% of the time, Pallas kernels for 2%

profile of v1, /device:TPU:1, one launch (start us, length us, event | category | flops | bytes accessed | tf_op | source)
XLA Modules:
  0.0 107.6 jit_solution(5793992525275189115)
XLA Ops:
  0.6 0.0 copy-start
  0.7 0.7 convert_element_type.93
  1.3 0.1 fusion.8
  1.4 0.6 fusion.7.embed
  2.1 0.7 pad_add_fusion.where
  2.7 5.1 %gen_part.1 = (f32[128,640]{1,0:T(8,128)}, bf16[192,640]{1,0:T(8,128)(2,1)}) custom-call(s32[3]{0:T(128)} %pad_add_fusion.where, bf16[128,2048]{1,0:T(8,128)(2,1)} %heads.1, bf16[2048,1280]{1,0:T(8,128)(2,1)} %weight.1, bf16[256,1280]{1,0:T(8,128)(2,1)} %time_w.3, bf16[8,256]{1,0:T(8,128)(2,1)} %fusion.7.embed, bf16[64,1280]{1,0:T(8,128)(2,1)} %resid.1, ...), custom_call_target="tpu_custom_call" | custom-call | tf_op jit(solution)/shard_map/gen_part/pallas_call | solution.py:193
  7.8 2.0 %collective-permute-start = (bf16[192,640]{1,0:T(8,128)(2,1)}, bf16[192,640]{1,0:T(8,128)(2,1)S(1)}, u32[]{:S(2)}, u32[]{:S(2)}) collective-permute-start(bf16[192,640]{1,0:T(8,128)(2,1)} %get-tuple-element.20), channel_id=1, source_target_pairs={{0,4},{4,0},{1,5},{5,1},{2,6},{6,2},{3,7},{7,3},{8,12},{12,8},{9,1... | collective-permute-start | bytes 737288 | tf_op jit(solution)/shard_map/ppermute | solution.py:446
  9.8 5.9 %collective-permute-done.arrived = bf16[192,640]{1,0:T(8,128)(2,1)S(1)} collective-permute-done((bf16[192,640]{1,0:T(8,128)(2,1)}, bf16[192,640]{1,0:T(8,128)(2,1)S(1)}, u32[]{:S(2)}, u32[]{:S(2)}) %collective-permute-start) | collective-permute-done | bytes 245792 | tf_op jit(solution)/shard_map/ppermute | solution.py:446
  15.7 1.0 add_convert_fusion.1.half
  16.7 0.7 pad_maximum_fusion
  17.5 1.3 %collective-permute-start.1 = (bf16[192,640]{1,0:T(8,128)(2,1)}, bf16[192,640]{1,0:T(8,128)(2,1)}, u32[]{:S(2)}, u32[]{:S(2)}) collective-permute-start(bf16[192,640]{1,0:T(8,128)(2,1)} %pad_maximum_fusion), channel_id=1, source_target_pairs={{0,8},{8,0},{16,24},{24,16},{1,9},{9,1},{17,25},{25,17},{2,10},{10... | collective-permute-start | bytes 737288 | tf_op jit(solution)/shard_map/ppermute | solution.py:446
  18.8 7.5 %dynamic-slice_bitcast_fusion = (bf16[3,1280,512]{2,1,0:T(8,128)(2,1)}, bf16[3,1280,512]{2,1,0:T(8,128)(2,1)}) fusion(bf16[1280,3,2048]{2,0,1:T(8,128)(2,1)} %param.24, s32[]{:T(128)S(6)} %select_n.21, bf16[1280,3,2048]{2,0,1:T(8,128)(2,1)} %param.20), kind=kLoop, calls=%fused_computation | loop fusion | bytes 15728644 | tf_op jit(solution)/shard_map/dynamic_slice | solution.py:486
  26.3 0.0 copy-start.5
  26.3 1.5 %copy-done.5 = bf16[256,3,1280]{2,0,1:T(8,128)(2,1)S(1)} copy-done((bf16[256,3,1280]{2,0,1:T(8,128)(2,1)S(1)}, bf16[256,3,1280]{2,0,1:T(8,128)(2,1)}, u32[]{:S(2)}) %copy-start.5) | copy-done | bytes 1966104
  27.9 0.7 mod_part.1
  28.6 0.1 convert_multiply_fusion.levels
  28.7 2.3 %copy-done.2 = bf16[3,1280,512]{2,1,0:T(8,128)(2,1)S(1)} copy-done((bf16[3,1280,512]{2,1,0:T(8,128)(2,1)S(1)}, bf16[3,1280,512]{2,1,0:T(8,128)(2,1)}, u32[]{:S(2)}) %copy-start.2) | copy-done | bytes 3932184
  30.9 3.1 %first_part.1 = (bf16[64,1280]{1,0:T(8,128)(2,1)}, bf16[256,1280]{1,0:T(8,128)(2,1)S(1)}, f32[8,256]{1,0:T(8,128)S(1)}, bf16[2,144,384]{2,1,0:T(8,128)(2,1)S(1)}...) custom-call(s32[3]{0:T(128)S(1)} %copy-done.8, ...), custom_call_target="tpu_custom_call" | custom-call | tf_op jit(solution)/shard_map/first_part/pallas_call | solution.py:295
  34.1 2.0 %second_part.1 = (bf16[2,144,384]{2,1,0:T(8,128)(2,1)S(1)}, bf16[2,144,384]{2,1,0:T(8,128)(2,1)S(1)}, bf16[2,144,384]{2,1,0:T(8,128)(2,1)S(1)}, bf16[2,144,384]{2,1,0:T(8,128)(2,1)S(1)}) custom-call(s32[3]{0:T(128)S(1)} %copy-done.8, bf16[256,1280]{1,0:T(8,128)(2,1)S(1)} %get-tuple-element.28.noisy, f32[8,256]{1,0:T(8,128)S(1)} %get-tuple-element.29.squares, ...), custom_call_target="tpu_custom_call" | custom-call | tf_op jit(solution)/shard_map/second_part/pallas_call | solution.py:317
  36.1 1.6 %collective-permute-start.11 = (bf16[2,144,384]{2,1,0:T(8,128)(2,1)S(1)}, bf16[2,144,384]{2,1,0:T(8,128)(2,1)S(1)}, u32[]{:S(2)}, u32[]{:S(2)}) collective-permute-start(bf16[2,144,384]{2,1,0:T(8,128)(2,1)S(1)} %get-tuple-element.33), channel_id=1, source_target_pairs={{0,1},{1,0},{2,3},{3,2},{4,5},{5,4},{6,7},{7,6},{8,9},{9,8},{10,11... | collective-permute-start | bytes 663560 | tf_op jit(solution)/shard_map/ppermute | solution.py:446
  37.7 0.7 constant_dynamic-slice_fusion.3.refs_4_
  38.4 0.0 collective-permute-start.9
  38.4 1.4 %collective-permute-start.4 = (bf16[2,144,384]{2,1,0:T(8,128)(2,1)S(1)}, bf16[2,144,384]{2,1,0:T(8,128)(2,1)S(1)}, u32[]{:S(2)}, u32[]{:S(2)}) collective-permute-start(bf16[2,144,384]{2,1,0:T(8,128)(2,1)S(1)} %get-tuple-element.27), channel_id=1, source_target_pairs={{0,1},{1,0},{2,3},{3,2},{4,5},{5,4},{6,7},{7,6},{8,9},{9,8},{10,11... | collective-permute-start | bytes 663560 | tf_op jit(solution)/shard_map/ppermute | solution.py:446
  39.9 0.0 collective-permute-start.2
  39.9 3.3 %collective-permute-done.11 = bf16[2,144,384]{2,1,0:T(8,128)(2,1)S(1)} collective-permute-done((bf16[2,144,384]{2,1,0:T(8,128)(2,1)S(1)}, bf16[2,144,384]{2,1,0:T(8,128)(2,1)S(1)}, u32[]{:S(2)}, u32[]{:S(2)}) %collective-permute-start.11) | collective-permute-done | bytes 221216 | tf_op jit(solution)/shard_map/ppermute | solution.py:446
  43.3 2.5 %collective-permute-start.12 = (bf16[144,384]{1,0:T(8,128)(2,1)S(1)}, bf16[144,384]{1,0:T(8,128)(2,1)S(1)}, u32[]{:S(2)}, u32[]{:S(2)}) collective-permute-start(bf16[144,384]{1,0:T(8,128)(2,1)S(1)} %fusion.4), channel_id=1, source_target_pairs={{0,2},{1,3},{2,0},{3,1},{4,6},{5,7},{6,4},{7,5},{8,10},{9,11},{10,... | collective-permute-start | bytes 331784 | tf_op jit(solution)/shard_map/ppermute | solution.py:446
  45.8 4.6 %collective-permute-done.9 = bf16[2,144,384]{2,1,0:T(8,128)(2,1)S(1)} collective-permute-done((bf16[2,144,384]{2,1,0:T(8,128)(2,1)S(1)}, bf16[2,144,384]{2,1,0:T(8,128)(2,1)S(1)}, u32[]{:S(2)}, u32[]{:S(2)}) %collective-permute-start.9) | collective-permute-done | bytes 221216 | tf_op jit(solution)/shard_map/ppermute | solution.py:446
  50.3 0.1 convert_add_fusion.1
  50.4 0.4 collective-permute-start.10
  50.8 6.6 %collective-permute-done.4 = bf16[2,144,384]{2,1,0:T(8,128)(2,1)S(1)} collective-permute-done((bf16[2,144,384]{2,1,0:T(8,128)(2,1)S(1)}, bf16[2,144,384]{2,1,0:T(8,128)(2,1)S(1)}, u32[]{:S(2)}, u32[]{:S(2)}) %collective-permute-start.4) | collective-permute-done | bytes 221216 | tf_op jit(solution)/shard_map/ppermute | solution.py:446
  57.4 0.1 convert_add_fusion.2
  57.5 0.4 collective-permute-start.5
  57.9 4.4 %collective-permute-done.2 = bf16[2,144,384]{2,1,0:T(8,128)(2,1)S(1)} collective-permute-done((bf16[2,144,384]{2,1,0:T(8,128)(2,1)S(1)}, bf16[2,144,384]{2,1,0:T(8,128)(2,1)S(1)}, u32[]{:S(2)}, u32[]{:S(2)}) %collective-permute-start.2) | collective-permute-done | bytes 221216 | tf_op jit(solution)/shard_map/ppermute | solution.py:446
  62.4 1.4 %collective-permute-start.3 = (bf16[144,384]{1,0:T(8,128)(2,1)S(1)}, bf16[144,384]{1,0:T(8,128)(2,1)S(1)}, u32[]{:S(2)}, u32[]{:S(2)}) collective-permute-start(bf16[144,384]{1,0:T(8,128)(2,1)S(1)} %fusion.1), channel_id=1, source_target_pairs={{0,2},{1,3},{2,0},{3,1},{4,6},{5,7},{6,4},{7,5},{8,10},{9,11},{10,... | collective-permute-start | bytes 331784 | tf_op jit(solution)/shard_map/ppermute | solution.py:446
  63.8 0.8 attend_part.3.refs_4_
  64.6 1.1 %collective-permute-start.14 = (bf16[2,128,128]{2,1,0:T(8,128)(2,1)S(1)}, bf16[2,128,128]{2,1,0:T(8,128)(2,1)S(1)}, u32[]{:S(2)}, u32[]{:S(2)}) collective-permute-start(bf16[2,128,128]{2,1,0:T(8,128)(2,1)S(1)} %attend_part.3.refs_4_), channel_id=1, source_target_pairs={{0,2},{1,3},{2,0},{3,1},{4,6},{5,7},{6,4},{7,5},{8,10},{9,11},{10,... | collective-permute-start | bytes 196616 | tf_op jit(solution)/shard_map/ppermute | solution.py:446
  65.7 7.6 %collective-permute-done.5.refs_3_ = bf16[144,384]{1,0:T(8,128)(2,1)S(1)} collective-permute-done((bf16[144,384]{1,0:T(8,128)(2,1)S(1)}, bf16[144,384]{1,0:T(8,128)(2,1)S(1)}, u32[]{:S(2)}, u32[]{:S(2)}) %collective-permute-start.5) | collective-permute-done | bytes 110624 | tf_op jit(solution)/shard_map/ppermute | solution.py:446
  73.3 2.4 %collective-permute-done.3.refs_1_ = bf16[144,384]{1,0:T(8,128)(2,1)S(1)} collective-permute-done((bf16[144,384]{1,0:T(8,128)(2,1)S(1)}, bf16[144,384]{1,0:T(8,128)(2,1)S(1)}, u32[]{:S(2)}, u32[]{:S(2)}) %collective-permute-start.3) | collective-permute-done | bytes 110624 | tf_op jit(solution)/shard_map/ppermute | solution.py:446
  75.6 0.8 attend_part.2.refs_0_
  76.5 0.1 collective-permute-start.7
  76.5 1.3 %collective-permute-start.13 = (bf16[2,128,128]{2,1,0:T(8,128)(2,1)S(1)}, bf16[2,128,128]{2,1,0:T(8,128)(2,1)S(1)}, u32[]{:S(2)}, u32[]{:S(2)}) collective-permute-start(bf16[2,128,128]{2,1,0:T(8,128)(2,1)S(1)} %attend_part.3.refs_4_), channel_id=1, source_target_pairs={{0,1},{1,0},{2,3},{3,2},{4,5},{5,4},{6,7},{7,6},{8,9},{9,8},{10,11... | collective-permute-start | bytes 196616 | tf_op jit(solution)/shard_map/ppermute | solution.py:446
  77.9 0.2 collective-permute-start.6
  78.1 1.3 %collective-permute-start.15 = (bf16[2,128,128]{2,1,0:T(8,128)(2,1)S(1)}, bf16[2,128,128]{2,1,0:T(8,128)(2,1)S(1)}, u32[]{:S(2)}, u32[]{:S(2)}) collective-permute-start(bf16[2,128,128]{2,1,0:T(8,128)(2,1)S(1)} %collective-permute-done.14.refs_6_), channel_id=1, source_target_pairs={{0,1},{1,0},{2,3},{3,2},{4,5},{5,4},{6,7},{7,6},{8,9},{9,8},{10,11... | collective-permute-start | bytes 196616 | tf_op jit(solution)/shard_map/ppermute | solution.py:446
  79.3 1.4 %collective-permute-done.7.refs_2_ = bf16[2,128,128]{2,1,0:T(8,128)(2,1)S(1)} collective-permute-done((bf16[2,128,128]{2,1,0:T(8,128)(2,1)S(1)}, bf16[2,128,128]{2,1,0:T(8,128)(2,1)S(1)}, u32[]{:S(2)}, u32[]{:S(2)}) %collective-permute-start.7) | collective-permute-done | bytes 65568 | tf_op jit(solution)/shard_map/ppermute | solution.py:446
  80.8 0.2 collective-permute-start.8
  80.9 1.9 %constant_dynamic-slice_fusion = (bf16[512,1280]{1,0:T(8,128)(2,1)S(1)}, bf16[512,1280]{1,0:T(8,128)(2,1)S(1)}) fusion(bf16[2048,1280]{1,0:T(8,128)(2,1)} %param.25, s32[]{:T(128)S(6)} %select_n.21, bf16[2048,1280]{1,0:T(8,128)(2,1)} %param.21), kind=kLoop, calls=%fused_computation.36 | loop fusion | bytes 5242884 | tf_op jit(solution)/shard_map/dynamic_slice | solution.py:496
  82.8 0.3 collective-permute-done.6.refs_1_
  83.1 1.4 %collective-permute-done.15.refs_7_ = bf16[2,128,128]{2,1,0:T(8,128)(2,1)S(1)} collective-permute-done((bf16[2,128,128]{2,1,0:T(8,128)(2,1)S(1)}, bf16[2,128,128]{2,1,0:T(8,128)(2,1)S(1)}, u32[]{:S(2)}, u32[]{:S(2)}) %collective-permute-start.15) | collective-permute-done | bytes 65568 | tf_op jit(solution)/shard_map/ppermute | solution.py:446
  84.5 1.4 %collective-permute-done.8.refs_3_ = bf16[2,128,128]{2,1,0:T(8,128)(2,1)S(1)} collective-permute-done((bf16[2,128,128]{2,1,0:T(8,128)(2,1)S(1)}, bf16[2,128,128]{2,1,0:T(8,128)(2,1)S(1)}, u32[]{:S(2)}, u32[]{:S(2)}) %collective-permute-start.8) | collective-permute-done | bytes 65568 | tf_op jit(solution)/shard_map/ppermute | solution.py:446
  85.9 1.5 %out_part.1 = (f32[128,640]{1,0:T(8,128)S(1)}, bf16[128,640]{1,0:T(8,128)(2,1)S(1)}) custom-call(s32[3]{0:T(128)S(1)} %copy-done.8, bf16[2,128,128]{2,1,0:T(8,128)(2,1)S(1)} %attend_part.2.refs_0_, bf16[2,128,128]{2,1,0:T(8,128)(2,1)S(1)} %collective-permute-done.6.refs_1_, bf16[2,128,128]{2,1,0:T(8,128)(2,1)S(1)} %collective-permute-done.7.refs_2_, ...), custom_call_target="tpu_custom_call" | custom-call | tf_op jit(solution)/shard_map/out_part/pallas_call | solution.py:393
  87.5 1.2 %collective-permute-start.16 = (bf16[128,640]{1,0:T(8,128)(2,1)S(1)}, bf16[128,640]{1,0:T(8,128)(2,1)S(1)}, u32[]{:S(2)}, u32[]{:S(2)}) collective-permute-start(bf16[128,640]{1,0:T(8,128)(2,1)S(1)} %get-tuple-element.35), channel_id=1, source_target_pairs={{0,8},{8,0},{16,24},{24,16},{1,9},{9,1},{17,25},{25,17},{2,10},{10... | collective-permute-start | bytes 491528 | tf_op jit(solution)/shard_map/ppermute | solution.py:446
  88.6 1.0 collective-permute-done.16
  89.7 1.3 %collective-permute-start.17 = (bf16[64,640]{1,0:T(8,128)(2,1)S(1)}, bf16[64,640]{1,0:T(8,128)(2,1)S(1)}, u32[]{:S(2)}, u32[]{:S(2)}) collective-permute-start(bf16[64,640]{1,0:T(8,128)(2,1)S(1)} %get-tuple-element.38), channel_id=1, source_target_pairs={{0,4},{4,0},{1,5},{5,1},{2,6},{6,2},{3,7},{7,3},{8,12},{12,8},{9,1... | collective-permute-start | bytes 245768 | tf_op jit(solution)/shard_map/ppermute | solution.py:446
  91.0 1.2 %collective-permute-start.19 = (bf16[64,640]{1,0:T(8,128)(2,1)S(1)}, bf16[64,640]{1,0:T(8,128)(2,1)S(1)}, u32[]{:S(2)}, u32[]{:S(2)}) collective-permute-start(bf16[64,640]{1,0:T(8,128)(2,1)S(1)} %get-tuple-element.39), channel_id=1, source_target_pairs={{0,16},{8,24},{16,0},{24,8},{1,17},{9,25},{17,1},{25,9},{2,18},{10... | collective-permute-start | bytes 245768 | tf_op jit(solution)/shard_map/ppermute | solution.py:446
  92.2 1.2 %collective-permute-done.17 = bf16[64,640]{1,0:T(8,128)(2,1)S(1)} collective-permute-done((bf16[64,640]{1,0:T(8,128)(2,1)S(1)}, bf16[64,640]{1,0:T(8,128)(2,1)S(1)}, u32[]{:S(2)}, u32[]{:S(2)}) %collective-permute-start.17) | collective-permute-done | bytes 81952 | tf_op jit(solution)/shard_map/ppermute | solution.py:446
  93.4 0.8 collective-permute-done.19
  94.3 1.3 %collective-permute-start.18 = (bf16[64,640]{1,0:T(8,128)(2,1)S(1)}, bf16[64,640]{1,0:T(8,128)(2,1)S(1)}, u32[]{:S(2)}, u32[]{:S(2)}) collective-permute-start(bf16[64,640]{1,0:T(8,128)(2,1)S(1)} %get-tuple-element.36), channel_id=1, source_target_pairs={{0,16},{8,24},{16,0},{24,8},{1,17},{9,25},{17,1},{25,9},{2,18},{10... | collective-permute-start | bytes 245768 | tf_op jit(solution)/shard_map/ppermute | solution.py:446
  95.7 0.6 collective-permute-start.20
  96.3 1.4 %collective-permute-done.18 = bf16[64,640]{1,0:T(8,128)(2,1)S(1)} collective-permute-done((bf16[64,640]{1,0:T(8,128)(2,1)S(1)}, bf16[64,640]{1,0:T(8,128)(2,1)S(1)}, u32[]{:S(2)}, u32[]{:S(2)}) %collective-permute-start.18) | collective-permute-done | bytes 81952 | tf_op jit(solution)/shard_map/ppermute | solution.py:446
  97.7 1.3 %collective-permute-done.20 = bf16[64,640]{1,0:T(8,128)(2,1)S(1)} collective-permute-done((bf16[64,640]{1,0:T(8,128)(2,1)S(1)}, bf16[64,640]{1,0:T(8,128)(2,1)S(1)}, u32[]{:S(2)}, u32[]{:S(2)}) %collective-permute-start.20) | collective-permute-done | bytes 81952 | tf_op jit(solution)/shard_map/ppermute | solution.py:446
  99.1 3.3 %collective-permute-start.21 = (bf16[128,640]{1,0:T(8,128)(2,1)S(1)}, bf16[128,640]{1,0:T(8,128)(2,1)S(1)}, u32[]{:S(2)}, u32[]{:S(2)}) collective-permute-start(bf16[128,640]{1,0:T(8,128)(2,1)S(1)} %fusion.mine), channel_id=1, source_target_pairs={{0,8},{8,0},{16,24},{24,16},{1,9},{9,1},{17,25},{25,17},{2,10},{10... | collective-permute-start | bytes 491528 | tf_op jit(solution)/shard_map/ppermute | solution.py:446
  102.4 0.3 copy.16
  102.6 0.8 collective-permute-done.21.theirs
  103.4 4.2 %grad_part.1 = bf16[2048,1280]{1,0:T(8,128)(2,1)} custom-call(s32[3]{0:T(128)S(1)} %copy-done.8, bf16[2048,128]{1,0:T(8,128)(2,1)S(1)} %bitcast.26, bf16[128,640]{1,0:T(8,128)(2,1)S(1)} %fusion.mine, bf16[128,640]{1,0:T(8,128)(2,1)S(1)} %collective-permute-done.21.theirs), custom_call_target="tpu_custom_call" | custom-call | tf_op jit(solution)/shard_map/grad_part/pallas_call | solution.py:436
  (43 shorter events, 0.5 us)
Async XLA Ops:
  0.6 37.1 %copy-start = (f32[2,2048]{1,0:T(2,128)S(1)}, f32[2,2048]{1,0:T(2,128)}, u32[]{:S(2)}) copy-start(f32[2,2048]{1,0:T(2,128)} %param.27) | copy-start | bytes 49156
  7.8 7.9 %collective-permute-start = (bf16[192,640]{1,0:T(8,128)(2,1)}, bf16[192,640]{1,0:T(8,128)(2,1)S(1)}, u32[]{:S(2)}, u32[]{:S(2)}) collective-permute-start(bf16[192,640]{1,0:T(8,128)(2,1)} %get-tuple-element.20), channel_id=1, source_target_pairs={{0,4},{4,0},{1,5},{5,1},{2,6},{6,2},{3,7},{7,3},{8,12},{12,8},{9,1... | collective-permute-start | bytes 737288 | tf_op jit(solution)/shard_map/ppermute | solution.py:446
  17.5 8.8 %copy-start.3 = (bf16[256,1280]{1,0:T(8,128)(2,1)S(1)}, bf16[256,1280]{1,0:T(8,128)(2,1)}, u32[]{:S(2)}) copy-start(bf16[256,1280]{1,0:T(8,128)(2,1)} %time_w.3) | copy-start | bytes 1966084
  17.5 8.8 %copy-start.4 = (bf16[256,3,1280]{2,0,1:T(8,128)(2,1)S(1)}, bf16[256,3,1280]{2,0,1:T(8,128)(2,1)}, u32[]{:S(2)}) copy-start(bf16[256,3,1280]{2,0,1:T(8,128)(2,1)} %param.22) | copy-start | bytes 5898244
  17.5 8.8 %copy-start.7 = (bf16[8,256]{1,0:T(8,128)(2,1)S(1)}, bf16[8,256]{1,0:T(8,128)(2,1)}, u32[]{:S(2)}) copy-start(bf16[8,256]{1,0:T(8,128)(2,1)} %fusion.7.embed) | copy-start | bytes 12292
  17.5 11.1 %copy-start.10 = (s32[3]{0:T(128)S(1)}, s32[3]{0:T(128)}, u32[]{:S(2)}) copy-start(s32[3]{0:T(128)} %param.19) | copy-start | bytes 40
  17.5 11.2 %copy-start.6 = (bf16[64,1280]{1,0:T(8,128)(2,1)S(1)}, bf16[64,1280]{1,0:T(8,128)(2,1)}, u32[]{:S(2)}) copy-start(bf16[64,1280]{1,0:T(8,128)(2,1)} %noise.3) | copy-start | bytes 491524
  17.5 11.2 %copy-start.8 = (s32[3]{0:T(128)S(1)}, s32[3]{0:T(128)}, u32[]{:S(2)}) copy-start(s32[3]{0:T(128)} %pad_add_fusion.where) | copy-start | bytes 40
  17.5 11.1 %collective-permute-start.1 = (bf16[192,640]{1,0:T(8,128)(2,1)}, bf16[192,640]{1,0:T(8,128)(2,1)}, u32[]{:S(2)}, u32[]{:S(2)}) collective-permute-start(bf16[192,640]{1,0:T(8,128)(2,1)} %pad_maximum_fusion), channel_id=1, source_target_pairs={{0,8},{8,0},{16,24},{24,16},{1,9},{9,1},{17,25},{25,17},{2,10},{10... | collective-permute-start | bytes 737288 | tf_op jit(solution)/shard_map/ppermute | solution.py:446
  26.3 1.5 %copy-start.5 = (bf16[256,3,1280]{2,0,1:T(8,128)(2,1)S(1)}, bf16[256,3,1280]{2,0,1:T(8,128)(2,1)}, u32[]{:S(2)}) copy-start(bf16[256,3,1280]{2,0,1:T(8,128)(2,1)} %param.26) | copy-start | bytes 5898244
  28.6 5.5 %copy-start.1 = (bf16[3,1280,512]{2,1,0:T(8,128)(2,1)S(1)}, bf16[3,1280,512]{2,1,0:T(8,128)(2,1)}, u32[]{:S(2)}) copy-start(bf16[3,1280,512]{2,1,0:T(8,128)(2,1)} %get-tuple-element.42.weight) | copy-start | bytes 11796484
  28.7 2.3 %copy-start.2 = (bf16[3,1280,512]{2,1,0:T(8,128)(2,1)S(1)}, bf16[3,1280,512]{2,1,0:T(8,128)(2,1)}, u32[]{:S(2)}) copy-start(bf16[3,1280,512]{2,1,0:T(8,128)(2,1)} %get-tuple-element.43.weight) | copy-start | bytes 11796484
  36.1 7.1 %collective-permute-start.11 = (bf16[2,144,384]{2,1,0:T(8,128)(2,1)S(1)}, bf16[2,144,384]{2,1,0:T(8,128)(2,1)S(1)}, u32[]{:S(2)}, u32[]{:S(2)}) collective-permute-start(bf16[2,144,384]{2,1,0:T(8,128)(2,1)S(1)} %get-tuple-element.33), channel_id=1, source_target_pairs={{0,1},{1,0},{2,3},{3,2},{4,5},{5,4},{6,7},{7,6},{8,9},{9,8},{10,11... | collective-permute-start | bytes 663560 | tf_op jit(solution)/shard_map/ppermute | solution.py:446
  38.4 11.9 %collective-permute-start.9 = (bf16[2,144,384]{2,1,0:T(8,128)(2,1)S(1)}, bf16[2,144,384]{2,1,0:T(8,128)(2,1)S(1)}, u32[]{:S(2)}, u32[]{:S(2)}) collective-permute-start(bf16[2,144,384]{2,1,0:T(8,128)(2,1)S(1)} %get-tuple-element.31), channel_id=1, source_target_pairs={{0,1},{1,0},{2,3},{3,2},{4,5},{5,4},{6,7},{7,6},{8,9},{9,8},{10,11... | collective-permute-start | bytes 663560 | tf_op jit(solution)/shard_map/ppermute | solution.py:446
  38.4 19.0 %collective-permute-start.4 = (bf16[2,144,384]{2,1,0:T(8,128)(2,1)S(1)}, bf16[2,144,384]{2,1,0:T(8,128)(2,1)S(1)}, u32[]{:S(2)}, u32[]{:S(2)}) collective-permute-start(bf16[2,144,384]{2,1,0:T(8,128)(2,1)S(1)} %get-tuple-element.27), channel_id=1, source_target_pairs={{0,1},{1,0},{2,3},{3,2},{4,5},{5,4},{6,7},{7,6},{8,9},{9,8},{10,11... | collective-permute-start | bytes 663560 | tf_op jit(solution)/shard_map/ppermute | solution.py:446
  39.9 22.4 %collective-permute-start.2 = (bf16[2,144,384]{2,1,0:T(8,128)(2,1)S(1)}, bf16[2,144,384]{2,1,0:T(8,128)(2,1)S(1)}, u32[]{:S(2)}, u32[]{:S(2)}) collective-permute-start(bf16[2,144,384]{2,1,0:T(8,128)(2,1)S(1)} %get-tuple-element.25), channel_id=1, source_target_pairs={{0,1},{1,0},{2,3},{3,2},{4,5},{5,4},{6,7},{7,6},{8,9},{9,8},{10,11... | collective-permute-start | bytes 663560 | tf_op jit(solution)/shard_map/ppermute | solution.py:446
  43.3 20.5 %collective-permute-start.12 = (bf16[144,384]{1,0:T(8,128)(2,1)S(1)}, bf16[144,384]{1,0:T(8,128)(2,1)S(1)}, u32[]{:S(2)}, u32[]{:S(2)}) collective-permute-start(bf16[144,384]{1,0:T(8,128)(2,1)S(1)} %fusion.4), channel_id=1, source_target_pairs={{0,2},{1,3},{2,0},{3,1},{4,6},{5,7},{6,4},{7,5},{8,10},{9,11},{10,... | collective-permute-start | bytes 331784 | tf_op jit(solution)/shard_map/ppermute | solution.py:446
  50.4 13.4 %collective-permute-start.10 = (bf16[144,384]{1,0:T(8,128)(2,1)S(1)}, bf16[144,384]{1,0:T(8,128)(2,1)S(1)}, u32[]{:S(2)}, u32[]{:S(2)}) collective-permute-start(bf16[144,384]{1,0:T(8,128)(2,1)S(1)} %fusion.3), channel_id=1, source_target_pairs={{0,2},{1,3},{2,0},{3,1},{4,6},{5,7},{6,4},{7,5},{8,10},{9,11},{10,... | collective-permute-start | bytes 331784 | tf_op jit(solution)/shard_map/ppermute | solution.py:446
  57.5 15.8 %collective-permute-start.5 = (bf16[144,384]{1,0:T(8,128)(2,1)S(1)}, bf16[144,384]{1,0:T(8,128)(2,1)S(1)}, u32[]{:S(2)}, u32[]{:S(2)}) collective-permute-start(bf16[144,384]{1,0:T(8,128)(2,1)S(1)} %fusion.2), channel_id=1, source_target_pairs={{0,2},{1,3},{2,0},{3,1},{4,6},{5,7},{6,4},{7,5},{8,10},{9,11},{10,... | collective-permute-start | bytes 331784 | tf_op jit(solution)/shard_map/ppermute | solution.py:446
  62.4 13.3 %collective-permute-start.3 = (bf16[144,384]{1,0:T(8,128)(2,1)S(1)}, bf16[144,384]{1,0:T(8,128)(2,1)S(1)}, u32[]{:S(2)}, u32[]{:S(2)}) collective-permute-start(bf16[144,384]{1,0:T(8,128)(2,1)S(1)} %fusion.1), channel_id=1, source_target_pairs={{0,2},{1,3},{2,0},{3,1},{4,6},{5,7},{6,4},{7,5},{8,10},{9,11},{10,... | collective-permute-start | bytes 331784 | tf_op jit(solution)/shard_map/ppermute | solution.py:446
  64.6 13.5 %collective-permute-start.14 = (bf16[2,128,128]{2,1,0:T(8,128)(2,1)S(1)}, bf16[2,128,128]{2,1,0:T(8,128)(2,1)S(1)}, u32[]{:S(2)}, u32[]{:S(2)}) collective-permute-start(bf16[2,128,128]{2,1,0:T(8,128)(2,1)S(1)} %attend_part.3.refs_4_), channel_id=1, source_target_pairs={{0,2},{1,3},{2,0},{3,1},{4,6},{5,7},{6,4},{7,5},{8,10},{9,11},{10,... | collective-permute-start | bytes 196616 | tf_op jit(solution)/shard_map/ppermute | solution.py:446
  76.4 25.9 %copy-start.9 = (bf16[128,2048]{1,0:T(8,128)(2,1)S(1)}, bf16[128,2048]{1,0:T(8,128)(2,1)}, u32[]{:S(2)}) copy-start(bf16[128,2048]{1,0:T(8,128)(2,1)} %heads.1) | copy-start | bytes 1572868
  76.5 4.3 %collective-permute-start.7 = (bf16[2,128,128]{2,1,0:T(8,128)(2,1)S(1)}, bf16[2,128,128]{2,1,0:T(8,128)(2,1)S(1)}, u32[]{:S(2)}, u32[]{:S(2)}) collective-permute-start(bf16[2,128,128]{2,1,0:T(8,128)(2,1)S(1)} %attend_part.2.refs_0_), channel_id=1, source_target_pairs={{0,2},{1,3},{2,0},{3,1},{4,6},{5,7},{6,4},{7,5},{8,10},{9,11},{10,... | collective-permute-start | bytes 196616 | tf_op jit(solution)/shard_map/ppermute | solution.py:446
  76.5 6.3 %collective-permute-start.13 = (bf16[2,128,128]{2,1,0:T(8,128)(2,1)S(1)}, bf16[2,128,128]{2,1,0:T(8,128)(2,1)S(1)}, u32[]{:S(2)}, u32[]{:S(2)}) collective-permute-start(bf16[2,128,128]{2,1,0:T(8,128)(2,1)S(1)} %attend_part.3.refs_4_), channel_id=1, source_target_pairs={{0,1},{1,0},{2,3},{3,2},{4,5},{5,4},{6,7},{7,6},{8,9},{9,8},{10,11... | collective-permute-start | bytes 196616 | tf_op jit(solution)/shard_map/ppermute | solution.py:446
  77.9 5.3 %collective-permute-start.6 = (bf16[2,128,128]{2,1,0:T(8,128)(2,1)S(1)}, bf16[2,128,128]{2,1,0:T(8,128)(2,1)S(1)}, u32[]{:S(2)}, u32[]{:S(2)}) collective-permute-start(bf16[2,128,128]{2,1,0:T(8,128)(2,1)S(1)} %attend_part.2.refs_0_), channel_id=1, source_target_pairs={{0,1},{1,0},{2,3},{3,2},{4,5},{5,4},{6,7},{7,6},{8,9},{9,8},{10,11... | collective-permute-start | bytes 196616 | tf_op jit(solution)/shard_map/ppermute | solution.py:446
  78.1 6.5 %collective-permute-start.15 = (bf16[2,128,128]{2,1,0:T(8,128)(2,1)S(1)}, bf16[2,128,128]{2,1,0:T(8,128)(2,1)S(1)}, u32[]{:S(2)}, u32[]{:S(2)}) collective-permute-start(bf16[2,128,128]{2,1,0:T(8,128)(2,1)S(1)} %collective-permute-done.14.refs_6_), channel_id=1, source_target_pairs={{0,1},{1,0},{2,3},{3,2},{4,5},{5,4},{6,7},{7,6},{8,9},{9,8},{10,11... | collective-permute-start | bytes 196616 | tf_op jit(solution)/shard_map/ppermute | solution.py:446
  80.8 5.2 %collective-permute-start.8 = (bf16[2,128,128]{2,1,0:T(8,128)(2,1)S(1)}, bf16[2,128,128]{2,1,0:T(8,128)(2,1)S(1)}, u32[]{:S(2)}, u32[]{:S(2)}) collective-permute-start(bf16[2,128,128]{2,1,0:T(8,128)(2,1)S(1)} %collective-permute-done.7.refs_2_), channel_id=1, source_target_pairs={{0,1},{1,0},{2,3},{3,2},{4,5},{5,4},{6,7},{7,6},{8,9},{9,8},{10,11... | collective-permute-start | bytes 196616 | tf_op jit(solution)/shard_map/ppermute | solution.py:446
  87.5 2.2 %collective-permute-start.16 = (bf16[128,640]{1,0:T(8,128)(2,1)S(1)}, bf16[128,640]{1,0:T(8,128)(2,1)S(1)}, u32[]{:S(2)}, u32[]{:S(2)}) collective-permute-start(bf16[128,640]{1,0:T(8,128)(2,1)S(1)} %get-tuple-element.35), channel_id=1, source_target_pairs={{0,8},{8,0},{16,24},{24,16},{1,9},{9,1},{17,25},{25,17},{2,10},{10... | collective-permute-start | bytes 491528 | tf_op jit(solution)/shard_map/ppermute | solution.py:446
  89.7 3.7 %collective-permute-start.17 = (bf16[64,640]{1,0:T(8,128)(2,1)S(1)}, bf16[64,640]{1,0:T(8,128)(2,1)S(1)}, u32[]{:S(2)}, u32[]{:S(2)}) collective-permute-start(bf16[64,640]{1,0:T(8,128)(2,1)S(1)} %get-tuple-element.38), channel_id=1, source_target_pairs={{0,4},{4,0},{1,5},{5,1},{2,6},{6,2},{3,7},{7,3},{8,12},{12,8},{9,1... | collective-permute-start | bytes 245768 | tf_op jit(solution)/shard_map/ppermute | solution.py:446
  91.0 3.3 %collective-permute-start.19 = (bf16[64,640]{1,0:T(8,128)(2,1)S(1)}, bf16[64,640]{1,0:T(8,128)(2,1)S(1)}, u32[]{:S(2)}, u32[]{:S(2)}) collective-permute-start(bf16[64,640]{1,0:T(8,128)(2,1)S(1)} %get-tuple-element.39), channel_id=1, source_target_pairs={{0,16},{8,24},{16,0},{24,8},{1,17},{9,25},{17,1},{25,9},{2,18},{10... | collective-permute-start | bytes 245768 | tf_op jit(solution)/shard_map/ppermute | solution.py:446
  94.3 3.4 %collective-permute-start.18 = (bf16[64,640]{1,0:T(8,128)(2,1)S(1)}, bf16[64,640]{1,0:T(8,128)(2,1)S(1)}, u32[]{:S(2)}, u32[]{:S(2)}) collective-permute-start(bf16[64,640]{1,0:T(8,128)(2,1)S(1)} %get-tuple-element.36), channel_id=1, source_target_pairs={{0,16},{8,24},{16,0},{24,8},{1,17},{9,25},{17,1},{25,9},{2,18},{10... | collective-permute-start | bytes 245768 | tf_op jit(solution)/shard_map/ppermute | solution.py:446
  95.7 3.4 %collective-permute-start.20 = (bf16[64,640]{1,0:T(8,128)(2,1)S(1)}, bf16[64,640]{1,0:T(8,128)(2,1)S(1)}, u32[]{:S(2)}, u32[]{:S(2)}) collective-permute-start(bf16[64,640]{1,0:T(8,128)(2,1)S(1)} %get-tuple-element.37), channel_id=1, source_target_pairs={{0,4},{4,0},{1,5},{5,1},{2,6},{6,2},{3,7},{7,3},{8,12},{12,8},{9,1... | collective-permute-start | bytes 245768 | tf_op jit(solution)/shard_map/ppermute | solution.py:446
  99.1 4.3 %collective-permute-start.21 = (bf16[128,640]{1,0:T(8,128)(2,1)S(1)}, bf16[128,640]{1,0:T(8,128)(2,1)S(1)}, u32[]{:S(2)}, u32[]{:S(2)}) collective-permute-start(bf16[128,640]{1,0:T(8,128)(2,1)S(1)} %fusion.mine), channel_id=1, source_target_pairs={{0,8},{8,0},{16,24},{24,16},{1,9},{9,1},{17,25},{25,17},{2,10},{10... | collective-permute-start | bytes 491528 | tf_op jit(solution)/shard_map/ppermute | solution.py:446

commit v2 on v1

--- a/solution.py
+++ b/solution.py
@@ -148,80 +148,147 @@
     return pl.ds(pl.multiple_of(index * size, size), size)
 
 
-def gen_kernel(where, heads, weight, time_w, embed, resid, noise, full, sent):
-    step = pl.program_id(0)
-    length = full.shape[0]
-    own = resid.shape[0]
-
-    @pl.when(step == 0)
-    def _():
-        full[...] = jnp.zeros_like(full)
-
-    full[...] += dot32(heads[...], weight[...])
-
-    @pl.when(step == pl.num_programs(0) - 1)
-    def _():
-        full[...] = full[...] * dot32(embed[...], time_w[...])[0:1]
-        at = at_block(where[0], own)
-        full[at, :] = full[at, :] + resid[...].astype(jnp.float32)
-        sent[pl.ds(0, length), :] = full[...].astype(jnp.bfloat16)
-        sent[pl.ds(length, own), :] = noise[...]
-
-
-def gen_part(where, heads, weight, time_w, embed, resid, noise, steps):
+def any_spec():
+    return pl.BlockSpec(memory_space=pl.ANY)
+
+
+def hbm_spec():
+    return pl.BlockSpec(memory_space=pltpu.HBM)
+
+
+def cost(flops, moved):
+    return pl.CostEstimate(flops=flops, bytes_accessed=moved, transcendentals=0)
+
+
+GEN_CUTS = 4
+
+
+def gen_kernel(seq, core, embed, heads, weight, time_w, resid, noise, full, sent, heads_v, weight_v, time_v, resid_v, sems):
+    length, width = full.shape
+    own = resid_v.shape[0]
+    cols = at_block(core[0], width)
+    tile = weight_v.shape[0] // GEN_CUTS
+    copies = [pltpu.make_async_copy(heads, heads_v, sems.at[GEN_CUTS])]
+    for k in range(GEN_CUTS):
+        rows = pl.ds(k * tile, tile)
+        copies.append(pltpu.make_async_copy(weight.at[rows, cols], weight_v.at[rows, :], sems.at[k]))
+    copies.append(pltpu.make_async_copy(time_w.at[:, cols], time_v, sems.at[GEN_CUTS + 1]))
+    copies.append(pltpu.make_async_copy(resid.at[:, cols], resid_v, sems.at[GEN_CUTS + 2]))
+    copies.append(pltpu.make_async_copy(noise.at[:, cols], sent.at[pl.ds(length, own), :], sems.at[GEN_CUTS + 3]))
+    for copy in copies:
+        copy.start()
+    copies[0].wait()
+    total = None
+    for k in range(GEN_CUTS):
+        copies[1 + k].wait()
+        rows = pl.ds(k * tile, tile)
+        term = dot32(heads_v[:, rows], weight_v[rows, :])
+        total = term if total is None else total + term
+    for copy in copies[1 + GEN_CUTS :]:
+        copy.wait()
+    full[...] = total * dot32(embed[...], time_v[...])[0:1]
+    at = at_block(seq[0], own)
+    full[at, :] = full[at, :] + resid_v[...].astype(jnp.float32)
+    sent[pl.ds(0, length), :] = full[...].astype(jnp.bfloat16)
+
+
+def gen_part(seq, core, embed, heads, weight, time_w, resid, noise):
     length, depth = heads.shape
     width = weight.shape[1] // 2
     freq = time_w.shape[0]
     own = resid.shape[0]
-    tile = depth // steps
-    grid_spec = pltpu.PrefetchScalarGridSpec(
-        num_scalar_prefetch=1,
-        grid=(steps,),
-        in_specs=[
-            pl.BlockSpec((length, tile), lambda n, w: (0, n)),
-            pl.BlockSpec((tile, width), lambda n, w: (n, w[1])),
-            pl.BlockSpec((freq, width), lambda n, w: (0, w[1])),
-            pl.BlockSpec((8, freq), lambda n, w: (0, 0)),
-            pl.BlockSpec((own, width), lambda n, w: (0, w[1])),
-            pl.BlockSpec((own, width), lambda n, w: (0, w[1])),
-        ],
-        out_specs=[
-            pl.BlockSpec((length, width), lambda n, w: (0, 0)),
-            pl.BlockSpec((length + own, width), lambda n, w: (0, 0)),
-        ],
-    )
     return pl.pallas_call(
         gen_kernel,
-        grid_spec=grid_spec,
+        in_specs=[smem_spec(), smem_spec(), vmem_spec()] + [hbm_spec()] * 5,
+        out_specs=[vmem_spec()] * 2,
         out_shape=[
             jax.ShapeDtypeStruct((length, width), jnp.float32),
             jax.ShapeDtypeStruct((length + own, width), jnp.bfloat16),
         ],
-        compiler_params=params(56),
+        scratch_shapes=[
+            pltpu.VMEM((length, depth), jnp.bfloat16),
+            pltpu.VMEM((depth, width), jnp.bfloat16),
+            pltpu.VMEM((freq, width), jnp.bfloat16),
+            pltpu.VMEM((own, width), jnp.bfloat16),
+            pltpu.SemaphoreType.DMA((GEN_CUTS + 4,)),
+        ],
+        compiler_params=params(16),
         name="gen_part",
-    )(where, heads, weight, time_w, embed, resid, noise)
-
-
-def mod_kernel(embed, time_a, time_b, time_w, mods, gate):
-    gate[...] = dot32(embed[...], time_w[...])
-    for k in range(3):
-        mods[0, k] = dot32(embed[...], time_a[k])
-        mods[1, k] = dot32(embed[...], time_b[k])
-
-
-def mod_part(embed, time_a, time_b, time_w):
-    width = time_a.shape[2]
-    return pl.pallas_call(
-        mod_kernel,
-        in_specs=[vmem_spec()] * 4,
-        out_specs=[vmem_spec()] * 2,
-        out_shape=[
-            jax.ShapeDtypeStruct((2, 3, 8, width), jnp.float32),
+    )(seq, core, embed, heads, weight, time_w, resid, noise)
+
+
+def load_kernel(role, embed, after, *refs):
+    qkv_a, qkv_b, out_a, out_b, time_a, time_b, time_w = refs[:7]
+    own_qkv_a, own_qkv_b, own_out_a, own_out_b, mods, gate = refs[7:13]
+    time_v, gate_v, sems = refs[13:]
+    cols = at_block(role[0], own_qkv_a.shape[2])
+    rows = at_block(role[0], own_out_a.shape[0])
+    pairs = (
+        (time_a, time_v.at[0]),
+        (time_b, time_v.at[1]),
+        (time_w, gate_v),
+        (qkv_a.at[:, :, cols], own_qkv_a),
+        (qkv_b.at[:, :, cols], own_qkv_b),
+        (out_a.at[rows, :], own_out_a),
+        (out_b.at[rows, :], own_out_b),
+    )
+    copies = [pltpu.make_async_copy(source, goal, sems.at[k]) for k, (source, goal) in enumerate(pairs)]
+    for copy in copies:
+        copy.start()
+    for index in range(2):
+        copies[index].wait()
+        for k in range(3):
+            mods[index, k] = dot32(embed[...], time_v[index, k])
+    copies[2].wait()
+    gate[...] = dot32(embed[...], gate_v[...])
+    for copy in copies[3:]:
+        copy.wait()
+
+
+def load_part(role, embed, after, qkv_a, qkv_b, out_a, out_b, time_a, time_b, time_w, roles):
+    parts, depth, heads_cols = qkv_a.shape
+    part_cols = heads_cols // roles
+    width = time_w.shape[1]
+    freq = time_w.shape[0]
+    moved = 4 * (parts * depth * part_cols + part_cols * width + parts * freq * width)
+    return pl.pallas_call(
+        load_kernel,
+        in_specs=[smem_spec(), vmem_spec(), any_spec()] + [hbm_spec()] * 7,
+        out_specs=[vmem_spec()] * 6,
+        out_shape=[jax.ShapeDtypeStruct((parts, depth, part_cols), jnp.bfloat16)] * 2
+        + [jax.ShapeDtypeStruct((part_cols, width), jnp.bfloat16)] * 2
+        + [
+            jax.ShapeDtypeStruct((2, parts, 8, width), jnp.float32),
             jax.ShapeDtypeStruct((8, width), jnp.float32),
         ],
-        compiler_params=params(16),
-        name="mod_part",
-    )(embed, time_a, time_b, time_w)
+        scratch_shapes=[
+            pltpu.VMEM((2, parts, freq, width), jnp.bfloat16),
+            pltpu.VMEM((freq, width), jnp.bfloat16),
+            pltpu.SemaphoreType.DMA((7,)),
+        ],
+        compiler_params=params(24),
+        cost_estimate=cost(moved, moved),
+        name="load_part",
+    )(role, embed, after, qkv_a, qkv_b, out_a, out_b, time_a, time_b, time_w)
+
+
+def join_kernel(full, arrived, after, joined):
+    length = full.shape[0]
+    own = arrived.shape[0] - length
+    top = full[...] + arrived[pl.ds(0, length), :].astype(jnp.float32)
+    joined[pl.ds(0, length), :] = top.astype(jnp.bfloat16)
+    joined[pl.ds(length, own), :] = arrived[pl.ds(length, own), :]
+
+
+def join_part(full, arrived, after):
+    return pl.pallas_call(
+        join_kernel,
+        in_specs=[vmem_spec(), vmem_spec(), any_spec()],
+        out_specs=vmem_spec(),
+        out_shape=jax.ShapeDtypeStruct(arrived.shape, jnp.bfloat16),
+        compiler_params=params(8),
+        name="join_part",
+    )(full, arrived, after)
 
 
 def project(index, mine, noisy, squares, mods, weight, kept, sent, result):
@@ -247,24 +314,25 @@
                 goal[level][slot // 2, pl.ds(0, length), cols] = result[pl.ds(level * length, length), at].astype(
                     jnp.bfloat16
                 )
-                tail = jnp.where(row_id == 0, result[pl.ds(tokens + level, 1), at], 0.0)
-                tail = jnp.where(row_id == 1, squares[0:1, level * length : (level + 1) * length], tail)
-                goal[level][slot // 2, pl.ds(length, EXTRA_ROWS), cols] = tail.astype(jnp.bfloat16)
-
-
-def first_kernel(where, levels, half, swapped, arrived, noise, mods, weight, *refs):
+            tail = jnp.where(row_id < 2, result[pl.ds(tokens, EXTRA_ROWS), at], 0.0)
+            for level in range(2):
+                tail = jnp.where(row_id == 2 + level, squares[0:1, level * length : (level + 1) * length], tail)
+            goal[0][slot // 2, pl.ds(length, EXTRA_ROWS), cols] = tail.astype(jnp.bfloat16)
+
+
+def first_kernel(seq, core, mine, levels, joined, swapped, noise, mods, weight, *refs):
     latent, noisy, squares, kept_a, kept_b, sent_a, sent_b, values, noises, result = refs
-    length, cols = half.shape
+    length, cols = values.shape[0], joined.shape[1]
     own = latent.shape[0]
     tokens = 2 * length
-    seq, core, mine = where[0], where[1], where[2]
-    values[:, at_block(core, cols)] = half[...]
-    values[:, at_block(1 - core, cols)] = swapped[pl.ds(0, length), :]
-    latent[...] = values[at_block(seq, own), :]
-    noises[at_block(seq, own), :] = noise[...]
-    theirs = at_block(1 - seq, own)
-    noises[theirs, at_block(core, cols)] = arrived[pl.ds(length, own), :]
-    noises[theirs, at_block(1 - core, cols)] = swapped[pl.ds(length, own), :]
+    left, right = at_block(core[0], cols), at_block(1 - core[0], cols)
+    values[:, left] = joined[pl.ds(0, length), :]
+    values[:, right] = swapped[pl.ds(0, length), :]
+    latent[...] = values[at_block(seq[0], own), :]
+    noises[at_block(seq[0], own), :] = noise[...]
+    theirs = at_block(1 - seq[0], own)
+    noises[theirs, left] = joined[pl.ds(length, own), :]
+    noises[theirs, right] = swapped[pl.ds(length, own), :]
     spread = values[...].astype(jnp.float32)
     noise_rows = noises[...].astype(jnp.float32)
     mixed = jnp.concatenate(
@@ -275,26 +343,29 @@
     sums = jnp.sum(wide * wide, axis=1, keepdims=True)
     sums = jnp.broadcast_to(sums, (tokens, length)).T[0:8]
     squares[...] = sums
-    project(0, mine, mixed, sums, mods, weight, (kept_a, kept_b), (sent_a, sent_b), result)
-
-
-def second_kernel(where, noisy, squares, mods, weight, kept_a, kept_b, sent_a, sent_b, result):
-    project(1, where[2], noisy[...], squares[...], mods, weight, (kept_a, kept_b), (sent_a, sent_b), result)
+    project(0, mine[0], mixed, sums, mods, weight, (kept_a, kept_b), (sent_a, sent_b), result)
+
+
+def second_kernel(mine, noisy, squares, mods, weight, kept_a, kept_b, sent_a, sent_b, result):
+    project(1, mine[0], noisy[...], squares[...], mods, weight, (kept_a, kept_b), (sent_a, sent_b), result)
 
 
 def chunk_shapes(length, weight):
     unit = length
     groups = weight.shape[2] // unit
-    return [jax.ShapeDtypeStruct((groups // 2, length + EXTRA_ROWS, 3 * unit), jnp.bfloat16)] * 4
-
-
-def first_part(where, levels, half, swapped, arrived, noise, mods, weight):
-    length, cols = half.shape
+    shapes = [
+        jax.ShapeDtypeStruct((groups // 2, rows, 3 * unit), jnp.bfloat16) for rows in (length + EXTRA_ROWS, length)
+    ]
+    return shapes * 2
+
+
+def first_part(seq, core, mine, levels, joined, swapped, noise, mods, weight):
     own, width = noise.shape
+    length = joined.shape[0] - own
     tokens = 2 * length
     return pl.pallas_call(
         first_kernel,
-        in_specs=[smem_spec(), smem_spec()] + [vmem_spec()] * 6,
+        in_specs=[smem_spec()] * 4 + [vmem_spec()] * 5,
         out_specs=[vmem_spec()] * 7,
         out_shape=[
             jax.ShapeDtypeStruct((own, width), jnp.bfloat16),
@@ -309,10 +380,10 @@
         ],
         compiler_params=params(24),
         name="first_part",
-    )(where, levels, half, swapped, arrived, noise, mods, weight)
-
-
-def second_part(where, noisy, squares, mods, weight):
+    )(seq, core, mine, levels, joined, swapped, noise, mods, weight)
+
+
+def second_part(mine, noisy, squares, mods, weight):
     tokens = noisy.shape[0]
     return pl.pallas_call(
         second_kernel,
@@ -322,19 +393,22 @@
         scratch_shapes=[pltpu.VMEM((tokens + EXTRA_ROWS, weight.shape[2]), jnp.float32)],
         compiler_params=params(24),
         name="second_part",
-    )(where, noisy, squares, mods, weight)
+    )(mine, noisy, squares, mods, weight)
 
 
 def attend_kernel(width, kept_a, other_a, kept_b, other_b, gains, out):
     _, length, unit = out.shape
+    extra = None
     for level, (kept, other) in enumerate(((kept_a, other_a), (kept_b, other_b))):
         mixed = kept[...] + other[...].astype(jnp.float32)
-        squares = jnp.broadcast_to(mixed[length + 1 : length + 2, :unit], (unit, unit)).T
+        if level == 0:
+            extra = mixed[length:]
+        squares = jnp.broadcast_to(extra[2 + level : 3 + level, :unit], (unit, unit)).T
         factor = lax.rsqrt(squares * (1.0 / width) + 1e-06)
 
         def pick(part):
             cols = slice(part * unit, (part + 1) * unit)
-            return mixed[:length, cols] * factor + mixed[length : length + 1, cols]
+            return mixed[:length, cols] * factor + extra[level : level + 1, cols]
 
         def normed(part):
             rows = pick(part)
@@ -365,14 +439,13 @@
     )(kept_a, chunks[0][1], kept_b, chunks[1][1], gains)
 
 
-def out_kernel(where, *refs):
+def out_kernel(core, mine, *refs):
     heads_a, heads_b = refs[0:4], refs[4:8]
     weight_a, weight_b, mods, kept, sent, rows, total = refs[8:]
     _, length, unit = heads_a[0].shape
-    core, mine = where[1], where[2]
     for index, (heads, weight) in enumerate(((heads_a, weight_a), (heads_b, weight_b))):
         for slot, head in enumerate(heads):
-            at = at_block(jnp.bitwise_xor(mine, slot), unit)
+            at = at_block(jnp.bitwise_xor(mine[0], slot), unit)
             for level in range(2):
                 rows[pl.ds(level * length, length), at] = head[level]
         result = dot32(rows[...], weight[...])
@@ -383,16 +456,16 @@
         else:
             total[...] = total[...] + 0.5 * signed
     cols = kept.shape[1]
-    kept[...] = total[:, at_block(core, cols)]
-    sent[...] = total[:, at_block(1 - core, cols)].astype(jnp.bfloat16)
-
-
-def out_part(where, heads_a, heads_b, weight_a, weight_b, mods):
+    kept[...] = total[:, at_block(core[0], cols)]
+    sent[...] = total[:, at_block(1 - core[0], cols)].astype(jnp.bfloat16)
+
+
+def out_part(core, mine, heads_a, heads_b, weight_a, weight_b, mods):
     _, length, unit = heads_a[0].shape
     depth, width = weight_a.shape
     return pl.pallas_call(
         out_kernel,
-        in_specs=[smem_spec()] + [vmem_spec()] * 11,
+        in_specs=[smem_spec()] * 2 + [vmem_spec()] * 11,
         out_specs=[vmem_spec()] * 2,
         out_shape=[
             jax.ShapeDtypeStruct((length, width // 2), jnp.float32),
@@ -404,42 +477,36 @@
         ],
         compiler_params=params(16),
         name="out_part",
-    )(where, *heads_a, *heads_b, weight_a, weight_b, mods)
-
-
-def grad_kernel(where, heads_t, mine, theirs, out, rows):
-    cols = mine.shape[1]
-
-    @pl.when(pl.program_id(0) == 0)
-    def _():
-        rows[:, at_block(where[1], cols)] = mine[...]
-        rows[:, at_block(1 - where[1], cols)] = theirs[...]
-
-    out[...] = dot32(heads_t[...], rows[...]).astype(jnp.bfloat16)
-
-
-def grad_part(where, heads_t, mine, theirs, steps):
+    )(core, mine, *heads_a, *heads_b, weight_a, weight_b, mods)
+
+
+def grad_kernel(half, heads_t, rows, *refs):
+    refs[-1][...] = dot32(heads_t[...], rows[...]).astype(jnp.bfloat16)
+
+
+def grad_part(half, heads_t, rows, before, steps):
     depth, length = heads_t.shape
-    cols = mine.shape[1]
+    cols = rows.shape[1]
     tile = depth // steps
+    rest = [] if before is None else [before]
     grid_spec = pltpu.PrefetchScalarGridSpec(
         num_scalar_prefetch=1,
         grid=(steps,),
         in_specs=[
             pl.BlockSpec((tile, length), lambda n, w: (n, 0)),
             pl.BlockSpec((length, cols), lambda n, w: (0, 0)),
-            pl.BlockSpec((length, cols), lambda n, w: (0, 0)),
-        ],
-        out_specs=pl.BlockSpec((tile, 2 * cols), lambda n, w: (n, 0)),
-        scratch_shapes=[pltpu.VMEM((length, 2 * cols), jnp.bfloat16)],
+        ]
+        + [any_spec()] * len(rest),
+        out_specs=pl.BlockSpec((tile, cols), lambda n, w: (n, w[0])),
     )
     return pl.pallas_call(
         grad_kernel,
         grid_spec=grid_spec,
         out_shape=jax.ShapeDtypeStruct((depth, 2 * cols), jnp.bfloat16),
+        input_output_aliases={3: 0} if rest else {},
         compiler_params=params(24),
         name="grad_part",
-    )(where, heads_t, mine, theirs)
+    )(half, heads_t, rows, *rest)
 
 
 def exchange(array, axis, bit):
@@ -471,29 +538,26 @@
     role, seq, mp = lax.axis_index("role"), lax.axis_index("seq"), lax.axis_index("mp")
     part_cols = gen_heads.shape[1] // roles
     freq = gen_time_w.shape[0]
-    core = role % 2
-    where = jnp.stack([seq, core, mp]).astype(jnp.int32)
+    role_at, seq_at, mine = [v.astype(jnp.int32).reshape(1) for v in (role, seq, mp)]
+    core = role_at % 2
     half_cols = gen_resid.shape[1] // 2
 
     embed = jax.vmap(lambda t: time_embed(t, freq))(steps)
     embed = jnp.concatenate([embed, jnp.zeros((5, freq), jnp.bfloat16)], axis=0)
     levels = steps[1:3].astype(jnp.float32) / 1000.0
-    full, sent = gen_part(where, gen_heads, gen_out_w, gen_time_w, embed, gen_resid, noise, 4)
+    full, sent = gen_part(seq_at, core, embed, gen_heads, gen_out_w, gen_time_w, gen_resid, noise)
     arrived = exchange(sent, "seq", 1)
+    planes = [w.transpose(1, 0, 2) for w in (teacher_qkv, critic_qkv, teacher_time, critic_time)]
+    weight_a, weight_b, out_a, out_b, mods, gate = load_part(
+        role_at, embed, full, planes[0], planes[1], teacher_out, critic_out, planes[2], planes[3], gen_time_w, roles
+    )
+    joined = join_part(full, arrived, gate)
+    swapped = exchange(joined, "role", 1)
+    first = first_part(seq_at, core, mine, levels, joined, swapped, noise, mods, weight_a)
+    latent, noisy, squares = first[:3]
+    second = second_part(mine, noisy, squares, mods, weight_b)
 
     start = role * part_cols
-    weight_a = lax.dynamic_slice_in_dim(teacher_qkv.transpose(1, 0, 2), start, part_cols, axis=2)
-    weight_b = lax.dynamic_slice_in_dim(critic_qkv.transpose(1, 0, 2), start, part_cols, axis=2)
-    mods, gate = mod_part(embed, teacher_time.transpose(1, 0, 2), critic_time.transpose(1, 0, 2), gen_time_w)
-
-    half = both(full, arrived[:length]).astype(jnp.bfloat16)
-    swapped = exchange(jnp.concatenate([half, arrived[length:]], axis=0), "role", 1)
-    first = first_part(where, levels, half, swapped, arrived, noise, mods, weight_a)
-    latent, noisy, squares = first[:3]
-    second = second_part(where, noisy, squares, mods, weight_b)
-
-    out_a = lax.dynamic_slice_in_dim(teacher_out, start, part_cols, axis=0)
-    out_b = lax.dynamic_slice_in_dim(critic_out, start, part_cols, axis=0)
     unit = part_cols // groups
     gathered = []
     for chunks, gains in ((first[3:], teacher_norm), (second, critic_norm)):
@@ -508,7 +572,7 @@
         far = exchange(head_out, "mp", 2)
         gathered.append((head_out, near, far, exchange(far, "mp", 1)))
 
-    kept, sent = out_part(where, *gathered, out_a, out_b, mods)
+    kept, sent = out_part(core, mine, *gathered, out_a, out_b, mods)
     total = both(kept, exchange(sent, "role", 1)).astype(jnp.bfloat16)
     middle = length // 2
     top, low = total[:middle], total[middle:]
@@ -516,9 +580,12 @@
     low = both(low, exchange(low, "role", 2)).astype(jnp.bfloat16)
     top = both(top, exchange(top, "role", 2))
     low = both(low, exchange(low, "seq", 1))
-    gate_row = lax.dynamic_slice_in_dim(gate, core * half_cols, half_cols, axis=1)[0:1]
+    gate_row = lax.dynamic_slice_in_dim(gate, core[0] * half_cols, half_cols, axis=1)[0:1]
     rows = (gate_row * jnp.concatenate([top, low], axis=0)).astype(jnp.bfloat16)
-    weight_grad = grad_part(where, gen_heads.T, rows, exchange(rows, "role", 1), 4)
+    heads_t = gen_heads.T
+    theirs = exchange(rows, "role", 1)
+    weight_grad = grad_part(core, heads_t, rows, None, 2)
+    weight_grad = grad_part(1 - core, heads_t, theirs, weight_grad, 2)
     return latent, weight_grad
 
 

time: 108 us -> 103 us (0.954)
  waiting for transfers between devices: 45.8 us -> 37.5 us
  local copies, waits for them, and re-layouts: 14.3 us -> 20.7 us
  other arithmetic: 4.24 us -> 1.21 us
  Pallas kernels: 18.2 us -> 16.5 us
  starting transfers between devices: 24.1 us -> 25.8 us
    unnamed x23 -> x41, local copies, waits for them, and re-layouts: 4.11 us -> 19.9 us
    dynamic_slice x2 -> x0, local copies, waits for them, and re-layouts: 9.36 us -> none  [the longest x1 7.48 us: heads_per_role(): lax.dynamic_slice_in_dim(critic_qkv.transpose(1, 0, 2), start, part_cols,...]
    ppermute x22, waiting for transfers between devices: 45.8 us -> 37.5 us  [exchange(): lax.ppermute(array, axis, [(i, i ^ bit) for i in range(lax.axis_size(axis...]
    ppermute x22, starting transfers between devices: 24.1 us -> 25.8 us  [exchange(): lax.ppermute(array, axis, [(i, i ^ bit) for i in range(lax.axis_size(axis...]
    pallas_call x4 -> x5, Pallas kernels: 10.4 us -> 9.42 us  [the longest x1 4.18 us: load_part(): pl.pallas_call(load_kernel, in_specs=[smem_spec(), vmem_spec(), any_spec(...]
    pallas_call x1 -> x2, Pallas kernels: 4.19 us -> 4.1 us  [grad_part(): pl.pallas_call(grad_kernel, grid_spec=grid_spec, out_shape=jax.ShapeDtype...]
  transfers between devices with their start and end apart: 22 -> 22, of which waited for: 17 -> 15; matrix products, arithmetic and copies ran while one was open for 10% -> 1% of each run, Pallas kernels for 2% -> 8%
where the time goes in v2:
time: 103 us
  waiting for transfers between devices  37.5 us (36%)
  starting transfers between devices  25.8 us (25%)
  local copies, waits for them, and re-layouts  20.7 us (20%)
  Pallas kernels  16.5 us (16%)
  other arithmetic  1.21 us (1%)
    ppermute x22, waiting for transfers between devices, exchange(): lax.ppermute(array, axis, [(i, i ^ bit) for i in range(lax.axis_size(axis...  37.5 us
    ppermute x22, starting transfers between devices, exchange(): lax.ppermute(array, axis, [(i, i ^ bit) for i in range(lax.axis_size(axis...  25.8 us
    unnamed x41, local copies, waits for them, and re-layouts  19.9 us
    pallas_call x1, Pallas kernels, load_part(): pl.pallas_call(load_kernel, in_specs=[smem_spec(), vmem_spec(), any_spec(...  4.18 us
    pallas_call x2, Pallas kernels, grad_part(): pl.pallas_call(grad_kernel, grid_spec=grid_spec, out_shape=jax.ShapeDtype...  4.1 us
    pallas_call x1, Pallas kernels, first_part(): pl.pallas_call(first_kernel, in_specs=[smem_spec()] * 4 + [vmem_spec()] *...  2.65 us
  transfers between devices with their start and end apart: 22, of which 15 were waited for; matrix products, arithmetic and copies ran while one was open for 1% of the time, Pallas kernels for 8%

profile of v2, /device:TPU:1, one launch (start us, length us, event | category | flops | bytes accessed | tf_op | source)
XLA Modules:
  0.0 102.6 jit_solution(488965739451588204)
XLA Ops:
  0.7 0.7 convert_element_type.87
  1.3 0.1 fusion.8
  1.5 2.6 %copy-done.3 = bf16[2048,1280]{1,0:T(8,128)(2,1)S(1)} copy-done((bf16[2048,1280]{1,0:T(8,128)(2,1)S(1)}, bf16[2048,1280]{1,0:T(8,128)(2,1)}, u32[]{:S(2)}) %copy-start.3) | copy-done | bytes 5242904
  4.1 1.4 %copy-done.8 = bf16[256,1280]{1,0:T(8,128)(2,1)S(1)} copy-done((bf16[256,1280]{1,0:T(8,128)(2,1)S(1)}, bf16[256,1280]{1,0:T(8,128)(2,1)}, u32[]{:S(2)}) %copy-start.8) | copy-done | bytes 655384
  5.5 1.0 %copy-done.10 = bf16[128,2048]{1,0:T(8,128)(2,1)S(1)} copy-done((bf16[128,2048]{1,0:T(8,128)(2,1)S(1)}, bf16[128,2048]{1,0:T(8,128)(2,1)}, u32[]{:S(2)}) %copy-start.10) | copy-done | bytes 524312
  6.6 0.9 copy-done.16
  7.5 0.9 copy-done.18
  8.4 1.6 %gen_part.1 = (f32[128,640]{1,0:T(8,128)S(1)}, bf16[192,640]{1,0:T(8,128)(2,1)S(1)}) custom-call(s32[1]{0:T(128)} %bitcast.seq, s32[1]{0:T(128)S(6)} %select_n.14.core.half, bf16[8,256]{1,0:T(8,128)(2,1)S(1)} %fusion.7.embed, bf16[128,2048]{1,0:T(8,128)(2,1)S(1)} %copy-done.10, bf16[2048,1280]{1,0:T(8,128)(2,1)S(1)} %copy-done.3, ...), custom_call_target="tpu_custom_call" | custom-call | tf_op jit(solution)/shard_map/gen_part/pallas_call | solution.py:200
  10.0 2.1 %collective-permute-start = (bf16[192,640]{1,0:T(8,128)(2,1)S(1)}, bf16[192,640]{1,0:T(8,128)(2,1)S(1)}, u32[]{:S(2)}, u32[]{:S(2)}) collective-permute-start(bf16[192,640]{1,0:T(8,128)(2,1)S(1)} %get-tuple-element.24), channel_id=1, source_target_pairs={{0,4},{4,0},{1,5},{5,1},{2,6},{6,2},{3,7},{7,3},{8,12},{12,8},{9,1... | collective-permute-start | bytes 737288 | tf_op jit(solution)/shard_map/ppermute | solution.py:513
  12.1 2.5 %copy-done.2 = bf16[2048,1280]{1,0:T(8,128)(2,1)S(1)} copy-done((bf16[2048,1280]{1,0:T(8,128)(2,1)S(1)}, bf16[2048,1280]{1,0:T(8,128)(2,1)}, u32[]{:S(2)}) %copy-start.2) | copy-done | bytes 5242904
  14.6 1.5 %copy-done.12 = bf16[256,3,1280]{2,0,1:T(8,128)(2,1)S(1)} copy-done((bf16[256,3,1280]{2,0,1:T(8,128)(2,1)S(1)}, bf16[256,3,1280]{2,0,1:T(8,128)(2,1)}, u32[]{:S(2)}) %copy-start.12) | copy-done | bytes 1966104
  16.1 1.5 %copy-done.13 = bf16[256,3,1280]{2,0,1:T(8,128)(2,1)S(1)} copy-done((bf16[256,3,1280]{2,0,1:T(8,128)(2,1)S(1)}, bf16[256,3,1280]{2,0,1:T(8,128)(2,1)}, u32[]{:S(2)}) %copy-start.13) | copy-done | bytes 1966104
  17.7 4.2 %load_part.1 = (bf16[3,1280,512]{2,1,0:T(8,128)(2,1)S(1)}, bf16[3,1280,512]{2,1,0:T(8,128)(2,1)S(1)}, bf16[512,1280]{1,0:T(8,128)(2,1)S(1)}, bf16[512,1280]{1,0:...) custom-call(s32[1]{0:T(128)} %bitcast.1.role, bf16[8,256]{1,0:T(8,128)(2,1)S(1)} %fusion.7.embed, ...), custom_call_target="tpu_custom_call" | custom-call | flops 14417920 | bytes 14417920 | tf_op jit(solution)/shard_map/load_part/pallas_call | solution.py:254
  21.9 1.9 %copy-done.4 = bf16[3,1280,512]{2,1,0:T(8,128)(2,1)} copy-done((bf16[3,1280,512]{2,1,0:T(8,128)(2,1)}, bf16[3,1280,512]{2,1,0:T(8,128)(2,1)S(1)}, u32[]{:S(2)}) %copy-start.4) | copy-done | bytes 3932184
  23.7 1.9 %copy-done.6 = bf16[3,1280,512]{2,1,0:T(8,128)(2,1)} copy-done((bf16[3,1280,512]{2,1,0:T(8,128)(2,1)}, bf16[3,1280,512]{2,1,0:T(8,128)(2,1)S(1)}, u32[]{:S(2)}) %copy-start.6) | copy-done | bytes 3932184
  25.7 1.1 %copy-done.14 = bf16[512,1280]{1,0:T(8,128)(2,1)} copy-done((bf16[512,1280]{1,0:T(8,128)(2,1)}, bf16[512,1280]{1,0:T(8,128)(2,1)S(1)}, u32[]{:S(2)}) %copy-start.14) | copy-done | bytes 1310744
  26.8 1.0 collective-permute-start.1
  27.9 0.1 convert_multiply_fusion.levels
  27.9 1.1 %collective-permute-done.1.swapped = bf16[192,640]{1,0:T(8,128)(2,1)S(1)} collective-permute-done((bf16[192,640]{1,0:T(8,128)(2,1)S(1)}, bf16[192,640]{1,0:T(8,128)(2,1)S(1)}, u32[]{:S(2)}, u32[]{:S(2)}) %collective-permute-start.1) | collective-permute-done | bytes 245792 | tf_op jit(solution)/shard_map/ppermute | solution.py:513
  29.0 2.2 %copy-done.7 = bf16[3,1280,512]{2,1,0:T(8,128)(2,1)S(1)} copy-done((bf16[3,1280,512]{2,1,0:T(8,128)(2,1)S(1)}, bf16[3,1280,512]{2,1,0:T(8,128)(2,1)}, u32[]{:S(2)}) %copy-start.7) | copy-done | bytes 3932184
  31.1 2.6 %first_part.1 = (bf16[64,1280]{1,0:T(8,128)(2,1)}, bf16[256,1280]{1,0:T(8,128)(2,1)S(1)}, f32[8,256]{1,0:T(8,128)S(1)}, bf16[2,144,384]{2,1,0:T(8,128)(2,1)S(1)}...) custom-call(s32[1]{0:T(128)} %bitcast.seq, ...), custom_call_target="tpu_custom_call" | custom-call | tf_op jit(solution)/shard_map/first_part/pallas_call | solution.py:366
  33.8 1.4 %second_part.1 = (bf16[2,144,384]{2,1,0:T(8,128)(2,1)S(1)}, bf16[2,128,384]{2,1,0:T(8,128)(2,1)S(1)}, bf16[2,144,384]{2,1,0:T(8,128)(2,1)S(1)}, bf16[2,128,384]{2,1,0:T(8,128)(2,1)S(1)}) custom-call(s32[1]{0:T(128)} %bitcast.2.mine, bf16[256,1280]{1,0:T(8,128)(2,1)S(1)} %get-tuple-element.33.noisy, f32[8,256]{1,0:T(8,128)S(1)} %get-tuple-element.34.squares, ...), custom_call_target="tpu_custom_call" | custom-call | tf_op jit(solution)/shard_map/second_part/pallas_call | solution.py:388
  35.2 1.4 %collective-permute-start.11 = (bf16[2,128,384]{2,1,0:T(8,128)(2,1)S(1)}, bf16[2,128,384]{2,1,0:T(8,128)(2,1)S(1)}, u32[]{:S(2)}, u32[]{:S(2)}) collective-permute-start(bf16[2,128,384]{2,1,0:T(8,128)(2,1)S(1)} %get-tuple-element.39), channel_id=1, source_target_pairs={{0,1},{1,0},{2,3},{3,2},{4,5},{5,4},{6,7},{7,6},{8,9},{9,8},{10,11... | collective-permute-start | bytes 589832 | tf_op jit(solution)/shard_map/ppermute | solution.py:513
  36.6 0.7 constant_dynamic-slice_fusion.1.refs_4_
  37.3 0.2 collective-permute-start.9
  37.4 1.3 %collective-permute-start.4 = (bf16[2,128,384]{2,1,0:T(8,128)(2,1)S(1)}, bf16[2,128,384]{2,1,0:T(8,128)(2,1)S(1)}, u32[]{:S(2)}, u32[]{:S(2)}) collective-permute-start(bf16[2,128,384]{2,1,0:T(8,128)(2,1)S(1)} %get-tuple-element.32), channel_id=1, source_target_pairs={{0,1},{1,0},{2,3},{3,2},{4,5},{5,4},{6,7},{7,6},{8,9},{9,8},{10,11... | collective-permute-start | bytes 589832 | tf_op jit(solution)/shard_map/ppermute | solution.py:513
  38.7 0.2 collective-permute-start.2
  38.9 2.5 %collective-permute-done.11 = bf16[2,128,384]{2,1,0:T(8,128)(2,1)S(1)} collective-permute-done((bf16[2,128,384]{2,1,0:T(8,128)(2,1)S(1)}, bf16[2,128,384]{2,1,0:T(8,128)(2,1)S(1)}, u32[]{:S(2)}, u32[]{:S(2)}) %collective-permute-start.11) | collective-permute-done | bytes 196640 | tf_op jit(solution)/shard_map/ppermute | solution.py:513
  41.5 2.4 %collective-permute-start.12 = (bf16[128,384]{1,0:T(8,128)(2,1)S(1)}, bf16[128,384]{1,0:T(8,128)(2,1)S(1)}, u32[]{:S(2)}, u32[]{:S(2)}) collective-permute-start(bf16[128,384]{1,0:T(8,128)(2,1)S(1)} %fusion.4), channel_id=1, source_target_pairs={{0,2},{1,3},{2,0},{3,1},{4,6},{5,7},{6,4},{7,5},{8,10},{9,11},{10,... | collective-permute-start | bytes 294920 | tf_op jit(solution)/shard_map/ppermute | solution.py:513
  43.9 8.6 %collective-permute-done.4 = bf16[2,128,384]{2,1,0:T(8,128)(2,1)S(1)} collective-permute-done((bf16[2,128,384]{2,1,0:T(8,128)(2,1)S(1)}, bf16[2,128,384]{2,1,0:T(8,128)(2,1)S(1)}, u32[]{:S(2)}, u32[]{:S(2)}) %collective-permute-start.4) | collective-permute-done | bytes 196640 | tf_op jit(solution)/shard_map/ppermute | solution.py:513
  52.6 1.5 %collective-permute-start.5 = (bf16[128,384]{1,0:T(8,128)(2,1)S(1)}, bf16[128,384]{1,0:T(8,128)(2,1)S(1)}, u32[]{:S(2)}, u32[]{:S(2)}) collective-permute-start(bf16[128,384]{1,0:T(8,128)(2,1)S(1)} %fusion.3), channel_id=1, source_target_pairs={{0,2},{1,3},{2,0},{3,1},{4,6},{5,7},{6,4},{7,5},{8,10},{9,11},{10,... | collective-permute-start | bytes 294920 | tf_op jit(solution)/shard_map/ppermute | solution.py:513
  54.1 0.1 convert_add_fusion
  54.2 1.0 collective-permute-start.10
  55.2 3.5 %collective-permute-done.2 = bf16[2,144,384]{2,1,0:T(8,128)(2,1)S(1)} collective-permute-done((bf16[2,144,384]{2,1,0:T(8,128)(2,1)S(1)}, bf16[2,144,384]{2,1,0:T(8,128)(2,1)S(1)}, u32[]{:S(2)}, u32[]{:S(2)}) %collective-permute-start.2) | collective-permute-done | bytes 221216 | tf_op jit(solution)/shard_map/ppermute | solution.py:513
  58.7 0.1 convert_add_fusion.1
  58.8 0.2 collective-permute-start.3
  59.0 9.5 %collective-permute-done.10.refs_1_ = bf16[144,384]{1,0:T(8,128)(2,1)S(1)} collective-permute-done((bf16[144,384]{1,0:T(8,128)(2,1)S(1)}, bf16[144,384]{1,0:T(8,128)(2,1)S(1)}, u32[]{:S(2)}, u32[]{:S(2)}) %collective-permute-start.10) | collective-permute-done | bytes 110624 | tf_op jit(solution)/shard_map/ppermute | solution.py:513
  68.5 0.8 attend_part.3.refs_4_
  69.3 0.1 collective-permute-start.14
  69.4 1.5 %collective-permute-done.3.refs_1_ = bf16[144,384]{1,0:T(8,128)(2,1)S(1)} collective-permute-done((bf16[144,384]{1,0:T(8,128)(2,1)S(1)}, bf16[144,384]{1,0:T(8,128)(2,1)S(1)}, u32[]{:S(2)}, u32[]{:S(2)}) %collective-permute-start.3) | collective-permute-done | bytes 110624 | tf_op jit(solution)/shard_map/ppermute | solution.py:513
  70.9 0.8 attend_part.2.refs_0_
  71.7 0.9 collective-permute-start.7
  72.6 3.8 %collective-permute-start.13 = (bf16[2,128,128]{2,1,0:T(8,128)(2,1)S(1)}, bf16[2,128,128]{2,1,0:T(8,128)(2,1)S(1)}, u32[]{:S(2)}, u32[]{:S(2)}) collective-permute-start(bf16[2,128,128]{2,1,0:T(8,128)(2,1)S(1)} %attend_part.3.refs_4_), channel_id=1, source_target_pairs={{0,1},{1,0},{2,3},{3,2},{4,5},{5,4},{6,7},{7,6},{8,9},{9,8},{10,11... | collective-permute-start | bytes 196616 | tf_op jit(solution)/shard_map/ppermute | solution.py:513
  76.4 1.4 %collective-permute-start.15 = (bf16[2,128,128]{2,1,0:T(8,128)(2,1)S(1)}, bf16[2,128,128]{2,1,0:T(8,128)(2,1)S(1)}, u32[]{:S(2)}, u32[]{:S(2)}) collective-permute-start(bf16[2,128,128]{2,1,0:T(8,128)(2,1)S(1)} %collective-permute-done.14.refs_6_), channel_id=1, source_target_pairs={{0,1},{1,0},{2,3},{3,2},{4,5},{5,4},{6,7},{7,6},{8,9},{9,8},{10,11... | collective-permute-start | bytes 196616 | tf_op jit(solution)/shard_map/ppermute | solution.py:513
  77.9 0.4 collective-permute-start.8
  78.3 0.6 collective-permute-done.13.refs_5_
  78.9 1.4 %collective-permute-done.6.refs_1_ = bf16[2,128,128]{2,1,0:T(8,128)(2,1)S(1)} collective-permute-done((bf16[2,128,128]{2,1,0:T(8,128)(2,1)S(1)}, bf16[2,128,128]{2,1,0:T(8,128)(2,1)S(1)}, u32[]{:S(2)}, u32[]{:S(2)}) %collective-permute-start.6) | collective-permute-done | bytes 65568 | tf_op jit(solution)/shard_map/ppermute | solution.py:513
  80.3 1.4 %collective-permute-done.15.refs_7_ = bf16[2,128,128]{2,1,0:T(8,128)(2,1)S(1)} collective-permute-done((bf16[2,128,128]{2,1,0:T(8,128)(2,1)S(1)}, bf16[2,128,128]{2,1,0:T(8,128)(2,1)S(1)}, u32[]{:S(2)}, u32[]{:S(2)}) %collective-permute-start.15) | collective-permute-done | bytes 65568 | tf_op jit(solution)/shard_map/ppermute | solution.py:513
  81.7 1.4 %collective-permute-done.8.refs_3_ = bf16[2,128,128]{2,1,0:T(8,128)(2,1)S(1)} collective-permute-done((bf16[2,128,128]{2,1,0:T(8,128)(2,1)S(1)}, bf16[2,128,128]{2,1,0:T(8,128)(2,1)S(1)}, u32[]{:S(2)}, u32[]{:S(2)}) %collective-permute-start.8) | collective-permute-done | bytes 65568 | tf_op jit(solution)/shard_map/ppermute | solution.py:513
  83.1 1.0 out_part.1
  84.1 1.4 %collective-permute-start.16 = (bf16[128,640]{1,0:T(8,128)(2,1)S(1)}, bf16[128,640]{1,0:T(8,128)(2,1)S(1)}, u32[]{:S(2)}, u32[]{:S(2)}) collective-permute-start(bf16[128,640]{1,0:T(8,128)(2,1)S(1)} %get-tuple-element.43), channel_id=1, source_target_pairs={{0,8},{8,0},{16,24},{24,16},{1,9},{9,1},{17,25},{25,17},{2,10},{10... | collective-permute-start | bytes 491528 | tf_op jit(solution)/shard_map/ppermute | solution.py:513
  85.5 1.0 %collective-permute-done.16 = bf16[128,640]{1,0:T(8,128)(2,1)S(1)} collective-permute-done((bf16[128,640]{1,0:T(8,128)(2,1)S(1)}, bf16[128,640]{1,0:T(8,128)(2,1)S(1)}, u32[]{:S(2)}, u32[]{:S(2)}) %collective-permute-start.16) | collective-permute-done | bytes 163872 | tf_op jit(solution)/shard_map/ppermute | solution.py:513
  86.6 0.3 collective-permute-start.17
  86.9 1.2 %collective-permute-start.19 = (bf16[64,640]{1,0:T(8,128)(2,1)S(1)}, bf16[64,640]{1,0:T(8,128)(2,1)S(1)}, u32[]{:S(2)}, u32[]{:S(2)}) collective-permute-start(bf16[64,640]{1,0:T(8,128)(2,1)S(1)} %get-tuple-element.47), channel_id=1, source_target_pairs={{0,16},{8,24},{16,0},{24,8},{1,17},{9,25},{17,1},{25,9},{2,18},{10... | collective-permute-start | bytes 245768 | tf_op jit(solution)/shard_map/ppermute | solution.py:513
  88.1 2.2 %collective-permute-done.17 = bf16[64,640]{1,0:T(8,128)(2,1)S(1)} collective-permute-done((bf16[64,640]{1,0:T(8,128)(2,1)S(1)}, bf16[64,640]{1,0:T(8,128)(2,1)S(1)}, u32[]{:S(2)}, u32[]{:S(2)}) %collective-permute-start.17) | collective-permute-done | bytes 81952 | tf_op jit(solution)/shard_map/ppermute | solution.py:513
  90.3 0.2 collective-permute-done.19
  90.5 1.3 %collective-permute-start.18 = (bf16[64,640]{1,0:T(8,128)(2,1)S(1)}, bf16[64,640]{1,0:T(8,128)(2,1)S(1)}, u32[]{:S(2)}, u32[]{:S(2)}) collective-permute-start(bf16[64,640]{1,0:T(8,128)(2,1)S(1)} %get-tuple-element.44), channel_id=1, source_target_pairs={{0,16},{8,24},{16,0},{24,8},{1,17},{9,25},{17,1},{25,9},{2,18},{10... | collective-permute-start | bytes 245768 | tf_op jit(solution)/shard_map/ppermute | solution.py:513
  91.8 1.0 collective-permute-start.20
  92.8 1.1 %collective-permute-done.18 = bf16[64,640]{1,0:T(8,128)(2,1)S(1)} collective-permute-done((bf16[64,640]{1,0:T(8,128)(2,1)S(1)}, bf16[64,640]{1,0:T(8,128)(2,1)S(1)}, u32[]{:S(2)}, u32[]{:S(2)}) %collective-permute-start.18) | collective-permute-done | bytes 81952 | tf_op jit(solution)/shard_map/ppermute | solution.py:513
  93.9 1.6 %collective-permute-done.20 = bf16[64,640]{1,0:T(8,128)(2,1)S(1)} collective-permute-done((bf16[64,640]{1,0:T(8,128)(2,1)S(1)}, bf16[64,640]{1,0:T(8,128)(2,1)S(1)}, u32[]{:S(2)}, u32[]{:S(2)}) %collective-permute-start.20) | collective-permute-done | bytes 81952 | tf_op jit(solution)/shard_map/ppermute | solution.py:513
  95.5 2.7 %collective-permute-start.21 = (bf16[128,640]{1,0:T(8,128)(2,1)S(1)}, bf16[128,640]{1,0:T(8,128)(2,1)S(1)}, u32[]{:S(2)}, u32[]{:S(2)}) collective-permute-start(bf16[128,640]{1,0:T(8,128)(2,1)S(1)} %fusion.rows), channel_id=1, source_target_pairs={{0,8},{8,0},{16,24},{24,16},{1,9},{9,1},{17,25},{25,17},{2,10},{10... | collective-permute-start | bytes 491528 | tf_op jit(solution)/shard_map/ppermute | solution.py:513
  98.2 0.3 copy.17
  98.5 2.1 %grad_part.2.refs_0_ = bf16[2048,1280]{1,0:T(8,128)(2,1)} custom-call(s32[1]{0:T(128)S(6)} %select_n.14.core.half, bf16[2048,128]{1,0:T(8,128)(2,1)S(1)} %bitcast.25, bf16[128,640]{1,0:T(8,128)(2,1)S(1)} %fusion.rows), custom_call_target="tpu_custom_call" | custom-call | tf_op jit(solution)/shard_map/grad_part/pallas_call | solution.py:502
  100.6 2.0 %grad_part.3 = bf16[2048,1280]{1,0:T(8,128)(2,1)} custom-call(s32[1]{0:T(128)S(6)} %sub.3.half, bf16[2048,128]{1,0:T(8,128)(2,1)S(1)} %bitcast.26, bf16[128,640]{1,0:T(8,128)(2,1)S(1)} %collective-permute-done.21.rows, bf16[2048,1280]{1,0:T(8,128)(2,1)} %grad_part.2.refs_0_), custom_call_target="tpu_custom_call", output_to_operand_aliasing={{}: (3, {})} | custom-call | tf_op jit(solution)/shard_map/grad_part/pallas_call | solution.py:502
  (57 shorter events, 0.6 us)
Async XLA Ops:
  0.6 36.0 %copy-start = (f32[2,2048]{1,0:T(2,128)S(1)}, f32[2,2048]{1,0:T(2,128)}, u32[]{:S(2)}) copy-start(f32[2,2048]{1,0:T(2,128)} %param.27) | copy-start | bytes 49156
  1.3 10.8 %copy-start.1 = (bf16[2048,1280]{1,0:T(8,128)(2,1)S(1)}, bf16[2048,1280]{1,0:T(8,128)(2,1)}, u32[]{:S(2)}) copy-start(bf16[2048,1280]{1,0:T(8,128)(2,1)} %refs_2_.1) | copy-start | bytes 15728644
  1.5 2.6 %copy-start.3 = (bf16[2048,1280]{1,0:T(8,128)(2,1)S(1)}, bf16[2048,1280]{1,0:T(8,128)(2,1)}, u32[]{:S(2)}) copy-start(bf16[2048,1280]{1,0:T(8,128)(2,1)} %weight.1) | copy-start | bytes 15728644
  4.1 1.4 %copy-start.8 = (bf16[256,1280]{1,0:T(8,128)(2,1)S(1)}, bf16[256,1280]{1,0:T(8,128)(2,1)}, u32[]{:S(2)}) copy-start(bf16[256,1280]{1,0:T(8,128)(2,1)} %refs_6_.1) | copy-start | bytes 1966084
  5.5 1.0 %copy-start.10 = (bf16[128,2048]{1,0:T(8,128)(2,1)S(1)}, bf16[128,2048]{1,0:T(8,128)(2,1)}, u32[]{:S(2)}) copy-start(bf16[128,2048]{1,0:T(8,128)(2,1)} %heads.1) | copy-start | bytes 1572868
  6.6 0.9 copy-start.16
  7.5 0.9 copy-start.18
  8.4 3.7 %copy-start.9 = (bf16[256,1280]{1,0:T(8,128)(2,1)S(1)}, bf16[256,1280]{1,0:T(8,128)(2,1)}, u32[]{:S(2)}) copy-start(bf16[256,1280]{1,0:T(8,128)(2,1)} %refs_6_.1) | copy-start | bytes 1966084
  10.0 16.8 %collective-permute-start = (bf16[192,640]{1,0:T(8,128)(2,1)S(1)}, bf16[192,640]{1,0:T(8,128)(2,1)S(1)}, u32[]{:S(2)}, u32[]{:S(2)}) collective-permute-start(bf16[192,640]{1,0:T(8,128)(2,1)S(1)} %get-tuple-element.24), channel_id=1, source_target_pairs={{0,4},{4,0},{1,5},{5,1},{2,6},{6,2},{3,7},{7,3},{8,12},{12,8},{9,1... | collective-permute-start | bytes 737288 | tf_op jit(solution)/shard_map/ppermute | solution.py:513
  12.1 2.5 %copy-start.2 = (bf16[2048,1280]{1,0:T(8,128)(2,1)S(1)}, bf16[2048,1280]{1,0:T(8,128)(2,1)}, u32[]{:S(2)}) copy-start(bf16[2048,1280]{1,0:T(8,128)(2,1)} %refs_3_.1) | copy-start | bytes 15728644
  14.6 1.5 %copy-start.12 = (bf16[256,3,1280]{2,0,1:T(8,128)(2,1)S(1)}, bf16[256,3,1280]{2,0,1:T(8,128)(2,1)}, u32[]{:S(2)}) copy-start(bf16[256,3,1280]{2,0,1:T(8,128)(2,1)} %param.22) | copy-start | bytes 5898244
  16.1 1.5 %copy-start.13 = (bf16[256,3,1280]{2,0,1:T(8,128)(2,1)S(1)}, bf16[256,3,1280]{2,0,1:T(8,128)(2,1)}, u32[]{:S(2)}) copy-start(bf16[256,3,1280]{2,0,1:T(8,128)(2,1)} %param.26) | copy-start | bytes 5898244
  17.7 10.2 %copy-start.19 = (s32[3]{0:T(128)S(1)}, s32[3]{0:T(128)}, u32[]{:S(2)}) copy-start(s32[3]{0:T(128)} %param.19) | copy-start | bytes 40
  17.7 11.3 %copy-start.17 = (bf16[64,1280]{1,0:T(8,128)(2,1)S(1)}, bf16[64,1280]{1,0:T(8,128)(2,1)}, u32[]{:S(2)}) copy-start(bf16[64,1280]{1,0:T(8,128)(2,1)} %noise.3) | copy-start | bytes 491524
  21.9 1.9 %copy-start.4 = (bf16[3,1280,512]{2,1,0:T(8,128)(2,1)}, bf16[3,1280,512]{2,1,0:T(8,128)(2,1)S(1)}, u32[]{:S(2)}) copy-start(bf16[3,1280,512]{2,1,0:T(8,128)(2,1)S(1)} %get-tuple-element.35.weight) | copy-start | bytes 11796484
  23.7 1.9 %copy-start.6 = (bf16[3,1280,512]{2,1,0:T(8,128)(2,1)}, bf16[3,1280,512]{2,1,0:T(8,128)(2,1)S(1)}, u32[]{:S(2)}) copy-start(bf16[3,1280,512]{2,1,0:T(8,128)(2,1)S(1)} %get-tuple-element.27.weight) | copy-start | bytes 11796484
  25.7 1.1 %copy-start.14 = (bf16[512,1280]{1,0:T(8,128)(2,1)}, bf16[512,1280]{1,0:T(8,128)(2,1)S(1)}, u32[]{:S(2)}) copy-start(bf16[512,1280]{1,0:T(8,128)(2,1)S(1)} %get-tuple-element.41.refs_9_) | copy-start | bytes 3932164
  26.8 2.2 %collective-permute-start.1 = (bf16[192,640]{1,0:T(8,128)(2,1)S(1)}, bf16[192,640]{1,0:T(8,128)(2,1)S(1)}, u32[]{:S(2)}, u32[]{:S(2)}) collective-permute-start(bf16[192,640]{1,0:T(8,128)(2,1)S(1)} %join_part.1.joined), channel_id=1, source_target_pairs={{0,8},{8,0},{16,24},{24,16},{1,9},{9,1},{17,25},{25,17},{2,10},{10... | collective-permute-start | bytes 737288 | tf_op jit(solution)/shard_map/ppermute | solution.py:513
  27.9 5.9 %copy-start.5 = (bf16[3,1280,512]{2,1,0:T(8,128)(2,1)S(1)}, bf16[3,1280,512]{2,1,0:T(8,128)(2,1)}, u32[]{:S(2)}) copy-start(bf16[3,1280,512]{2,1,0:T(8,128)(2,1)} %copy-done.4) | copy-start | bytes 11796484
  29.0 2.2 %copy-start.7 = (bf16[3,1280,512]{2,1,0:T(8,128)(2,1)S(1)}, bf16[3,1280,512]{2,1,0:T(8,128)(2,1)}, u32[]{:S(2)}) copy-start(bf16[3,1280,512]{2,1,0:T(8,128)(2,1)} %copy-done.6) | copy-start | bytes 11796484
  33.8 49.3 %copy-start.15 = (bf16[512,1280]{1,0:T(8,128)(2,1)S(1)}, bf16[512,1280]{1,0:T(8,128)(2,1)}, u32[]{:S(2)}) copy-start(bf16[512,1280]{1,0:T(8,128)(2,1)} %copy-done.14) | copy-start | bytes 3932164
  35.2 6.2 %collective-permute-start.11 = (bf16[2,128,384]{2,1,0:T(8,128)(2,1)S(1)}, bf16[2,128,384]{2,1,0:T(8,128)(2,1)S(1)}, u32[]{:S(2)}, u32[]{:S(2)}) collective-permute-start(bf16[2,128,384]{2,1,0:T(8,128)(2,1)S(1)} %get-tuple-element.39), channel_id=1, source_target_pairs={{0,1},{1,0},{2,3},{3,2},{4,5},{5,4},{6,7},{7,6},{8,9},{9,8},{10,11... | collective-permute-start | bytes 589832 | tf_op jit(solution)/shard_map/ppermute | solution.py:513
  37.3 16.8 %collective-permute-start.9 = (bf16[2,144,384]{2,1,0:T(8,128)(2,1)S(1)}, bf16[2,144,384]{2,1,0:T(8,128)(2,1)S(1)}, u32[]{:S(2)}, u32[]{:S(2)}) collective-permute-start(bf16[2,144,384]{2,1,0:T(8,128)(2,1)S(1)} %get-tuple-element.37), channel_id=1, source_target_pairs={{0,1},{1,0},{2,3},{3,2},{4,5},{5,4},{6,7},{7,6},{8,9},{9,8},{10,11... | collective-permute-start | bytes 663560 | tf_op jit(solution)/shard_map/ppermute | solution.py:513
  37.4 15.1 %collective-permute-start.4 = (bf16[2,128,384]{2,1,0:T(8,128)(2,1)S(1)}, bf16[2,128,384]{2,1,0:T(8,128)(2,1)S(1)}, u32[]{:S(2)}, u32[]{:S(2)}) collective-permute-start(bf16[2,128,384]{2,1,0:T(8,128)(2,1)S(1)} %get-tuple-element.32), channel_id=1, source_target_pairs={{0,1},{1,0},{2,3},{3,2},{4,5},{5,4},{6,7},{7,6},{8,9},{9,8},{10,11... | collective-permute-start | bytes 589832 | tf_op jit(solution)/shard_map/ppermute | solution.py:513
  38.7 20.0 %collective-permute-start.2 = (bf16[2,144,384]{2,1,0:T(8,128)(2,1)S(1)}, bf16[2,144,384]{2,1,0:T(8,128)(2,1)S(1)}, u32[]{:S(2)}, u32[]{:S(2)}) collective-permute-start(bf16[2,144,384]{2,1,0:T(8,128)(2,1)S(1)} %get-tuple-element.30), channel_id=1, source_target_pairs={{0,1},{1,0},{2,3},{3,2},{4,5},{5,4},{6,7},{7,6},{8,9},{9,8},{10,11... | collective-permute-start | bytes 663560 | tf_op jit(solution)/shard_map/ppermute | solution.py:513
  41.5 17.5 %collective-permute-start.12 = (bf16[128,384]{1,0:T(8,128)(2,1)S(1)}, bf16[128,384]{1,0:T(8,128)(2,1)S(1)}, u32[]{:S(2)}, u32[]{:S(2)}) collective-permute-start(bf16[128,384]{1,0:T(8,128)(2,1)S(1)} %fusion.4), channel_id=1, source_target_pairs={{0,2},{1,3},{2,0},{3,1},{4,6},{5,7},{6,4},{7,5},{8,10},{9,11},{10,... | collective-permute-start | bytes 294920 | tf_op jit(solution)/shard_map/ppermute | solution.py:513
  52.6 16.8 %collective-permute-start.5 = (bf16[128,384]{1,0:T(8,128)(2,1)S(1)}, bf16[128,384]{1,0:T(8,128)(2,1)S(1)}, u32[]{:S(2)}, u32[]{:S(2)}) collective-permute-start(bf16[128,384]{1,0:T(8,128)(2,1)S(1)} %fusion.3), channel_id=1, source_target_pairs={{0,2},{1,3},{2,0},{3,1},{4,6},{5,7},{6,4},{7,5},{8,10},{9,11},{10,... | collective-permute-start | bytes 294920 | tf_op jit(solution)/shard_map/ppermute | solution.py:513
  54.1 44.1 %copy-start.11 = (bf16[128,2048]{1,0:T(8,128)(2,1)S(1)}, bf16[128,2048]{1,0:T(8,128)(2,1)}, u32[]{:S(2)}) copy-start(bf16[128,2048]{1,0:T(8,128)(2,1)} %heads.1) | copy-start | bytes 1572868
  54.2 14.3 %collective-permute-start.10 = (bf16[144,384]{1,0:T(8,128)(2,1)S(1)}, bf16[144,384]{1,0:T(8,128)(2,1)S(1)}, u32[]{:S(2)}, u32[]{:S(2)}) collective-permute-start(bf16[144,384]{1,0:T(8,128)(2,1)S(1)} %fusion.2), channel_id=1, source_target_pairs={{0,2},{1,3},{2,0},{3,1},{4,6},{5,7},{6,4},{7,5},{8,10},{9,11},{10,... | collective-permute-start | bytes 331784 | tf_op jit(solution)/shard_map/ppermute | solution.py:513
  58.8 12.1 %collective-permute-start.3 = (bf16[144,384]{1,0:T(8,128)(2,1)S(1)}, bf16[144,384]{1,0:T(8,128)(2,1)S(1)}, u32[]{:S(2)}, u32[]{:S(2)}) collective-permute-start(bf16[144,384]{1,0:T(8,128)(2,1)S(1)} %fusion.1), channel_id=1, source_target_pairs={{0,2},{1,3},{2,0},{3,1},{4,6},{5,7},{6,4},{7,5},{8,10},{9,11},{10,... | collective-permute-start | bytes 331784 | tf_op jit(solution)/shard_map/ppermute | solution.py:513
  69.3 7.1 %collective-permute-start.14 = (bf16[2,128,128]{2,1,0:T(8,128)(2,1)S(1)}, bf16[2,128,128]{2,1,0:T(8,128)(2,1)S(1)}, u32[]{:S(2)}, u32[]{:S(2)}) collective-permute-start(bf16[2,128,128]{2,1,0:T(8,128)(2,1)S(1)} %attend_part.3.refs_4_), channel_id=1, source_target_pairs={{0,2},{1,3},{2,0},{3,1},{4,6},{5,7},{6,4},{7,5},{8,10},{9,11},{10,... | collective-permute-start | bytes 196616 | tf_op jit(solution)/shard_map/ppermute | solution.py:513
  71.7 6.2 %collective-permute-start.7 = (bf16[2,128,128]{2,1,0:T(8,128)(2,1)S(1)}, bf16[2,128,128]{2,1,0:T(8,128)(2,1)S(1)}, u32[]{:S(2)}, u32[]{:S(2)}) collective-permute-start(bf16[2,128,128]{2,1,0:T(8,128)(2,1)S(1)} %attend_part.2.refs_0_), channel_id=1, source_target_pairs={{0,2},{1,3},{2,0},{3,1},{4,6},{5,7},{6,4},{7,5},{8,10},{9,11},{10,... | collective-permute-start | bytes 196616 | tf_op jit(solution)/shard_map/ppermute | solution.py:513
  72.6 6.3 %collective-permute-start.13 = (bf16[2,128,128]{2,1,0:T(8,128)(2,1)S(1)}, bf16[2,128,128]{2,1,0:T(8,128)(2,1)S(1)}, u32[]{:S(2)}, u32[]{:S(2)}) collective-permute-start(bf16[2,128,128]{2,1,0:T(8,128)(2,1)S(1)} %attend_part.3.refs_4_), channel_id=1, source_target_pairs={{0,1},{1,0},{2,3},{3,2},{4,5},{5,4},{6,7},{7,6},{8,9},{9,8},{10,11... | collective-permute-start | bytes 196616 | tf_op jit(solution)/shard_map/ppermute | solution.py:513
  76.4 3.9 %collective-permute-start.6 = (bf16[2,128,128]{2,1,0:T(8,128)(2,1)S(1)}, bf16[2,128,128]{2,1,0:T(8,128)(2,1)S(1)}, u32[]{:S(2)}, u32[]{:S(2)}) collective-permute-start(bf16[2,128,128]{2,1,0:T(8,128)(2,1)S(1)} %attend_part.2.refs_0_), channel_id=1, source_target_pairs={{0,1},{1,0},{2,3},{3,2},{4,5},{5,4},{6,7},{7,6},{8,9},{9,8},{10,11... | collective-permute-start | bytes 196616 | tf_op jit(solution)/shard_map/ppermute | solution.py:513
  76.4 5.3 %collective-permute-start.15 = (bf16[2,128,128]{2,1,0:T(8,128)(2,1)S(1)}, bf16[2,128,128]{2,1,0:T(8,128)(2,1)S(1)}, u32[]{:S(2)}, u32[]{:S(2)}) collective-permute-start(bf16[2,128,128]{2,1,0:T(8,128)(2,1)S(1)} %collective-permute-done.14.refs_6_), channel_id=1, source_target_pairs={{0,1},{1,0},{2,3},{3,2},{4,5},{5,4},{6,7},{7,6},{8,9},{9,8},{10,11... | collective-permute-start | bytes 196616 | tf_op jit(solution)/shard_map/ppermute | solution.py:513
  77.9 5.2 %collective-permute-start.8 = (bf16[2,128,128]{2,1,0:T(8,128)(2,1)S(1)}, bf16[2,128,128]{2,1,0:T(8,128)(2,1)S(1)}, u32[]{:S(2)}, u32[]{:S(2)}) collective-permute-start(bf16[2,128,128]{2,1,0:T(8,128)(2,1)S(1)} %collective-permute-done.7.refs_2_), channel_id=1, source_target_pairs={{0,1},{1,0},{2,3},{3,2},{4,5},{5,4},{6,7},{7,6},{8,9},{9,8},{10,11... | collective-permute-start | bytes 196616 | tf_op jit(solution)/shard_map/ppermute | solution.py:513
  84.1 2.4 %collective-permute-start.16 = (bf16[128,640]{1,0:T(8,128)(2,1)S(1)}, bf16[128,640]{1,0:T(8,128)(2,1)S(1)}, u32[]{:S(2)}, u32[]{:S(2)}) collective-permute-start(bf16[128,640]{1,0:T(8,128)(2,1)S(1)} %get-tuple-element.43), channel_id=1, source_target_pairs={{0,8},{8,0},{16,24},{24,16},{1,9},{9,1},{17,25},{25,17},{2,10},{10... | collective-permute-start | bytes 491528 | tf_op jit(solution)/shard_map/ppermute | solution.py:513
  86.6 3.7 %collective-permute-start.17 = (bf16[64,640]{1,0:T(8,128)(2,1)S(1)}, bf16[64,640]{1,0:T(8,128)(2,1)S(1)}, u32[]{:S(2)}, u32[]{:S(2)}) collective-permute-start(bf16[64,640]{1,0:T(8,128)(2,1)S(1)} %get-tuple-element.46), channel_id=1, source_target_pairs={{0,4},{4,0},{1,5},{5,1},{2,6},{6,2},{3,7},{7,3},{8,12},{12,8},{9,1... | collective-permute-start | bytes 245768 | tf_op jit(solution)/shard_map/ppermute | solution.py:513
  86.9 3.6 %collective-permute-start.19 = (bf16[64,640]{1,0:T(8,128)(2,1)S(1)}, bf16[64,640]{1,0:T(8,128)(2,1)S(1)}, u32[]{:S(2)}, u32[]{:S(2)}) collective-permute-start(bf16[64,640]{1,0:T(8,128)(2,1)S(1)} %get-tuple-element.47), channel_id=1, source_target_pairs={{0,16},{8,24},{16,0},{24,8},{1,17},{9,25},{17,1},{25,9},{2,18},{10... | collective-permute-start | bytes 245768 | tf_op jit(solution)/shard_map/ppermute | solution.py:513
  90.5 3.4 %collective-permute-start.18 = (bf16[64,640]{1,0:T(8,128)(2,1)S(1)}, bf16[64,640]{1,0:T(8,128)(2,1)S(1)}, u32[]{:S(2)}, u32[]{:S(2)}) collective-permute-start(bf16[64,640]{1,0:T(8,128)(2,1)S(1)} %get-tuple-element.44), channel_id=1, source_target_pairs={{0,16},{8,24},{16,0},{24,8},{1,17},{9,25},{17,1},{25,9},{2,18},{10... | collective-permute-start | bytes 245768 | tf_op jit(solution)/shard_map/ppermute | solution.py:513
  91.8 3.7 %collective-permute-start.20 = (bf16[64,640]{1,0:T(8,128)(2,1)S(1)}, bf16[64,640]{1,0:T(8,128)(2,1)S(1)}, u32[]{:S(2)}, u32[]{:S(2)}) collective-permute-start(bf16[64,640]{1,0:T(8,128)(2,1)S(1)} %get-tuple-element.45), channel_id=1, source_target_pairs={{0,4},{4,0},{1,5},{5,1},{2,6},{6,2},{3,7},{7,3},{8,12},{12,8},{9,1... | collective-permute-start | bytes 245768 | tf_op jit(solution)/shard_map/ppermute | solution.py:513
  95.5 5.1 %collective-permute-start.21 = (bf16[128,640]{1,0:T(8,128)(2,1)S(1)}, bf16[128,640]{1,0:T(8,128)(2,1)S(1)}, u32[]{:S(2)}, u32[]{:S(2)}) collective-permute-start(bf16[128,640]{1,0:T(8,128)(2,1)S(1)} %fusion.rows), channel_id=1, source_target_pairs={{0,8},{8,0},{16,24},{24,16},{1,9},{9,1},{17,25},{25,17},{2,10},{10... | collective-permute-start | bytes 491528 | tf_op jit(solution)/shard_map/ppermute | solution.py:513

commit v3 on v2

--- a/solution.py
+++ b/solution.py
@@ -212,64 +212,33 @@
             pltpu.VMEM((own, width), jnp.bfloat16),
             pltpu.SemaphoreType.DMA((GEN_CUTS + 4,)),
         ],
-        compiler_params=params(16),
+        compiler_params=params(56),
         name="gen_part",
     )(seq, core, embed, heads, weight, time_w, resid, noise)
 
 
-def load_kernel(role, embed, after, *refs):
-    qkv_a, qkv_b, out_a, out_b, time_a, time_b, time_w = refs[:7]
-    own_qkv_a, own_qkv_b, own_out_a, own_out_b, mods, gate = refs[7:13]
-    time_v, gate_v, sems = refs[13:]
-    cols = at_block(role[0], own_qkv_a.shape[2])
-    rows = at_block(role[0], own_out_a.shape[0])
-    pairs = (
-        (time_a, time_v.at[0]),
-        (time_b, time_v.at[1]),
-        (time_w, gate_v),
-        (qkv_a.at[:, :, cols], own_qkv_a),
-        (qkv_b.at[:, :, cols], own_qkv_b),
-        (out_a.at[rows, :], own_out_a),
-        (out_b.at[rows, :], own_out_b),
-    )
-    copies = [pltpu.make_async_copy(source, goal, sems.at[k]) for k, (source, goal) in enumerate(pairs)]
-    for copy in copies:
-        copy.start()
-    for index in range(2):
-        copies[index].wait()
-        for k in range(3):
-            mods[index, k] = dot32(embed[...], time_v[index, k])
-    copies[2].wait()
-    gate[...] = dot32(embed[...], gate_v[...])
-    for copy in copies[3:]:
-        copy.wait()
-
-
-def load_part(role, embed, after, qkv_a, qkv_b, out_a, out_b, time_a, time_b, time_w, roles):
-    parts, depth, heads_cols = qkv_a.shape
-    part_cols = heads_cols // roles
-    width = time_w.shape[1]
-    freq = time_w.shape[0]
-    moved = 4 * (parts * depth * part_cols + part_cols * width + parts * freq * width)
-    return pl.pallas_call(
-        load_kernel,
-        in_specs=[smem_spec(), vmem_spec(), any_spec()] + [hbm_spec()] * 7,
-        out_specs=[vmem_spec()] * 6,
-        out_shape=[jax.ShapeDtypeStruct((parts, depth, part_cols), jnp.bfloat16)] * 2
-        + [jax.ShapeDtypeStruct((part_cols, width), jnp.bfloat16)] * 2
-        + [
-            jax.ShapeDtypeStruct((2, parts, 8, width), jnp.float32),
+def mod_kernel(embed, time_a, time_b, time_w, after, mods, gate):
+    gate[...] = dot32(embed[...], time_w[...])
+    for k in range(3):
+        mods[0, k] = dot32(embed[...], time_a[k])
+        mods[1, k] = dot32(embed[...], time_b[k])
+
+
+def mod_part(embed, time_a, time_b, time_w, after):
+    width = time_a.shape[2]
+    moved = 2 * (time_a.size + time_b.size + time_w.size)
+    return pl.pallas_call(
+        mod_kernel,
+        in_specs=[vmem_spec()] * 4 + [any_spec()],
+        out_specs=[vmem_spec()] * 2,
+        out_shape=[
+            jax.ShapeDtypeStruct((2, 3, 8, width), jnp.float32),
             jax.ShapeDtypeStruct((8, width), jnp.float32),
         ],
-        scratch_shapes=[
-            pltpu.VMEM((2, parts, freq, width), jnp.bfloat16),
-            pltpu.VMEM((freq, width), jnp.bfloat16),
-            pltpu.SemaphoreType.DMA((7,)),
-        ],
-        compiler_params=params(24),
-        cost_estimate=cost(moved, moved),
-        name="load_part",
-    )(role, embed, after, qkv_a, qkv_b, out_a, out_b, time_a, time_b, time_w)
+        compiler_params=params(16),
+        cost_estimate=cost(8 * moved, moved),
+        name="mod_part",
+    )(embed, time_a, time_b, time_w, after)
 
 
 def join_kernel(full, arrived, after, joined):
@@ -291,7 +260,7 @@
     )(full, arrived, after)
 
 
-def project(index, mine, noisy, squares, mods, weight, kept, sent, result):
+def project(index, mine, noisy, squares, mods, weight, copies, kept, sent, result):
     tokens = noisy.shape[0]
     length = tokens // 2
     unit = squares.shape[1] // 2
@@ -305,6 +274,7 @@
     rows = jnp.concatenate([top, low, extra], axis=0).astype(jnp.bfloat16)
     row_id = lax.broadcasted_iota(jnp.int32, (EXTRA_ROWS, unit), 0)
     for part in range(3):
+        copies[part].wait()
         result[...] = dot32(rows, weight[part])
         cols = pl.ds(part * unit, unit)
         for slot in range(groups):
@@ -320,8 +290,23 @@
             goal[0][slot // 2, pl.ds(length, EXTRA_ROWS), cols] = tail.astype(jnp.bfloat16)
 
 
-def first_kernel(seq, core, mine, levels, joined, swapped, noise, mods, weight, *refs):
-    latent, noisy, squares, kept_a, kept_b, sent_a, sent_b, values, noises, result = refs
+def weight_copies(role, planes, weight, sems):
+    cols = at_block(role[0], weight.shape[3])
+    copies = [
+        [
+            pltpu.make_async_copy(planes[index].at[part, :, cols], weight.at[index, part], sems.at[3 * index + part])
+            for part in range(3)
+        ]
+        for index in range(2)
+    ]
+    for copy in copies[0] + copies[1]:
+        copy.start()
+    return copies
+
+
+def qkv_kernel(role, seq, core, mine, levels, joined, swapped, noise, mods, planes_a, planes_b, latent, *refs):
+    chunks, (values, noises, result, weight, sems) = refs[:8], refs[8:]
+    copies = weight_copies(role, (planes_a, planes_b), weight, sems)
     length, cols = values.shape[0], joined.shape[1]
     own = latent.shape[0]
     tokens = 2 * length
@@ -338,65 +323,65 @@
     mixed = jnp.concatenate(
         [(1.0 - levels[level]) * spread + levels[level] * noise_rows for level in range(2)], axis=0
     ).astype(jnp.bfloat16)
-    noisy[...] = mixed
     wide = mixed.astype(jnp.float32)
     sums = jnp.sum(wide * wide, axis=1, keepdims=True)
     sums = jnp.broadcast_to(sums, (tokens, length)).T[0:8]
-    squares[...] = sums
-    project(0, mine[0], mixed, sums, mods, weight, (kept_a, kept_b), (sent_a, sent_b), result)
-
-
-def second_kernel(mine, noisy, squares, mods, weight, kept_a, kept_b, sent_a, sent_b, result):
-    project(1, mine[0], noisy[...], squares[...], mods, weight, (kept_a, kept_b), (sent_a, sent_b), result)
-
-
-def chunk_shapes(length, weight):
-    unit = length
-    groups = weight.shape[2] // unit
+    for index in range(2):
+        kept, sent = chunks[4 * index : 4 * index + 2], chunks[4 * index + 2 : 4 * index + 4]
+        project(index, mine[0], mixed, sums, mods, weight.at[index], copies[index], kept, sent, result)
+
+
+def chunk_shapes(length, cols):
+    groups = cols // length
     shapes = [
-        jax.ShapeDtypeStruct((groups // 2, rows, 3 * unit), jnp.bfloat16) for rows in (length + EXTRA_ROWS, length)
+        jax.ShapeDtypeStruct((groups // 2, rows, 3 * length), jnp.bfloat16) for rows in (length + EXTRA_ROWS, length)
     ]
     return shapes * 2
 
 
-def first_part(seq, core, mine, levels, joined, swapped, noise, mods, weight):
+def qkv_part(role, seq, core, mine, levels, joined, swapped, noise, mods, planes_a, planes_b, cols):
     own, width = noise.shape
     length = joined.shape[0] - own
     tokens = 2 * length
     return pl.pallas_call(
-        first_kernel,
-        in_specs=[smem_spec()] * 4 + [vmem_spec()] * 5,
-        out_specs=[vmem_spec()] * 7,
-        out_shape=[
-            jax.ShapeDtypeStruct((own, width), jnp.bfloat16),
-            jax.ShapeDtypeStruct((tokens, width), jnp.bfloat16),
-            jax.ShapeDtypeStruct((8, tokens), jnp.float32),
-        ]
-        + chunk_shapes(length, weight),
+        qkv_kernel,
+        in_specs=[smem_spec()] * 5 + [vmem_spec()] * 4 + [hbm_spec()] * 2,
+        out_specs=[vmem_spec()] * 9,
+        out_shape=[jax.ShapeDtypeStruct((own, width), jnp.bfloat16)] + chunk_shapes(length, cols) * 2,
         scratch_shapes=[
             pltpu.VMEM((length, width), jnp.bfloat16),
             pltpu.VMEM((length, width), jnp.bfloat16),
-            pltpu.VMEM((tokens + EXTRA_ROWS, weight.shape[2]), jnp.float32),
+            pltpu.VMEM((tokens + EXTRA_ROWS, cols), jnp.float32),
+            pltpu.VMEM((2, 3, width, cols), jnp.bfloat16),
+            pltpu.SemaphoreType.DMA((6,)),
         ],
-        compiler_params=params(24),
-        name="first_part",
-    )(seq, core, mine, levels, joined, swapped, noise, mods, weight)
-
-
-def second_part(mine, noisy, squares, mods, weight):
-    tokens = noisy.shape[0]
-    return pl.pallas_call(
-        second_kernel,
-        in_specs=[smem_spec()] + [vmem_spec()] * 4,
-        out_specs=[vmem_spec()] * 4,
-        out_shape=chunk_shapes(tokens // 2, weight),
-        scratch_shapes=[pltpu.VMEM((tokens + EXTRA_ROWS, weight.shape[2]), jnp.float32)],
-        compiler_params=params(24),
-        name="second_part",
-    )(mine, noisy, squares, mods, weight)
-
-
-def attend_kernel(width, kept_a, other_a, kept_b, other_b, gains, out):
+        compiler_params=params(48),
+        name="qkv_part",
+    )(role, seq, core, mine, levels, joined, swapped, noise, mods, planes_a, planes_b)
+
+
+def add_kernel(mine, theirs, *refs):
+    kept, sent = refs[-3:-1] if len(refs) > 2 else refs
+    kept[...] = mine[0].astype(jnp.float32) + theirs[0].astype(jnp.float32)
+    sent[...] = (mine[1].astype(jnp.float32) + theirs[1].astype(jnp.float32)).astype(jnp.bfloat16)
+
+
+def add_part(mine, theirs, later=None):
+    rest = [] if later is None else [later]
+    shape = mine.shape[1:]
+    return pl.pallas_call(
+        add_kernel,
+        in_specs=[vmem_spec()] * 2 + [any_spec()] * len(rest),
+        out_specs=[vmem_spec()] * 2 + [any_spec()] * len(rest),
+        out_shape=[jax.ShapeDtypeStruct(shape, jnp.float32), jax.ShapeDtypeStruct(shape, jnp.bfloat16)]
+        + [jax.ShapeDtypeStruct(x.shape, x.dtype) for x in rest],
+        input_output_aliases={2: 2} if rest else {},
+        compiler_params=params(8),
+        name="add_part",
+    )(mine, theirs, *rest)
+
+
+def attend_kernel(width, kept_a, other_a, kept_b, other_b, gains, after, out):
     _, length, unit = out.shape
     extra = None
     for level, (kept, other) in enumerate(((kept_a, other_a), (kept_b, other_b))):
@@ -425,18 +410,18 @@
         out[level] = dot32(probs, value).astype(jnp.bfloat16)
 
 
-def attend_part(chunks, gains, width):
+def attend_part(chunks, gains, after, width):
     kept_a, kept_b = chunks[0][0], chunks[1][0]
     unit = kept_a.shape[1] // 3
     length = kept_a.shape[0] - EXTRA_ROWS
     return pl.pallas_call(
         lambda *refs: attend_kernel(width, *refs),
-        in_specs=[vmem_spec()] * 5,
+        in_specs=[vmem_spec()] * 5 + [any_spec()],
         out_specs=vmem_spec(),
         out_shape=jax.ShapeDtypeStruct((2, length, unit), jnp.bfloat16),
         compiler_params=params(8),
         name="attend_part",
-    )(kept_a, chunks[0][1], kept_b, chunks[1][1], gains)
+    )(kept_a, chunks[0][1], kept_b, chunks[1][1], gains, after)
 
 
 def out_kernel(core, mine, *refs):
@@ -548,40 +533,38 @@
     full, sent = gen_part(seq_at, core, embed, gen_heads, gen_out_w, gen_time_w, gen_resid, noise)
     arrived = exchange(sent, "seq", 1)
     planes = [w.transpose(1, 0, 2) for w in (teacher_qkv, critic_qkv, teacher_time, critic_time)]
-    weight_a, weight_b, out_a, out_b, mods, gate = load_part(
-        role_at, embed, full, planes[0], planes[1], teacher_out, critic_out, planes[2], planes[3], gen_time_w, roles
-    )
+    mods, gate = mod_part(embed, planes[2], planes[3], gen_time_w, full)
     joined = join_part(full, arrived, gate)
     swapped = exchange(joined, "role", 1)
-    first = first_part(seq_at, core, mine, levels, joined, swapped, noise, mods, weight_a)
-    latent, noisy, squares = first[:3]
-    second = second_part(mine, noisy, squares, mods, weight_b)
-
     start = role * part_cols
+    out_a, out_b = [lax.dynamic_slice_in_dim(w, start, part_cols, axis=0) for w in (teacher_out, critic_out)]
     unit = part_cols // groups
-    gathered = []
-    for chunks, gains in ((first[3:], teacher_norm), (second, critic_norm)):
-        kept, sends = chunks[:2], chunks[2:]
-        pieces = []
-        for level in range(2):
-            summed = both(kept[level], exchange(sends[level], "mp", 1))
-            pieces.append((summed[0], exchange(summed[1].astype(jnp.bfloat16), "mp", 2)))
-        gains = lax.dynamic_slice_in_dim(gains, start + mp * unit, unit, axis=1)
-        head_out = attend_part(pieces, gains, D)
-        near = exchange(head_out, "mp", 1)
-        far = exchange(head_out, "mp", 2)
-        gathered.append((head_out, near, far, exchange(far, "mp", 1)))
+    gains = [lax.dynamic_slice_in_dim(g, start + mp * unit, unit, axis=1) for g in (teacher_norm, critic_norm)]
+
+    latent, *chunks = qkv_part(
+        role_at, seq_at, core, mine, levels, joined, swapped, noise, mods, planes[0], planes[1], part_cols
+    )
+    first, second = chunks[:4], chunks[4:]
+    kept_a, send_a, third = add_part(first[0], exchange(first[2], "mp", 1), second[2])
+    kept_b, send_b, last = add_part(first[1], exchange(first[3], "mp", 1), second[3])
+    kept_c, send_c = add_part(second[0], exchange(third, "mp", 1))
+    kept_d, send_d = add_part(second[1], exchange(last, "mp", 1))
+    sums = [(kept, exchange(send, "mp", 2)) for kept, send in ((kept_a, send_a), (kept_b, send_b))]
+    head_a = attend_part(sums, gains[0], out_a, D)
+    sums = [(kept, exchange(send, "mp", 2)) for kept, send in ((kept_c, send_c), (kept_d, send_d))]
+    head_b = attend_part(sums, gains[1], out_b, D)
+    gathered = [[head] + [exchange(head, "mp", bits) for bits in range(1, groups)] for head in (head_a, head_b)]
 
     kept, sent = out_part(core, mine, *gathered, out_a, out_b, mods)
     total = both(kept, exchange(sent, "role", 1)).astype(jnp.bfloat16)
-    middle = length // 2
-    top, low = total[:middle], total[middle:]
-    top = both(top, exchange(top, "seq", 1)).astype(jnp.bfloat16)
-    low = both(low, exchange(low, "role", 2)).astype(jnp.bfloat16)
-    top = both(top, exchange(top, "role", 2))
-    low = both(low, exchange(low, "seq", 1))
+    along_x = exchange(total, "seq", 1)
+    along_y = exchange(total, "role", 2)
+    across = lax.ppermute(
+        total, ("role", "seq"), [(i, i ^ (2 * lax.axis_size("seq") + 1)) for i in range(roles * lax.axis_size("seq"))]
+    )
+    total = both(total, along_x) + both(along_y, across)
     gate_row = lax.dynamic_slice_in_dim(gate, core[0] * half_cols, half_cols, axis=1)[0:1]
-    rows = (gate_row * jnp.concatenate([top, low], axis=0)).astype(jnp.bfloat16)
+    rows = (gate_row * total).astype(jnp.bfloat16)
     heads_t = gen_heads.T
     theirs = exchange(rows, "role", 1)
     weight_grad = grad_part(core, heads_t, rows, None, 2)

time: 103 us -> 95.6 us (0.928)
  local copies, waits for them, and re-layouts: 20.7 us -> 8.63 us
  Pallas kernels: 16.5 us -> 19.1 us
  starting transfers between devices: 25.8 us -> 27 us
    unnamed x41 -> x33, local copies, waits for them, and re-layouts: 19.9 us -> 4.4 us
    ppermute x0 -> x1, waiting for transfers between devices: none -> 2.92 us  [heads_per_role(): lax.ppermute(total, ('role', 'seq'), [(i, i ^ 2 * lax.axis_size('seq') +...]
    dynamic_slice x2 -> x4, local copies, waits for them, and re-layouts: 0.68 us -> 3.48 us  [the longest x2 2.8 us: heads_per_role(): lax.dynamic_slice_in_dim(w, start, part_cols, axis=0)]
    pallas_call x1, Pallas kernels: 1.57 us -> 4.16 us  [gen_part(): pl.pallas_call(gen_kernel, in_specs=[smem_spec(), smem_spec(), vmem_spec(...]
    ppermute x22 -> x20, waiting for transfers between devices: 37.5 us -> 35 us  [exchange(): lax.ppermute(array, axis, [(i, i ^ bit) for i in range(lax.axis_size(axis...]
    ppermute x0 -> x1, starting transfers between devices: none -> 2.24 us  [heads_per_role(): lax.ppermute(total, ('role', 'seq'), [(i, i ^ 2 * lax.axis_size('seq') +...]
    ppermute x22 -> x20, starting transfers between devices: 25.8 us -> 24.8 us  [exchange(): lax.ppermute(array, axis, [(i, i ^ bit) for i in range(lax.axis_size(axis...]
    pallas_call x3 -> x6, Pallas kernels: 8.25 us -> 8.27 us  [the longest x1 6.42 us: qkv_part(): pl.pallas_call(qkv_kernel, in_specs=[smem_spec()] * 5 + [vmem_spec()] * 4...]
  transfers between devices with their start and end apart: 22 -> 21, of which waited for: 15 -> 13; matrix products, arithmetic and copies ran while one was open for 1% -> 5% of each run, Pallas kernels for 8% -> 6%
where the time goes in v3:
time: 95.6 us; the launch traced here: 95.3 us
  waiting for transfers between devices  37.9 us (40%)
  starting transfers between devices  27 us (28%)
  Pallas kernels  19.1 us (20%)
  local copies, waits for them, and re-layouts  8.63 us (9%)
  other arithmetic  1.74 us (2%)
    ppermute x20, waiting for transfers between devices, exchange(): lax.ppermute(array, axis, [(i, i ^ bit) for i in range(lax.axis_size(axis...  35 us
    ppermute x20, starting transfers between devices, exchange(): lax.ppermute(array, axis, [(i, i ^ bit) for i in range(lax.axis_size(axis...  24.8 us
    pallas_call x1, Pallas kernels, qkv_part(): pl.pallas_call(qkv_kernel, in_specs=[smem_spec()] * 5 + [vmem_spec()] * 4...  6.42 us
    unnamed x33, local copies, waits for them, and re-layouts  4.4 us
    pallas_call x1, Pallas kernels, gen_part(): pl.pallas_call(gen_kernel, in_specs=[smem_spec(), smem_spec(), vmem_spec(...  4.16 us
    pallas_call x2, Pallas kernels, grad_part(): pl.pallas_call(grad_kernel, grid_spec=grid_spec, out_shape=jax.ShapeDtype...  4.1 us
    ppermute x1, waiting for transfers between devices, heads_per_role(): lax.ppermute(total, ('role', 'seq'), [(i, i ^ 2 * lax.axis_size('seq') +...  2.92 us
    dynamic_slice x2, local copies, waits for them, and re-layouts, heads_per_role(): lax.dynamic_slice_in_dim(w, start, part_cols, axis=0)  2.8 us
  transfers between devices with their start and end apart: 21, of which 13 were waited for; matrix products, arithmetic and copies ran while one was open for 5% of the time, Pallas kernels for 6%

profile of v3, /device:TPU:1, one launch (start us, length us, event | category | flops | bytes accessed | tf_op | source)
XLA Modules:
  0.0 95.3 jit_solution(11449677428455033740)
XLA Ops:
  0.6 0.0 copy-start
  0.6 0.0 copy-start.1
  0.7 0.0 copy-start.3
  0.7 0.8 convert_element_type.29
  1.5 0.1 fusion.3
  1.6 0.6 fusion.2.embed
  2.2 4.2 %gen_part.1 = (f32[128,640]{1,0:T(8,128)}, bf16[192,640]{1,0:T(8,128)(2,1)}) custom-call(s32[1]{0:T(128)} %bitcast.1.seq, s32[1]{0:T(128)S(6)} %select_n.18.core.half, bf16[8,256]{1,0:T(8,128)(2,1)} %fusion.2.embed, bf16[128,2048]{1,0:T(8,128)(2,1)} %heads.1, bf16[2048,1280]{1,0:T(8,128)(2,1)} %weight.1, bf16[256,1280]{1,0:T(8,128)(2,1)} %time_w.3, ...), custom_call_target="tpu_custom_call" | custom-call | tf_op jit(solution)/shard_map/gen_part/pallas_call | solution.py:200
  6.4 2.1 %collective-permute-start = (bf16[192,640]{1,0:T(8,128)(2,1)}, bf16[192,640]{1,0:T(8,128)(2,1)S(1)}, u32[]{:S(2)}, u32[]{:S(2)}) collective-permute-start(bf16[192,640]{1,0:T(8,128)(2,1)} %get-tuple-element.28), channel_id=1, source_target_pairs={{0,4},{4,0},{1,5},{5,1},{2,6},{6,2},{3,7},{7,3},{8,12},{12,8},{9,1... | collective-permute-start | bytes 737288 | tf_op jit(solution)/shard_map/ppermute | solution.py:498
  8.5 0.0 copy-start.4
  8.5 1.0 %copy-done.4 = f32[128,640]{1,0:T(8,128)S(1)} copy-done((f32[128,640]{1,0:T(8,128)S(1)}, f32[128,640]{1,0:T(8,128)}, u32[]{:S(2)}) %copy-start.4) | copy-done | bytes 327704
  9.5 0.7 mod_part.1
  10.2 4.2 %collective-permute-done.arrived = bf16[192,640]{1,0:T(8,128)(2,1)S(1)} collective-permute-done((bf16[192,640]{1,0:T(8,128)(2,1)}, bf16[192,640]{1,0:T(8,128)(2,1)S(1)}, u32[]{:S(2)}, u32[]{:S(2)}) %collective-permute-start) | collective-permute-done | bytes 245792 | tf_op jit(solution)/shard_map/ppermute | solution.py:498
  14.5 1.3 %collective-permute-start.1 = (bf16[192,640]{1,0:T(8,128)(2,1)S(1)}, bf16[192,640]{1,0:T(8,128)(2,1)S(1)}, u32[]{:S(2)}, u32[]{:S(2)}) collective-permute-start(bf16[192,640]{1,0:T(8,128)(2,1)S(1)} %join_part.1.joined), channel_id=1, source_target_pairs={{0,8},{8,0},{16,24},{24,16},{1,9},{9,1},{17,25},{25,17},{2,10},{10... | collective-permute-start | bytes 737288 | tf_op jit(solution)/shard_map/ppermute | solution.py:498
  15.8 0.1 convert_multiply_fusion.levels
  15.8 1.1 %collective-permute-done.1.swapped = bf16[192,640]{1,0:T(8,128)(2,1)S(1)} collective-permute-done((bf16[192,640]{1,0:T(8,128)(2,1)S(1)}, bf16[192,640]{1,0:T(8,128)(2,1)S(1)}, u32[]{:S(2)}, u32[]{:S(2)}) %collective-permute-start.1) | collective-permute-done | bytes 245792 | tf_op jit(solution)/shard_map/ppermute | solution.py:498
  16.9 6.4 %qkv_part.1 = (bf16[64,1280]{1,0:T(8,128)(2,1)}, bf16[2,144,384]{2,1,0:T(8,128)(2,1)S(1)}, bf16[2,128,384]{2,1,0:T(8,128)(2,1)S(1)}, bf16[2,144,384]{2,1,0:T(8,1...) custom-call(s32[1]{0:T(128)} %bitcast.role, ...), custom_call_target="tpu_custom_call" | custom-call | tf_op jit(solution)/shard_map/qkv_part/pallas_call | solution.py:346
  23.3 1.6 %collective-permute-start.4 = (bf16[2,128,384]{2,1,0:T(8,128)(2,1)S(1)}, bf16[2,128,384]{2,1,0:T(8,128)(2,1)S(1)}, u32[]{:S(2)}, u32[]{:S(2)}) collective-permute-start(bf16[2,128,384]{2,1,0:T(8,128)(2,1)S(1)} %get-tuple-element.38), channel_id=1, source_target_pairs={{0,1},{1,0},{2,3},{3,2},{4,5},{5,4},{6,7},{7,6},{8,9},{9,8},{10,11... | collective-permute-start | bytes 589832 | tf_op jit(solution)/shard_map/ppermute | solution.py:498
  24.9 0.1 collective-permute-start.2
  25.0 1.4 %constant_dynamic-slice_fusion.2.refs_5_.refs_8_ = bf16[512,1280]{1,0:T(8,128)(2,1)S(1)} fusion(bf16[2048,1280]{1,0:T(8,128)(2,1)} %param.21, s32[]{:T(128)S(6)} %select_n.21), kind=kLoop, calls=%fused_computation.13 | loop fusion | bytes 2621444 | tf_op jit(solution)/shard_map/dynamic_slice | solution.py:540
  26.4 3.3 %collective-permute-done.4.theirs = bf16[2,128,384]{2,1,0:T(8,128)(2,1)S(1)} collective-permute-done((bf16[2,128,384]{2,1,0:T(8,128)(2,1)S(1)}, bf16[2,128,384]{2,1,0:T(8,128)(2,1)S(1)}, u32[]{:S(2)}, u32[]{:S(2)}) %collective-permute-start.4) | collective-permute-done | bytes 196640 | tf_op jit(solution)/shard_map/ppermute | solution.py:498
  29.7 0.1 add_part.5
  29.8 0.6 copy-done.13
  30.4 1.4 %collective-permute-start.11 = (bf16[2,128,384]{2,1,0:T(8,128)(2,1)}, bf16[2,128,384]{2,1,0:T(8,128)(2,1)}, u32[]{:S(2)}, u32[]{:S(2)}) collective-permute-start(bf16[2,128,384]{2,1,0:T(8,128)(2,1)} %get-tuple-element.47), channel_id=1, source_target_pairs={{0,1},{1,0},{2,3},{3,2},{4,5},{5,4},{6,7},{7,6},{8,9},{9,8},{10,11... | collective-permute-start | bytes 589832 | tf_op jit(solution)/shard_map/ppermute | solution.py:498
  31.8 2.7 %collective-permute-done.2.theirs = bf16[2,144,384]{2,1,0:T(8,128)(2,1)S(1)} collective-permute-done((bf16[2,144,384]{2,1,0:T(8,128)(2,1)S(1)}, bf16[2,144,384]{2,1,0:T(8,128)(2,1)S(1)}, u32[]{:S(2)}, u32[]{:S(2)}) %collective-permute-start.2) | collective-permute-done | bytes 221216 | tf_op jit(solution)/shard_map/ppermute | solution.py:498
  34.4 0.1 add_part.4
  34.5 0.6 copy-done.12
  35.1 1.4 %collective-permute-start.9 = (bf16[2,144,384]{2,1,0:T(8,128)(2,1)}, bf16[2,144,384]{2,1,0:T(8,128)(2,1)S(1)}, u32[]{:S(2)}, u32[]{:S(2)}) collective-permute-start(bf16[2,144,384]{2,1,0:T(8,128)(2,1)} %get-tuple-element.43), channel_id=1, source_target_pairs={{0,1},{1,0},{2,3},{3,2},{4,5},{5,4},{6,7},{7,6},{8,9},{9,8},{10,11... | collective-permute-start | bytes 663560 | tf_op jit(solution)/shard_map/ppermute | solution.py:498
  36.5 1.4 %constant_dynamic-slice_fusion.refs_5_.refs_9_ = bf16[512,1280]{1,0:T(8,128)(2,1)S(1)} fusion(bf16[2048,1280]{1,0:T(8,128)(2,1)} %param.25, s32[]{:T(128)S(6)} %select_n.21), kind=kLoop, calls=%fused_computation.11 | loop fusion | bytes 2621444 | tf_op jit(solution)/shard_map/dynamic_slice | solution.py:540
  37.9 2.4 %collective-permute-start.5 = (bf16[128,384]{1,0:T(8,128)(2,1)}, bf16[128,384]{1,0:T(8,128)(2,1)S(1)}, u32[]{:S(2)}, u32[]{:S(2)}) collective-permute-start(bf16[128,384]{1,0:T(8,128)(2,1)} %copy-done.13), channel_id=1, source_target_pairs={{0,2},{1,3},{2,0},{3,1},{4,6},{5,7},{6,4},{7,5},{8,10},{9,11},{10,... | collective-permute-start | bytes 294920 | tf_op jit(solution)/shard_map/ppermute | solution.py:498
  40.3 0.1 collective-permute-start.3
  40.4 4.1 %collective-permute-done.5.refs_3_ = bf16[128,384]{1,0:T(8,128)(2,1)S(1)} collective-permute-done((bf16[128,384]{1,0:T(8,128)(2,1)}, bf16[128,384]{1,0:T(8,128)(2,1)S(1)}, u32[]{:S(2)}, u32[]{:S(2)}) %collective-permute-start.5) | collective-permute-done | bytes 98336 | tf_op jit(solution)/shard_map/ppermute | solution.py:498
  44.4 2.7 %collective-permute-done.3.refs_1_ = bf16[144,384]{1,0:T(8,128)(2,1)S(1)} collective-permute-done((bf16[144,384]{1,0:T(8,128)(2,1)}, bf16[144,384]{1,0:T(8,128)(2,1)S(1)}, u32[]{:S(2)}, u32[]{:S(2)}) %collective-permute-start.3) | collective-permute-done | bytes 110624 | tf_op jit(solution)/shard_map/ppermute | solution.py:498
  47.2 0.9 copy-done.7
  48.1 0.8 attend_part.2.refs_0_
  48.9 2.0 %collective-permute-start.8 = (bf16[2,128,128]{2,1,0:T(8,128)(2,1)S(1)}, bf16[2,128,128]{2,1,0:T(8,128)(2,1)S(1)}, u32[]{:S(2)}, u32[]{:S(2)}) collective-permute-start(bf16[2,128,128]{2,1,0:T(8,128)(2,1)S(1)} %attend_part.2.refs_0_), channel_id=1, source_target_pairs={{0,3},{1,2},{2,1},{3,0},{4,7},{5,6},{6,5},{7,4},{8,11},{9,10},{10,... | collective-permute-start | bytes 196616 | tf_op jit(solution)/shard_map/ppermute | solution.py:498
  50.8 0.9 copy-done.9
  51.8 1.0 %add_part.7 = (f32[128,384]{1,0:T(8,128)S(1)}, bf16[128,384]{1,0:T(8,128)(2,1)S(1)}) custom-call(bf16[2,128,384]{2,1,0:T(8,128)(2,1)S(1)} %copy-done.9, bf16[2,128,384]{2,1,0:T(8,128)(2,1)} %collective-permute-done.11.theirs), custom_call_target="tpu_custom_call" | custom-call | tf_op jit(solution)/shard_map/add_part/pallas_call | solution.py:372
  52.7 2.2 %collective-permute-start.12 = (bf16[128,384]{1,0:T(8,128)(2,1)S(1)}, bf16[128,384]{1,0:T(8,128)(2,1)S(1)}, u32[]{:S(2)}, u32[]{:S(2)}) collective-permute-start(bf16[128,384]{1,0:T(8,128)(2,1)S(1)} %get-tuple-element.49), channel_id=1, source_target_pairs={{0,2},{1,3},{2,0},{3,1},{4,6},{5,7},{6,4},{7,5},{8,10},{9,11},{10,... | collective-permute-start | bytes 294920 | tf_op jit(solution)/shard_map/ppermute | solution.py:498
  54.9 0.1 add_part.6
  55.0 0.0 copy-start.14
  55.0 0.3 collective-permute-start.10
  55.3 0.7 constant_dynamic-slice_fusion.1.refs_4_
  56.0 2.1 %collective-permute-start.7 = (bf16[2,128,128]{2,1,0:T(8,128)(2,1)S(1)}, bf16[2,128,128]{2,1,0:T(8,128)(2,1)S(1)}, u32[]{:S(2)}, u32[]{:S(2)}) collective-permute-start(bf16[2,128,128]{2,1,0:T(8,128)(2,1)S(1)} %attend_part.2.refs_0_), channel_id=1, source_target_pairs={{0,2},{1,3},{2,0},{3,1},{4,6},{5,7},{6,4},{7,5},{8,10},{9,11},{10,... | collective-permute-start | bytes 196616 | tf_op jit(solution)/shard_map/ppermute | solution.py:498
  58.1 4.2 %collective-permute-done.12.refs_3_ = bf16[128,384]{1,0:T(8,128)(2,1)S(1)} collective-permute-done((bf16[128,384]{1,0:T(8,128)(2,1)S(1)}, bf16[128,384]{1,0:T(8,128)(2,1)S(1)}, u32[]{:S(2)}, u32[]{:S(2)}) %collective-permute-start.12) | collective-permute-done | bytes 98336 | tf_op jit(solution)/shard_map/ppermute | solution.py:498
  62.3 4.7 %collective-permute-done.10.refs_1_ = bf16[144,384]{1,0:T(8,128)(2,1)S(1)} collective-permute-done((bf16[144,384]{1,0:T(8,128)(2,1)S(1)}, bf16[144,384]{1,0:T(8,128)(2,1)S(1)}, u32[]{:S(2)}, u32[]{:S(2)}) %collective-permute-start.10) | collective-permute-done | bytes 110624 | tf_op jit(solution)/shard_map/ppermute | solution.py:498
  67.0 0.8 attend_part.3.refs_4_
  67.8 1.3 %collective-permute-start.15 = (bf16[2,128,128]{2,1,0:T(8,128)(2,1)S(1)}, bf16[2,128,128]{2,1,0:T(8,128)(2,1)S(1)}, u32[]{:S(2)}, u32[]{:S(2)}) collective-permute-start(bf16[2,128,128]{2,1,0:T(8,128)(2,1)S(1)} %attend_part.3.refs_4_), channel_id=1, source_target_pairs={{0,3},{1,2},{2,1},{3,0},{4,7},{5,6},{6,5},{7,4},{8,11},{9,10},{10,... | collective-permute-start | bytes 196616 | tf_op jit(solution)/shard_map/ppermute | solution.py:498
  69.2 2.3 %collective-permute-start.13 = (bf16[2,128,128]{2,1,0:T(8,128)(2,1)S(1)}, bf16[2,128,128]{2,1,0:T(8,128)(2,1)S(1)}, u32[]{:S(2)}, u32[]{:S(2)}) collective-permute-start(bf16[2,128,128]{2,1,0:T(8,128)(2,1)S(1)} %attend_part.3.refs_4_), channel_id=1, source_target_pairs={{0,1},{1,0},{2,3},{3,2},{4,5},{5,4},{6,7},{7,6},{8,9},{9,8},{10,11... | collective-permute-start | bytes 196616 | tf_op jit(solution)/shard_map/ppermute | solution.py:498
  71.5 1.4 %collective-permute-done.15.refs_7_ = bf16[2,128,128]{2,1,0:T(8,128)(2,1)S(1)} collective-permute-done((bf16[2,128,128]{2,1,0:T(8,128)(2,1)S(1)}, bf16[2,128,128]{2,1,0:T(8,128)(2,1)S(1)}, u32[]{:S(2)}, u32[]{:S(2)}) %collective-permute-start.15) | collective-permute-done | bytes 65568 | tf_op jit(solution)/shard_map/ppermute | solution.py:498
  72.9 1.3 %collective-permute-done.14.refs_6_ = bf16[2,128,128]{2,1,0:T(8,128)(2,1)S(1)} collective-permute-done((bf16[2,128,128]{2,1,0:T(8,128)(2,1)S(1)}, bf16[2,128,128]{2,1,0:T(8,128)(2,1)S(1)}, u32[]{:S(2)}, u32[]{:S(2)}) %collective-permute-start.14) | collective-permute-done | bytes 65568 | tf_op jit(solution)/shard_map/ppermute | solution.py:498
  74.2 1.0 %out_part.1 = (f32[128,640]{1,0:T(8,128)S(1)}, bf16[128,640]{1,0:T(8,128)(2,1)S(1)}) custom-call(s32[1]{0:T(128)S(6)} %select_n.18.core.half, s32[1]{0:T(128)} %bitcast.2.mine, bf16[2,128,128]{2,1,0:T(8,128)(2,1)S(1)} %attend_part.2.refs_0_, bf16[2,128,128]{2,1,0:T(8,128)(2,1)S(1)} %collective-permute-done.6.refs_1_, ...), custom_call_target="tpu_custom_call" | custom-call | tf_op jit(solution)/shard_map/out_part/pallas_call | solution.py:451
  75.2 3.2 %collective-permute-start.16 = (bf16[128,640]{1,0:T(8,128)(2,1)S(1)}, bf16[128,640]{1,0:T(8,128)(2,1)S(1)}, u32[]{:S(2)}, u32[]{:S(2)}) collective-permute-start(bf16[128,640]{1,0:T(8,128)(2,1)S(1)} %get-tuple-element.51), channel_id=1, source_target_pairs={{0,8},{8,0},{16,24},{24,16},{1,9},{9,1},{17,25},{25,17},{2,10},{10... | collective-permute-start | bytes 491528 | tf_op jit(solution)/shard_map/ppermute | solution.py:498
  78.5 1.0 %collective-permute-done.16 = bf16[128,640]{1,0:T(8,128)(2,1)S(1)} collective-permute-done((bf16[128,640]{1,0:T(8,128)(2,1)S(1)}, bf16[128,640]{1,0:T(8,128)(2,1)S(1)}, u32[]{:S(2)}, u32[]{:S(2)}) %collective-permute-start.16) | collective-permute-done | bytes 163872 | tf_op jit(solution)/shard_map/ppermute | solution.py:498
  79.5 2.2 %collective-permute-start.19 = (bf16[128,640]{1,0:T(8,128)(2,1)S(1)}, bf16[128,640]{1,0:T(8,128)(2,1)S(1)}, u32[]{:S(2)}, u32[]{:S(2)}) collective-permute-start(bf16[128,640]{1,0:T(8,128)(2,1)S(1)} %add_convert_fusion), channel_id=1, source_target_pairs={{0,20},{4,16},{8,28},{12,24},{16,4},{20,0},{24,12},{28,8},{1,21},{... | collective-permute-start | bytes 491528 | tf_op jit(solution)/shard_map/ppermute | solution.py:562
  81.8 0.2 collective-permute-start.18
  82.0 0.2 collective-permute-start.17
  82.2 0.7 dynamic-slice_reduce_fusion
  83.0 2.9 %collective-permute-done.19 = bf16[128,640]{1,0:T(8,128)(2,1)S(1)} collective-permute-done((bf16[128,640]{1,0:T(8,128)(2,1)S(1)}, bf16[128,640]{1,0:T(8,128)(2,1)S(1)}, u32[]{:S(2)}, u32[]{:S(2)}) %collective-permute-start.19) | collective-permute-done | bytes 163872 | tf_op jit(solution)/shard_map/ppermute | solution.py:562
  85.9 4.2 %collective-permute-done.18 = bf16[128,640]{1,0:T(8,128)(2,1)S(1)} collective-permute-done((bf16[128,640]{1,0:T(8,128)(2,1)S(1)}, bf16[128,640]{1,0:T(8,128)(2,1)S(1)}, u32[]{:S(2)}, u32[]{:S(2)}) %collective-permute-start.18) | collective-permute-done | bytes 163872 | tf_op jit(solution)/shard_map/ppermute | solution.py:498
  90.1 0.1 multiply_convert_fusion.rows
  90.2 0.7 collective-permute-start.20
  90.9 0.3 copy.19
  91.2 2.1 %grad_part.2.refs_0_ = bf16[2048,1280]{1,0:T(8,128)(2,1)} custom-call(s32[1]{0:T(128)S(6)} %select_n.18.core.half, bf16[2048,128]{1,0:T(8,128)(2,1)S(1)} %bitcast.9, bf16[128,640]{1,0:T(8,128)(2,1)S(1)} %multiply_convert_fusion.rows), custom_call_target="tpu_custom_call" | custom-call | tf_op jit(solution)/shard_map/grad_part/pallas_call | solution.py:487
  93.2 2.0 %grad_part.3 = bf16[2048,1280]{1,0:T(8,128)(2,1)} custom-call(s32[1]{0:T(128)S(6)} %sub.3.half, bf16[2048,128]{1,0:T(8,128)(2,1)S(1)} %bitcast.10, bf16[128,640]{1,0:T(8,128)(2,1)S(1)} %collective-permute-done.20.rows, bf16[2048,1280]{1,0:T(8,128)(2,1)} %grad_part.2.refs_0_), custom_call_target="tpu_custom_call", output_to_operand_aliasing={{}: (3, {})} | custom-call | tf_op jit(solution)/shard_map/grad_part/pallas_call | solution.py:487
  (36 shorter events, 0.1 us)
Async XLA Ops:
  0.6 39.7 %copy-start = (f32[2,2048]{1,0:T(2,128)S(1)}, f32[2,2048]{1,0:T(2,128)}, u32[]{:S(2)}) copy-start(f32[2,2048]{1,0:T(2,128)} %param.23) | copy-start | bytes 49156
  0.6 7.9 %copy-start.1 = (bf16[256,1280]{1,0:T(8,128)(2,1)S(1)}, bf16[256,1280]{1,0:T(8,128)(2,1)}, u32[]{:S(2)}) copy-start(bf16[256,1280]{1,0:T(8,128)(2,1)} %time_w.3) | copy-start | bytes 1966084
  0.7 7.9 %copy-start.2 = (bf16[256,3,1280]{2,0,1:T(8,128)(2,1)S(1)}, bf16[256,3,1280]{2,0,1:T(8,128)(2,1)}, u32[]{:S(2)}) copy-start(bf16[256,3,1280]{2,0,1:T(8,128)(2,1)} %param.22) | copy-start | bytes 5898244
  0.7 7.8 %copy-start.3 = (bf16[256,3,1280]{2,0,1:T(8,128)(2,1)S(1)}, bf16[256,3,1280]{2,0,1:T(8,128)(2,1)}, u32[]{:S(2)}) copy-start(bf16[256,3,1280]{2,0,1:T(8,128)(2,1)} %param.26) | copy-start | bytes 5898244
  2.2 6.3 %copy-start.11 = (bf16[8,256]{1,0:T(8,128)(2,1)S(1)}, bf16[8,256]{1,0:T(8,128)(2,1)}, u32[]{:S(2)}) copy-start(bf16[8,256]{1,0:T(8,128)(2,1)} %fusion.2.embed) | copy-start | bytes 12292
  2.2 13.5 %copy-start.15 = (s32[3]{0:T(128)S(1)}, s32[3]{0:T(128)}, u32[]{:S(2)}) copy-start(s32[3]{0:T(128)} %param.19) | copy-start | bytes 40
  2.2 14.7 %copy-start.5 = (bf16[64,1280]{1,0:T(8,128)(2,1)S(1)}, bf16[64,1280]{1,0:T(8,128)(2,1)}, u32[]{:S(2)}) copy-start(bf16[64,1280]{1,0:T(8,128)(2,1)} %noise.3) | copy-start | bytes 491524
  6.4 8.0 %collective-permute-start = (bf16[192,640]{1,0:T(8,128)(2,1)}, bf16[192,640]{1,0:T(8,128)(2,1)S(1)}, u32[]{:S(2)}, u32[]{:S(2)}) collective-permute-start(bf16[192,640]{1,0:T(8,128)(2,1)} %get-tuple-element.28), channel_id=1, source_target_pairs={{0,4},{4,0},{1,5},{5,1},{2,6},{6,2},{3,7},{7,3},{8,12},{12,8},{9,1... | collective-permute-start | bytes 737288 | tf_op jit(solution)/shard_map/ppermute | solution.py:498
  8.5 1.0 %copy-start.4 = (f32[128,640]{1,0:T(8,128)S(1)}, f32[128,640]{1,0:T(8,128)}, u32[]{:S(2)}) copy-start(f32[128,640]{1,0:T(8,128)} %get-tuple-element.27.after.full) | copy-start | bytes 983044
  10.2 4.2 %copy-start.10 = (f32[8,1280]{1,0:T(8,128)}, f32[8,1280]{1,0:T(8,128)S(1)}, u32[]{:S(2)}) copy-start(f32[8,1280]{1,0:T(8,128)S(1)} %get-tuple-element.29.after) | copy-start | bytes 122884
  14.5 2.4 %collective-permute-start.1 = (bf16[192,640]{1,0:T(8,128)(2,1)S(1)}, bf16[192,640]{1,0:T(8,128)(2,1)S(1)}, u32[]{:S(2)}, u32[]{:S(2)}) collective-permute-start(bf16[192,640]{1,0:T(8,128)(2,1)S(1)} %join_part.1.joined), channel_id=1, source_target_pairs={{0,8},{8,0},{16,24},{24,16},{1,9},{9,1},{17,25},{25,17},{2,10},{10... | collective-permute-start | bytes 737288 | tf_op jit(solution)/shard_map/ppermute | solution.py:498
  23.3 13.2 %copy-start.8 = (bf16[2,128,384]{2,1,0:T(8,128)(2,1)}, bf16[2,128,384]{2,1,0:T(8,128)(2,1)S(1)}, u32[]{:S(2)}) copy-start(bf16[2,128,384]{2,1,0:T(8,128)(2,1)S(1)} %get-tuple-element.46.mine) | copy-start | bytes 589828
  23.3 6.4 %collective-permute-start.4 = (bf16[2,128,384]{2,1,0:T(8,128)(2,1)S(1)}, bf16[2,128,384]{2,1,0:T(8,128)(2,1)S(1)}, u32[]{:S(2)}, u32[]{:S(2)}) collective-permute-start(bf16[2,128,384]{2,1,0:T(8,128)(2,1)S(1)} %get-tuple-element.38), channel_id=1, source_target_pairs={{0,1},{1,0},{2,3},{3,2},{4,5},{5,4},{6,7},{7,6},{8,9},{9,8},{10,11... | collective-permute-start | bytes 589832 | tf_op jit(solution)/shard_map/ppermute | solution.py:498
  24.9 9.5 %collective-permute-start.2 = (bf16[2,144,384]{2,1,0:T(8,128)(2,1)S(1)}, bf16[2,144,384]{2,1,0:T(8,128)(2,1)S(1)}, u32[]{:S(2)}, u32[]{:S(2)}) collective-permute-start(bf16[2,144,384]{2,1,0:T(8,128)(2,1)S(1)} %get-tuple-element.33), channel_id=1, source_target_pairs={{0,1},{1,0},{2,3},{3,2},{4,5},{5,4},{6,7},{7,6},{8,9},{9,8},{10,11... | collective-permute-start | bytes 663560 | tf_op jit(solution)/shard_map/ppermute | solution.py:498
  29.8 0.6 copy-start.13
  30.4 4.7 %copy-start.6 = (f32[128,384]{1,0:T(8,128)}, f32[128,384]{1,0:T(8,128)S(1)}, u32[]{:S(2)}) copy-start(f32[128,384]{1,0:T(8,128)S(1)} %get-tuple-element.40.refs_2_) | copy-start | bytes 589828
  30.4 20.4 %collective-permute-start.11 = (bf16[2,128,384]{2,1,0:T(8,128)(2,1)}, bf16[2,128,384]{2,1,0:T(8,128)(2,1)}, u32[]{:S(2)}, u32[]{:S(2)}) collective-permute-start(bf16[2,128,384]{2,1,0:T(8,128)(2,1)} %get-tuple-element.47), channel_id=1, source_target_pairs={{0,1},{1,0},{2,3},{3,2},{4,5},{5,4},{6,7},{7,6},{8,9},{9,8},{10,11... | collective-permute-start | bytes 589832 | tf_op jit(solution)/shard_map/ppermute | solution.py:498
  34.5 0.6 copy-start.12
  35.1 19.8 %collective-permute-start.9 = (bf16[2,144,384]{2,1,0:T(8,128)(2,1)}, bf16[2,144,384]{2,1,0:T(8,128)(2,1)S(1)}, u32[]{:S(2)}, u32[]{:S(2)}) collective-permute-start(bf16[2,144,384]{2,1,0:T(8,128)(2,1)} %get-tuple-element.43), channel_id=1, source_target_pairs={{0,1},{1,0},{2,3},{3,2},{4,5},{5,4},{6,7},{7,6},{8,9},{9,8},{10,11... | collective-permute-start | bytes 663560 | tf_op jit(solution)/shard_map/ppermute | solution.py:498
  37.9 6.5 %collective-permute-start.5 = (bf16[128,384]{1,0:T(8,128)(2,1)}, bf16[128,384]{1,0:T(8,128)(2,1)S(1)}, u32[]{:S(2)}, u32[]{:S(2)}) collective-permute-start(bf16[128,384]{1,0:T(8,128)(2,1)} %copy-done.13), channel_id=1, source_target_pairs={{0,2},{1,3},{2,0},{3,1},{4,6},{5,7},{6,4},{7,5},{8,10},{9,11},{10,... | collective-permute-start | bytes 294920 | tf_op jit(solution)/shard_map/ppermute | solution.py:498
  40.3 6.9 %collective-permute-start.3 = (bf16[144,384]{1,0:T(8,128)(2,1)}, bf16[144,384]{1,0:T(8,128)(2,1)S(1)}, u32[]{:S(2)}, u32[]{:S(2)}) collective-permute-start(bf16[144,384]{1,0:T(8,128)(2,1)} %copy-done.12), channel_id=1, source_target_pairs={{0,2},{1,3},{2,0},{3,1},{4,6},{5,7},{6,4},{7,5},{8,10},{9,11},{10,... | collective-permute-start | bytes 331784 | tf_op jit(solution)/shard_map/ppermute | solution.py:498
  47.2 0.9 copy-start.7
  48.9 20.3 %collective-permute-start.8 = (bf16[2,128,128]{2,1,0:T(8,128)(2,1)S(1)}, bf16[2,128,128]{2,1,0:T(8,128)(2,1)S(1)}, u32[]{:S(2)}, u32[]{:S(2)}) collective-permute-start(bf16[2,128,128]{2,1,0:T(8,128)(2,1)S(1)} %attend_part.2.refs_0_), channel_id=1, source_target_pairs={{0,3},{1,2},{2,1},{3,0},{4,7},{5,6},{6,5},{7,4},{8,11},{9,10},{10,... | collective-permute-start | bytes 196616 | tf_op jit(solution)/shard_map/ppermute | solution.py:498
  50.8 0.9 copy-start.9
  52.7 9.6 %collective-permute-start.12 = (bf16[128,384]{1,0:T(8,128)(2,1)S(1)}, bf16[128,384]{1,0:T(8,128)(2,1)S(1)}, u32[]{:S(2)}, u32[]{:S(2)}) collective-permute-start(bf16[128,384]{1,0:T(8,128)(2,1)S(1)} %get-tuple-element.49), channel_id=1, source_target_pairs={{0,2},{1,3},{2,0},{3,1},{4,6},{5,7},{6,4},{7,5},{8,10},{9,11},{10,... | collective-permute-start | bytes 294920 | tf_op jit(solution)/shard_map/ppermute | solution.py:498
  55.0 35.9 %copy-start.14 = (bf16[128,2048]{1,0:T(8,128)(2,1)S(1)}, bf16[128,2048]{1,0:T(8,128)(2,1)}, u32[]{:S(2)}) copy-start(bf16[128,2048]{1,0:T(8,128)(2,1)} %heads.1) | copy-start | bytes 1572868
  55.0 12.1 %collective-permute-start.10 = (bf16[144,384]{1,0:T(8,128)(2,1)S(1)}, bf16[144,384]{1,0:T(8,128)(2,1)S(1)}, u32[]{:S(2)}, u32[]{:S(2)}) collective-permute-start(bf16[144,384]{1,0:T(8,128)(2,1)S(1)} %get-tuple-element.45), channel_id=1, source_target_pairs={{0,2},{1,3},{2,0},{3,1},{4,6},{5,7},{6,4},{7,5},{8,10},{9,11},{10,... | collective-permute-start | bytes 331784 | tf_op jit(solution)/shard_map/ppermute | solution.py:498
  56.0 15.5 %collective-permute-start.7 = (bf16[2,128,128]{2,1,0:T(8,128)(2,1)S(1)}, bf16[2,128,128]{2,1,0:T(8,128)(2,1)S(1)}, u32[]{:S(2)}, u32[]{:S(2)}) collective-permute-start(bf16[2,128,128]{2,1,0:T(8,128)(2,1)S(1)} %attend_part.2.refs_0_), channel_id=1, source_target_pairs={{0,2},{1,3},{2,0},{3,1},{4,6},{5,7},{6,4},{7,5},{8,10},{9,11},{10,... | collective-permute-start | bytes 196616 | tf_op jit(solution)/shard_map/ppermute | solution.py:498
  58.1 13.4 %collective-permute-start.6 = (bf16[2,128,128]{2,1,0:T(8,128)(2,1)S(1)}, bf16[2,128,128]{2,1,0:T(8,128)(2,1)S(1)}, u32[]{:S(2)}, u32[]{:S(2)}) collective-permute-start(bf16[2,128,128]{2,1,0:T(8,128)(2,1)S(1)} %attend_part.2.refs_0_), channel_id=1, source_target_pairs={{0,1},{1,0},{2,3},{3,2},{4,5},{5,4},{6,7},{7,6},{8,9},{9,8},{10,11... | collective-permute-start | bytes 196616 | tf_op jit(solution)/shard_map/ppermute | solution.py:498
  67.8 5.1 %collective-permute-start.15 = (bf16[2,128,128]{2,1,0:T(8,128)(2,1)S(1)}, bf16[2,128,128]{2,1,0:T(8,128)(2,1)S(1)}, u32[]{:S(2)}, u32[]{:S(2)}) collective-permute-start(bf16[2,128,128]{2,1,0:T(8,128)(2,1)S(1)} %attend_part.3.refs_4_), channel_id=1, source_target_pairs={{0,3},{1,2},{2,1},{3,0},{4,7},{5,6},{6,5},{7,4},{8,11},{9,10},{10,... | collective-permute-start | bytes 196616 | tf_op jit(solution)/shard_map/ppermute | solution.py:498
  69.2 5.1 %collective-permute-start.14 = (bf16[2,128,128]{2,1,0:T(8,128)(2,1)S(1)}, bf16[2,128,128]{2,1,0:T(8,128)(2,1)S(1)}, u32[]{:S(2)}, u32[]{:S(2)}) collective-permute-start(bf16[2,128,128]{2,1,0:T(8,128)(2,1)S(1)} %attend_part.3.refs_4_), channel_id=1, source_target_pairs={{0,2},{1,3},{2,0},{3,1},{4,6},{5,7},{6,4},{7,5},{8,10},{9,11},{10,... | collective-permute-start | bytes 196616 | tf_op jit(solution)/shard_map/ppermute | solution.py:498
  69.2 5.1 %collective-permute-start.13 = (bf16[2,128,128]{2,1,0:T(8,128)(2,1)S(1)}, bf16[2,128,128]{2,1,0:T(8,128)(2,1)S(1)}, u32[]{:S(2)}, u32[]{:S(2)}) collective-permute-start(bf16[2,128,128]{2,1,0:T(8,128)(2,1)S(1)} %attend_part.3.refs_4_), channel_id=1, source_target_pairs={{0,1},{1,0},{2,3},{3,2},{4,5},{5,4},{6,7},{7,6},{8,9},{9,8},{10,11... | collective-permute-start | bytes 196616 | tf_op jit(solution)/shard_map/ppermute | solution.py:498
  75.2 4.3 %collective-permute-start.16 = (bf16[128,640]{1,0:T(8,128)(2,1)S(1)}, bf16[128,640]{1,0:T(8,128)(2,1)S(1)}, u32[]{:S(2)}, u32[]{:S(2)}) collective-permute-start(bf16[128,640]{1,0:T(8,128)(2,1)S(1)} %get-tuple-element.51), channel_id=1, source_target_pairs={{0,8},{8,0},{16,24},{24,16},{1,9},{9,1},{17,25},{25,17},{2,10},{10... | collective-permute-start | bytes 491528 | tf_op jit(solution)/shard_map/ppermute | solution.py:498
  79.5 6.4 %collective-permute-start.19 = (bf16[128,640]{1,0:T(8,128)(2,1)S(1)}, bf16[128,640]{1,0:T(8,128)(2,1)S(1)}, u32[]{:S(2)}, u32[]{:S(2)}) collective-permute-start(bf16[128,640]{1,0:T(8,128)(2,1)S(1)} %add_convert_fusion), channel_id=1, source_target_pairs={{0,20},{4,16},{8,28},{12,24},{16,4},{20,0},{24,12},{28,8},{1,21},{... | collective-permute-start | bytes 491528 | tf_op jit(solution)/shard_map/ppermute | solution.py:562
  81.8 8.4 %collective-permute-start.18 = (bf16[128,640]{1,0:T(8,128)(2,1)S(1)}, bf16[128,640]{1,0:T(8,128)(2,1)S(1)}, u32[]{:S(2)}, u32[]{:S(2)}) collective-permute-start(bf16[128,640]{1,0:T(8,128)(2,1)S(1)} %add_convert_fusion), channel_id=1, source_target_pairs={{0,16},{8,24},{16,0},{24,8},{1,17},{9,25},{17,1},{25,9},{2,18},{10... | collective-permute-start | bytes 491528 | tf_op jit(solution)/shard_map/ppermute | solution.py:498
  82.0 8.1 %collective-permute-start.17 = (bf16[128,640]{1,0:T(8,128)(2,1)S(1)}, bf16[128,640]{1,0:T(8,128)(2,1)S(1)}, u32[]{:S(2)}, u32[]{:S(2)}) collective-permute-start(bf16[128,640]{1,0:T(8,128)(2,1)S(1)} %add_convert_fusion), channel_id=1, source_target_pairs={{0,4},{4,0},{1,5},{5,1},{2,6},{6,2},{3,7},{7,3},{8,12},{12,8},{9,1... | collective-permute-start | bytes 491528 | tf_op jit(solution)/shard_map/ppermute | solution.py:498
  90.2 3.0 %collective-permute-start.20 = (bf16[128,640]{1,0:T(8,128)(2,1)S(1)}, bf16[128,640]{1,0:T(8,128)(2,1)S(1)}, u32[]{:S(2)}, u32[]{:S(2)}) collective-permute-start(bf16[128,640]{1,0:T(8,128)(2,1)S(1)} %multiply_convert_fusion.rows), channel_id=1, source_target_pairs={{0,8},{8,0},{16,24},{24,16},{1,9},{9,1},{17,25},{25,17},{2,10},{10... | collective-permute-start | bytes 491528 | tf_op jit(solution)/shard_map/ppermute | solution.py:498

commit v4 on v3

--- a/solution.py
+++ b/solution.py
@@ -161,6 +161,7 @@
 
 
 GEN_CUTS = 4
+AHEAD = 2
 
 
 def gen_kernel(seq, core, embed, heads, weight, time_w, resid, noise, full, sent, heads_v, weight_v, time_v, resid_v, sems):
@@ -175,12 +176,15 @@
     copies.append(pltpu.make_async_copy(time_w.at[:, cols], time_v, sems.at[GEN_CUTS + 1]))
     copies.append(pltpu.make_async_copy(resid.at[:, cols], resid_v, sems.at[GEN_CUTS + 2]))
     copies.append(pltpu.make_async_copy(noise.at[:, cols], sent.at[pl.ds(length, own), :], sems.at[GEN_CUTS + 3]))
-    for copy in copies:
+    for copy in copies[: 1 + AHEAD]:
         copy.start()
     copies[0].wait()
     total = None
     for k in range(GEN_CUTS):
         copies[1 + k].wait()
+        following = copies[1 + k + AHEAD : 2 + k + AHEAD] if k + AHEAD < GEN_CUTS - 1 else copies[GEN_CUTS:]
+        for copy in following if k + AHEAD < GEN_CUTS else []:
+            copy.start()
         rows = pl.ds(k * tile, tile)
         term = dot32(heads_v[:, rows], weight_v[rows, :])
         total = term if total is None else total + term
@@ -274,7 +278,10 @@
     rows = jnp.concatenate([top, low, extra], axis=0).astype(jnp.bfloat16)
     row_id = lax.broadcasted_iota(jnp.int32, (EXTRA_ROWS, unit), 0)
     for part in range(3):
-        copies[part].wait()
+        turn = 3 * index + part
+        copies[turn].wait()
+        if turn + AHEAD < len(copies):
+            copies[turn + AHEAD].start()
         result[...] = dot32(rows, weight[part])
         cols = pl.ds(part * unit, unit)
         for slot in range(groups):
@@ -299,7 +306,8 @@
         ]
         for index in range(2)
     ]
-    for copy in copies[0] + copies[1]:
+    copies = copies[0] + copies[1]
+    for copy in copies[:AHEAD]:
         copy.start()
     return copies
 
@@ -328,7 +336,7 @@
     sums = jnp.broadcast_to(sums, (tokens, length)).T[0:8]
     for index in range(2):
         kept, sent = chunks[4 * index : 4 * index + 2], chunks[4 * index + 2 : 4 * index + 4]
-        project(index, mine[0], mixed, sums, mods, weight.at[index], copies[index], kept, sent, result)
+        project(index, mine[0], mixed, sums, mods, weight.at[index], copies, kept, sent, result)
 
 
 def chunk_shapes(length, cols):
@@ -360,28 +368,29 @@
     )(role, seq, core, mine, levels, joined, swapped, noise, mods, planes_a, planes_b)
 
 
-def add_kernel(mine, theirs, *refs):
-    kept, sent = refs[-3:-1] if len(refs) > 2 else refs
+def add_kernel(passed, mine, theirs, *refs):
+    kept, sent = refs[-2 - passed :][:2]
+    if passed:
+        refs[-1][...] = refs[0][...]
     kept[...] = mine[0].astype(jnp.float32) + theirs[0].astype(jnp.float32)
     sent[...] = (mine[1].astype(jnp.float32) + theirs[1].astype(jnp.float32)).astype(jnp.bfloat16)
 
 
-def add_part(mine, theirs, later=None):
+def add_part(mine, theirs, later=None, after=()):
     rest = [] if later is None else [later]
     shape = mine.shape[1:]
     return pl.pallas_call(
-        add_kernel,
-        in_specs=[vmem_spec()] * 2 + [any_spec()] * len(rest),
-        out_specs=[vmem_spec()] * 2 + [any_spec()] * len(rest),
+        lambda *refs: add_kernel(len(rest), *refs),
+        in_specs=[vmem_spec()] * (2 + len(rest)) + [any_spec()] * len(after),
+        out_specs=[vmem_spec()] * (2 + len(rest)),
         out_shape=[jax.ShapeDtypeStruct(shape, jnp.float32), jax.ShapeDtypeStruct(shape, jnp.bfloat16)]
         + [jax.ShapeDtypeStruct(x.shape, x.dtype) for x in rest],
-        input_output_aliases={2: 2} if rest else {},
         compiler_params=params(8),
         name="add_part",
-    )(mine, theirs, *rest)
-
-
-def attend_kernel(width, kept_a, other_a, kept_b, other_b, gains, after, out):
+    )(mine, theirs, *rest, *after)
+
+
+def attend_kernel(width, kept_a, other_a, kept_b, other_b, gains, after_a, after_b, out):
     _, length, unit = out.shape
     extra = None
     for level, (kept, other) in enumerate(((kept_a, other_a), (kept_b, other_b))):
@@ -416,12 +425,12 @@
     length = kept_a.shape[0] - EXTRA_ROWS
     return pl.pallas_call(
         lambda *refs: attend_kernel(width, *refs),
-        in_specs=[vmem_spec()] * 5 + [any_spec()],
+        in_specs=[vmem_spec()] * 5 + [any_spec()] * 2,
         out_specs=vmem_spec(),
         out_shape=jax.ShapeDtypeStruct((2, length, unit), jnp.bfloat16),
         compiler_params=params(8),
         name="attend_part",
-    )(kept_a, chunks[0][1], kept_b, chunks[1][1], gains, after)
+    )(kept_a, chunks[0][1], kept_b, chunks[1][1], gains, *after)
 
 
 def out_kernel(core, mine, *refs):
@@ -545,14 +554,15 @@
         role_at, seq_at, core, mine, levels, joined, swapped, noise, mods, planes[0], planes[1], part_cols
     )
     first, second = chunks[:4], chunks[4:]
-    kept_a, send_a, third = add_part(first[0], exchange(first[2], "mp", 1), second[2])
+    early = (out_a, out_b, *gains)
+    kept_a, send_a, third = add_part(first[0], exchange(first[2], "mp", 1), second[2], early)
     kept_b, send_b, last = add_part(first[1], exchange(first[3], "mp", 1), second[3])
     kept_c, send_c = add_part(second[0], exchange(third, "mp", 1))
     kept_d, send_d = add_part(second[1], exchange(last, "mp", 1))
     sums = [(kept, exchange(send, "mp", 2)) for kept, send in ((kept_a, send_a), (kept_b, send_b))]
-    head_a = attend_part(sums, gains[0], out_a, D)
+    head_a = attend_part(sums, gains[0], (send_c, send_d), D)
     sums = [(kept, exchange(send, "mp", 2)) for kept, send in ((kept_c, send_c), (kept_d, send_d))]
-    head_b = attend_part(sums, gains[1], out_b, D)
+    head_b = attend_part(sums, gains[1], (out_a, out_b), D)
     gathered = [[head] + [exchange(head, "mp", bits) for bits in range(1, groups)] for head in (head_a, head_b)]
 
     kept, sent = out_part(core, mine, *gathered, out_a, out_b, mods)

time: 95.6 us -> 97.6 us (1.021)
  local copies, waits for them, and re-layouts: 8.63 us -> 10.3 us
  Pallas kernels: 19.1 us -> 20.7 us
    unnamed x33, local copies, waits for them, and re-layouts: 4.4 us -> 7.68 us
    ppermute x20, waiting for transfers between devices: 35 us -> 33.5 us  [exchange(): lax.ppermute(array, axis, [(i, i ^ bit) for i in range(lax.axis_size(axis...]
    pallas_call x4, Pallas kernels: 1.14 us -> 2.17 us  [add_part(): pl.pallas_call(lambda *refs: add_kernel(len(rest), *refs), in_specs=[vmem...]
    dynamic_slice x2 -> x1, local copies, waits for them, and re-layouts: 2.8 us -> 1.88 us  [heads_per_role(): lax.dynamic_slice_in_dim(w, start, part_cols, axis=0)]
  transfers between devices with their start and end apart: 21 -> 21, of which waited for: 13 -> 11; matrix products, arithmetic and copies ran while one was open for 5% -> 3% of each run, Pallas kernels for 6% -> 7%
where the time goes in v4:
time: 97.6 us; the launch traced here: 97 us
  waiting for transfers between devices  37.2 us (38%)
  starting transfers between devices  26.4 us (27%)
  Pallas kernels  20.7 us (21%)
  local copies, waits for them, and re-layouts  10.3 us (11%)
  other arithmetic  1.75 us (2%)
    ppermute x20, waiting for transfers between devices, exchange(): lax.ppermute(array, axis, [(i, i ^ bit) for i in range(lax.axis_size(axis...  33.5 us
    ppermute x20, starting transfers between devices, exchange(): lax.ppermute(array, axis, [(i, i ^ bit) for i in range(lax.axis_size(axis...  24.2 us
    unnamed x33, local copies, waits for them, and re-layouts  7.68 us
    pallas_call x1, Pallas kernels, qkv_part(): pl.pallas_call(qkv_kernel, in_specs=[smem_spec()] * 5 + [vmem_spec()] * 4...  6.33 us
    pallas_call x1, Pallas kernels, gen_part(): pl.pallas_call(gen_kernel, in_specs=[smem_spec(), smem_spec(), vmem_spec(...  4.73 us
    pallas_call x2, Pallas kernels, grad_part(): pl.pallas_call(grad_kernel, grid_spec=grid_spec, out_shape=jax.ShapeDtype...  4.11 us
    ppermute x1, waiting for transfers between devices, heads_per_role(): lax.ppermute(total, ('role', 'seq'), [(i, i ^ 2 * lax.axis_size('seq') +...  3.65 us
    pallas_call x4, Pallas kernels, add_part(): pl.pallas_call(lambda *refs: add_kernel(len(rest), *refs), in_specs=[vmem...  2.17 us
  transfers between devices with their start and end apart: 21, of which 11 were waited for; matrix products, arithmetic and copies ran while one was open for 3% of the time, Pallas kernels for 7%

profile of v4, /device:TPU:1, one launch (start us, length us, event | category | flops | bytes accessed | tf_op | source)
XLA Modules:
  0.0 97.0 jit_solution(3473952004226067155)
XLA Ops:
  0.6 0.0 copy-start
  0.7 0.0 copy-start.2
  0.7 0.8 convert_element_type.29
  1.5 0.1 fusion.3
  1.6 0.6 fusion.2.embed
  2.2 4.7 %gen_part.1 = (f32[128,640]{1,0:T(8,128)}, bf16[192,640]{1,0:T(8,128)(2,1)}) custom-call(s32[1]{0:T(128)} %bitcast.1.seq, s32[1]{0:T(128)S(6)} %select_n.18.core.half, bf16[8,256]{1,0:T(8,128)(2,1)} %fusion.2.embed, bf16[128,2048]{1,0:T(8,128)(2,1)} %heads.1, bf16[2048,1280]{1,0:T(8,128)(2,1)} %weight.1, bf16[256,1280]{1,0:T(8,128)(2,1)} %time_w.3, ...), custom_call_target="tpu_custom_call" | custom-call | tf_op jit(solution)/shard_map/gen_part/pallas_call | solution.py:204
  7.0 2.1 %collective-permute-start = (bf16[192,640]{1,0:T(8,128)(2,1)}, bf16[192,640]{1,0:T(8,128)(2,1)S(1)}, u32[]{:S(2)}, u32[]{:S(2)}) collective-permute-start(bf16[192,640]{1,0:T(8,128)(2,1)} %get-tuple-element.28), channel_id=1, source_target_pairs={{0,4},{4,0},{1,5},{5,1},{2,6},{6,2},{3,7},{7,3},{8,12},{12,8},{9,1... | collective-permute-start | bytes 737288 | tf_op jit(solution)/shard_map/ppermute | solution.py:507
  9.1 0.0 copy-start.3
  9.1 1.0 copy-done.3
  10.1 0.7 mod_part.1
  10.8 4.2 %collective-permute-done.arrived = bf16[192,640]{1,0:T(8,128)(2,1)S(1)} collective-permute-done((bf16[192,640]{1,0:T(8,128)(2,1)}, bf16[192,640]{1,0:T(8,128)(2,1)S(1)}, u32[]{:S(2)}, u32[]{:S(2)}) %collective-permute-start) | collective-permute-done | bytes 245792 | tf_op jit(solution)/shard_map/ppermute | solution.py:507
  15.0 1.3 %collective-permute-start.1 = (bf16[192,640]{1,0:T(8,128)(2,1)S(1)}, bf16[192,640]{1,0:T(8,128)(2,1)S(1)}, u32[]{:S(2)}, u32[]{:S(2)}) collective-permute-start(bf16[192,640]{1,0:T(8,128)(2,1)S(1)} %join_part.1.joined), channel_id=1, source_target_pairs={{0,8},{8,0},{16,24},{24,16},{1,9},{9,1},{17,25},{25,17},{2,10},{10... | collective-permute-start | bytes 737288 | tf_op jit(solution)/shard_map/ppermute | solution.py:507
  16.3 0.1 convert_multiply_fusion.levels
  16.4 1.1 %collective-permute-done.1.swapped = bf16[192,640]{1,0:T(8,128)(2,1)S(1)} collective-permute-done((bf16[192,640]{1,0:T(8,128)(2,1)S(1)}, bf16[192,640]{1,0:T(8,128)(2,1)S(1)}, u32[]{:S(2)}, u32[]{:S(2)}) %collective-permute-start.1) | collective-permute-done | bytes 245792 | tf_op jit(solution)/shard_map/ppermute | solution.py:507
  17.4 6.3 %qkv_part.1 = (bf16[64,1280]{1,0:T(8,128)(2,1)}, bf16[2,144,384]{2,1,0:T(8,128)(2,1)S(1)}, bf16[2,128,384]{2,1,0:T(8,128)(2,1)S(1)}, bf16[2,144,384]{2,1,0:T(8,1...) custom-call(s32[1]{0:T(128)} %bitcast.role, ...), custom_call_target="tpu_custom_call" | custom-call | tf_op jit(solution)/shard_map/qkv_part/pallas_call | solution.py:354
  23.8 0.7 copy-done.5
  24.5 0.7 copy-done.7
  25.1 0.7 copy-done.9
  25.8 0.7 copy-done.11
  26.5 1.5 %collective-permute-start.4 = (bf16[2,128,384]{2,1,0:T(8,128)(2,1)}, bf16[2,128,384]{2,1,0:T(8,128)(2,1)}, u32[]{:S(2)}, u32[]{:S(2)}) collective-permute-start(bf16[2,128,384]{2,1,0:T(8,128)(2,1)} %get-tuple-element.38), channel_id=1, source_target_pairs={{0,1},{1,0},{2,3},{3,2},{4,5},{5,4},{6,7},{7,6},{8,9},{9,8},{10,11... | collective-permute-start | bytes 589832 | tf_op jit(solution)/shard_map/ppermute | solution.py:507
  28.0 0.0 collective-permute-start.2
  28.1 1.9 %constant_dynamic-slice_fusion.2 = (bf16[512,1280]{1,0:T(8,128)(2,1)S(1)}, bf16[512,1280]{1,0:T(8,128)(2,1)S(1)}) fusion(bf16[2048,1280]{1,0:T(8,128)(2,1)} %param.25, s32[]{:T(128)S(6)} %select_n.20, bf16[2048,1280]{1,0:T(8,128)(2,1)} %param.21), kind=kLoop, calls=%fused_computation.13 | loop fusion | bytes 5242884 | tf_op jit(solution)/shard_map/dynamic_slice | solution.py:549
  30.0 0.7 constant_dynamic-slice_fusion
  30.7 7.2 %collective-permute-done.2.refs_1_ = bf16[2,144,384]{2,1,0:T(8,128)(2,1)} collective-permute-done((bf16[2,144,384]{2,1,0:T(8,128)(2,1)}, bf16[2,144,384]{2,1,0:T(8,128)(2,1)}, u32[]{:S(2)}, u32[]{:S(2)}) %collective-permute-start.2) | collective-permute-done | bytes 221216 | tf_op jit(solution)/shard_map/ppermute | solution.py:507
  37.8 1.0 %add_part.4 = (f32[144,384]{1,0:T(8,128)S(1)}, bf16[144,384]{1,0:T(8,128)(2,1)S(1)}, bf16[2,144,384]{2,1,0:T(8,128)(2,1)S(1)}) custom-call(bf16[2,144,384]{2,1,0:T(8,128)(2,1)S(1)} %get-tuple-element.32.refs_0_, bf16[2,144,384]{2,1,0:T(8,128)(2,1)} %collective-permute-done.2.refs_1_, bf16[2,144,384]{2,1,0:T(8,128)(2,1)S(1)} %get-tuple-element.34.refs_2_, ...), custom_call_target="tpu_custom_call" | custom-call | tf_op jit(solution)/shard_map/add_part/pallas_call | solution.py:382
  38.8 1.4 %collective-permute-start.6 = (bf16[2,144,384]{2,1,0:T(8,128)(2,1)S(1)}, bf16[2,144,384]{2,1,0:T(8,128)(2,1)S(1)}, u32[]{:S(2)}, u32[]{:S(2)}) collective-permute-start(bf16[2,144,384]{2,1,0:T(8,128)(2,1)S(1)} %get-tuple-element.43), channel_id=1, source_target_pairs={{0,1},{1,0},{2,3},{3,2},{4,5},{5,4},{6,7},{7,6},{8,9},{9,8},{10,11... | collective-permute-start | bytes 663560 | tf_op jit(solution)/shard_map/ppermute | solution.py:507
  40.3 0.9 copy-done.10
  41.2 0.9 copy-done.12
  42.1 1.0 %add_part.5 = (f32[128,384]{1,0:T(8,128)S(1)}, bf16[128,384]{1,0:T(8,128)(2,1)S(1)}, bf16[2,128,384]{2,1,0:T(8,128)(2,1)S(1)}) custom-call(bf16[2,128,384]{2,1,0:T(8,128)(2,1)S(1)} %copy-done.10, bf16[2,128,384]{2,1,0:T(8,128)(2,1)} %collective-permute-done.4.refs_1_, bf16[2,128,384]{2,1,0:T(8,128)(2,1)S(1)} %copy-done.12), custom_call_target="tpu_custom_call" | custom-call | tf_op jit(solution)/shard_map/add_part/pallas_call | solution.py:382
  43.2 0.2 collective-permute-start.7
  43.4 2.4 %collective-permute-start.3 = (bf16[144,384]{1,0:T(8,128)(2,1)S(1)}, bf16[144,384]{1,0:T(8,128)(2,1)S(1)}, u32[]{:S(2)}, u32[]{:S(2)}) collective-permute-start(bf16[144,384]{1,0:T(8,128)(2,1)S(1)} %get-tuple-element.36), channel_id=1, source_target_pairs={{0,2},{1,3},{2,0},{3,1},{4,6},{5,7},{6,4},{7,5},{8,10},{9,11},{10,... | collective-permute-start | bytes 331784 | tf_op jit(solution)/shard_map/ppermute | solution.py:507
  45.7 0.0 collective-permute-start.5
  45.8 0.0 collective-permute-done.6.refs_1_
  45.8 0.9 copy-done.6
  46.7 0.1 add_part.6
  46.8 2.4 %collective-permute-start.11 = (bf16[144,384]{1,0:T(8,128)(2,1)S(1)}, bf16[144,384]{1,0:T(8,128)(2,1)S(1)}, u32[]{:S(2)}, u32[]{:S(2)}) collective-permute-start(bf16[144,384]{1,0:T(8,128)(2,1)S(1)} %get-tuple-element.44.refs_5_), channel_id=1, source_target_pairs={{0,2},{1,3},{2,0},{3,1},{4,6},{5,7},{6,4},{7,5},{8,10},{9,11},{10,... | collective-permute-start | bytes 331784 | tf_op jit(solution)/shard_map/ppermute | solution.py:507
  49.2 5.4 %collective-permute-done.7.refs_1_ = bf16[2,128,384]{2,1,0:T(8,128)(2,1)S(1)} collective-permute-done((bf16[2,128,384]{2,1,0:T(8,128)(2,1)S(1)}, bf16[2,128,384]{2,1,0:T(8,128)(2,1)S(1)}, u32[]{:S(2)}, u32[]{:S(2)}) %collective-permute-start.7) | collective-permute-done | bytes 196640 | tf_op jit(solution)/shard_map/ppermute | solution.py:507
  54.6 0.9 copy-done.8
  55.6 0.1 collective-permute-start.12
  55.7 0.0 collective-permute-done.5.refs_3_
  55.7 0.8 attend_part.2.refs_0_
  56.5 1.3 %collective-permute-start.10 = (bf16[2,128,128]{2,1,0:T(8,128)(2,1)S(1)}, bf16[2,128,128]{2,1,0:T(8,128)(2,1)S(1)}, u32[]{:S(2)}, u32[]{:S(2)}) collective-permute-start(bf16[2,128,128]{2,1,0:T(8,128)(2,1)S(1)} %attend_part.2.refs_0_), channel_id=1, source_target_pairs={{0,3},{1,2},{2,1},{3,0},{4,7},{5,6},{6,5},{7,4},{8,11},{9,10},{10,... | collective-permute-start | bytes 196616 | tf_op jit(solution)/shard_map/ppermute | solution.py:507
  57.8 1.4 %collective-permute-start.9 = (bf16[2,128,128]{2,1,0:T(8,128)(2,1)S(1)}, bf16[2,128,128]{2,1,0:T(8,128)(2,1)S(1)}, u32[]{:S(2)}, u32[]{:S(2)}) collective-permute-start(bf16[2,128,128]{2,1,0:T(8,128)(2,1)S(1)} %attend_part.2.refs_0_), channel_id=1, source_target_pairs={{0,2},{1,3},{2,0},{3,1},{4,6},{5,7},{6,4},{7,5},{8,10},{9,11},{10,... | collective-permute-start | bytes 196616 | tf_op jit(solution)/shard_map/ppermute | solution.py:507
  59.3 0.8 collective-permute-start.8
  60.1 5.9 %collective-permute-done.12.refs_3_ = bf16[128,384]{1,0:T(8,128)(2,1)S(1)} collective-permute-done((bf16[128,384]{1,0:T(8,128)(2,1)S(1)}, bf16[128,384]{1,0:T(8,128)(2,1)S(1)}, u32[]{:S(2)}, u32[]{:S(2)}) %collective-permute-start.12) | collective-permute-done | bytes 98336 | tf_op jit(solution)/shard_map/ppermute | solution.py:507
  66.0 0.8 attend_part.3.refs_4_
  66.8 1.9 %collective-permute-start.15 = (bf16[2,128,128]{2,1,0:T(8,128)(2,1)S(1)}, bf16[2,128,128]{2,1,0:T(8,128)(2,1)S(1)}, u32[]{:S(2)}, u32[]{:S(2)}) collective-permute-start(bf16[2,128,128]{2,1,0:T(8,128)(2,1)S(1)} %attend_part.3.refs_4_), channel_id=1, source_target_pairs={{0,3},{1,2},{2,1},{3,0},{4,7},{5,6},{6,5},{7,4},{8,11},{9,10},{10,... | collective-permute-start | bytes 196616 | tf_op jit(solution)/shard_map/ppermute | solution.py:507
  68.7 1.7 %collective-permute-start.13 = (bf16[2,128,128]{2,1,0:T(8,128)(2,1)S(1)}, bf16[2,128,128]{2,1,0:T(8,128)(2,1)S(1)}, u32[]{:S(2)}, u32[]{:S(2)}) collective-permute-start(bf16[2,128,128]{2,1,0:T(8,128)(2,1)S(1)} %attend_part.3.refs_4_), channel_id=1, source_target_pairs={{0,1},{1,0},{2,3},{3,2},{4,5},{5,4},{6,7},{7,6},{8,9},{9,8},{10,11... | collective-permute-start | bytes 196616 | tf_op jit(solution)/shard_map/ppermute | solution.py:507
  70.5 1.7 %collective-permute-done.15.refs_7_ = bf16[2,128,128]{2,1,0:T(8,128)(2,1)S(1)} collective-permute-done((bf16[2,128,128]{2,1,0:T(8,128)(2,1)S(1)}, bf16[2,128,128]{2,1,0:T(8,128)(2,1)S(1)}, u32[]{:S(2)}, u32[]{:S(2)}) %collective-permute-start.15) | collective-permute-done | bytes 65568 | tf_op jit(solution)/shard_map/ppermute | solution.py:507
  72.2 2.3 %collective-permute-done.14.refs_6_ = bf16[2,128,128]{2,1,0:T(8,128)(2,1)S(1)} collective-permute-done((bf16[2,128,128]{2,1,0:T(8,128)(2,1)S(1)}, bf16[2,128,128]{2,1,0:T(8,128)(2,1)S(1)}, u32[]{:S(2)}, u32[]{:S(2)}) %collective-permute-start.14) | collective-permute-done | bytes 65568 | tf_op jit(solution)/shard_map/ppermute | solution.py:507
  74.4 0.5 collective-permute-done.13.refs_5_
  74.9 1.0 %out_part.1 = (f32[128,640]{1,0:T(8,128)S(1)}, bf16[128,640]{1,0:T(8,128)(2,1)S(1)}) custom-call(s32[1]{0:T(128)S(6)} %select_n.18.core.half, s32[1]{0:T(128)} %bitcast.2.mine, bf16[2,128,128]{2,1,0:T(8,128)(2,1)S(1)} %attend_part.2.refs_0_, bf16[2,128,128]{2,1,0:T(8,128)(2,1)S(1)} %collective-permute-done.8.refs_1_, ...), custom_call_target="tpu_custom_call" | custom-call | tf_op jit(solution)/shard_map/out_part/pallas_call | solution.py:460
  75.9 4.4 %collective-permute-start.16 = (bf16[128,640]{1,0:T(8,128)(2,1)S(1)}, bf16[128,640]{1,0:T(8,128)(2,1)S(1)}, u32[]{:S(2)}, u32[]{:S(2)}) collective-permute-start(bf16[128,640]{1,0:T(8,128)(2,1)S(1)} %get-tuple-element.51), channel_id=1, source_target_pairs={{0,8},{8,0},{16,24},{24,16},{1,9},{9,1},{17,25},{25,17},{2,10},{10... | collective-permute-start | bytes 491528 | tf_op jit(solution)/shard_map/ppermute | solution.py:507
  80.3 1.0 %collective-permute-done.16 = bf16[128,640]{1,0:T(8,128)(2,1)S(1)} collective-permute-done((bf16[128,640]{1,0:T(8,128)(2,1)S(1)}, bf16[128,640]{1,0:T(8,128)(2,1)S(1)}, u32[]{:S(2)}, u32[]{:S(2)}) %collective-permute-start.16) | collective-permute-done | bytes 163872 | tf_op jit(solution)/shard_map/ppermute | solution.py:507
  81.4 2.2 %collective-permute-start.19 = (bf16[128,640]{1,0:T(8,128)(2,1)S(1)}, bf16[128,640]{1,0:T(8,128)(2,1)S(1)}, u32[]{:S(2)}, u32[]{:S(2)}) collective-permute-start(bf16[128,640]{1,0:T(8,128)(2,1)S(1)} %add_convert_fusion), channel_id=1, source_target_pairs={{0,20},{4,16},{8,28},{12,24},{16,4},{20,0},{24,12},{28,8},{1,21},{... | collective-permute-start | bytes 491528 | tf_op jit(solution)/shard_map/ppermute | solution.py:572
  83.5 0.2 collective-permute-start.18
  83.8 0.3 collective-permute-start.17
  84.1 3.7 %collective-permute-done.19 = bf16[128,640]{1,0:T(8,128)(2,1)S(1)} collective-permute-done((bf16[128,640]{1,0:T(8,128)(2,1)S(1)}, bf16[128,640]{1,0:T(8,128)(2,1)S(1)}, u32[]{:S(2)}, u32[]{:S(2)}) %collective-permute-start.19) | collective-permute-done | bytes 163872 | tf_op jit(solution)/shard_map/ppermute | solution.py:572
  87.8 4.2 %collective-permute-done.18 = bf16[128,640]{1,0:T(8,128)(2,1)S(1)} collective-permute-done((bf16[128,640]{1,0:T(8,128)(2,1)S(1)}, bf16[128,640]{1,0:T(8,128)(2,1)S(1)}, u32[]{:S(2)}, u32[]{:S(2)}) %collective-permute-start.18) | collective-permute-done | bytes 163872 | tf_op jit(solution)/shard_map/ppermute | solution.py:507
  92.0 0.1 multiply_convert_fusion.rows
  92.1 0.6 collective-permute-start.20
  92.7 0.3 copy.17
  92.9 2.1 %grad_part.2.refs_0_ = bf16[2048,1280]{1,0:T(8,128)(2,1)} custom-call(s32[1]{0:T(128)S(6)} %select_n.18.core.half, bf16[2048,128]{1,0:T(8,128)(2,1)S(1)} %bitcast.9, bf16[128,640]{1,0:T(8,128)(2,1)S(1)} %multiply_convert_fusion.rows), custom_call_target="tpu_custom_call" | custom-call | tf_op jit(solution)/shard_map/grad_part/pallas_call | solution.py:496
  95.0 2.0 %grad_part.3 = bf16[2048,1280]{1,0:T(8,128)(2,1)} custom-call(s32[1]{0:T(128)S(6)} %sub.3.half, bf16[2048,128]{1,0:T(8,128)(2,1)S(1)} %bitcast.10, bf16[128,640]{1,0:T(8,128)(2,1)S(1)} %collective-permute-done.20.rows, bf16[2048,1280]{1,0:T(8,128)(2,1)} %grad_part.2.refs_0_), custom_call_target="tpu_custom_call", output_to_operand_aliasing={{}: (3, {})} | custom-call | tf_op jit(solution)/shard_map/grad_part/pallas_call | solution.py:496
  (34 shorter events, 0.2 us)
Async XLA Ops:
  0.6 8.4 %copy-start = (bf16[256,1280]{1,0:T(8,128)(2,1)S(1)}, bf16[256,1280]{1,0:T(8,128)(2,1)}, u32[]{:S(2)}) copy-start(bf16[256,1280]{1,0:T(8,128)(2,1)} %time_w.3) | copy-start | bytes 1966084
  0.6 8.4 %copy-start.1 = (bf16[256,3,1280]{2,0,1:T(8,128)(2,1)S(1)}, bf16[256,3,1280]{2,0,1:T(8,128)(2,1)}, u32[]{:S(2)}) copy-start(bf16[256,3,1280]{2,0,1:T(8,128)(2,1)} %param.22) | copy-start | bytes 5898244
  0.7 8.4 %copy-start.2 = (bf16[256,3,1280]{2,0,1:T(8,128)(2,1)S(1)}, bf16[256,3,1280]{2,0,1:T(8,128)(2,1)}, u32[]{:S(2)}) copy-start(bf16[256,3,1280]{2,0,1:T(8,128)(2,1)} %param.26) | copy-start | bytes 5898244
  2.2 6.9 %copy-start.13 = (bf16[8,256]{1,0:T(8,128)(2,1)S(1)}, bf16[8,256]{1,0:T(8,128)(2,1)}, u32[]{:S(2)}) copy-start(bf16[8,256]{1,0:T(8,128)(2,1)} %fusion.2.embed) | copy-start | bytes 12292
  2.2 14.1 %copy-start.15 = (s32[3]{0:T(128)S(1)}, s32[3]{0:T(128)}, u32[]{:S(2)}) copy-start(s32[3]{0:T(128)} %param.19) | copy-start | bytes 40
  2.2 15.2 %copy-start.4 = (bf16[64,1280]{1,0:T(8,128)(2,1)S(1)}, bf16[64,1280]{1,0:T(8,128)(2,1)}, u32[]{:S(2)}) copy-start(bf16[64,1280]{1,0:T(8,128)(2,1)} %noise.3) | copy-start | bytes 491524
  7.0 8.0 %collective-permute-start = (bf16[192,640]{1,0:T(8,128)(2,1)}, bf16[192,640]{1,0:T(8,128)(2,1)S(1)}, u32[]{:S(2)}, u32[]{:S(2)}) collective-permute-start(bf16[192,640]{1,0:T(8,128)(2,1)} %get-tuple-element.28), channel_id=1, source_target_pairs={{0,4},{4,0},{1,5},{5,1},{2,6},{6,2},{3,7},{7,3},{8,12},{12,8},{9,1... | collective-permute-start | bytes 737288 | tf_op jit(solution)/shard_map/ppermute | solution.py:507
  9.1 1.0 %copy-start.3 = (f32[128,640]{1,0:T(8,128)S(1)}, f32[128,640]{1,0:T(8,128)}, u32[]{:S(2)}) copy-start(f32[128,640]{1,0:T(8,128)} %get-tuple-element.27.after.full) | copy-start | bytes 983044
  15.0 2.4 %collective-permute-start.1 = (bf16[192,640]{1,0:T(8,128)(2,1)S(1)}, bf16[192,640]{1,0:T(8,128)(2,1)S(1)}, u32[]{:S(2)}, u32[]{:S(2)}) collective-permute-start(bf16[192,640]{1,0:T(8,128)(2,1)S(1)} %join_part.1.joined), channel_id=1, source_target_pairs={{0,8},{8,0},{16,24},{24,16},{1,9},{9,1},{17,25},{25,17},{2,10},{10... | collective-permute-start | bytes 737288 | tf_op jit(solution)/shard_map/ppermute | solution.py:507
  23.8 0.7 copy-start.5
  24.5 0.7 copy-start.7
  25.1 0.7 copy-start.9
  25.8 0.7 copy-start.11
  26.5 13.8 %collective-permute-start.4 = (bf16[2,128,384]{2,1,0:T(8,128)(2,1)}, bf16[2,128,384]{2,1,0:T(8,128)(2,1)}, u32[]{:S(2)}, u32[]{:S(2)}) collective-permute-start(bf16[2,128,384]{2,1,0:T(8,128)(2,1)} %get-tuple-element.38), channel_id=1, source_target_pairs={{0,1},{1,0},{2,3},{3,2},{4,5},{5,4},{6,7},{7,6},{8,9},{9,8},{10,11... | collective-permute-start | bytes 589832 | tf_op jit(solution)/shard_map/ppermute | solution.py:507
  28.0 9.8 %collective-permute-start.2 = (bf16[2,144,384]{2,1,0:T(8,128)(2,1)}, bf16[2,144,384]{2,1,0:T(8,128)(2,1)}, u32[]{:S(2)}, u32[]{:S(2)}) collective-permute-start(bf16[2,144,384]{2,1,0:T(8,128)(2,1)} %get-tuple-element.33), channel_id=1, source_target_pairs={{0,1},{1,0},{2,3},{3,2},{4,5},{5,4},{6,7},{7,6},{8,9},{9,8},{10,11... | collective-permute-start | bytes 663560 | tf_op jit(solution)/shard_map/ppermute | solution.py:507
  38.8 6.9 %collective-permute-start.6 = (bf16[2,144,384]{2,1,0:T(8,128)(2,1)S(1)}, bf16[2,144,384]{2,1,0:T(8,128)(2,1)S(1)}, u32[]{:S(2)}, u32[]{:S(2)}) collective-permute-start(bf16[2,144,384]{2,1,0:T(8,128)(2,1)S(1)} %get-tuple-element.43), channel_id=1, source_target_pairs={{0,1},{1,0},{2,3},{3,2},{4,5},{5,4},{6,7},{7,6},{8,9},{9,8},{10,11... | collective-permute-start | bytes 663560 | tf_op jit(solution)/shard_map/ppermute | solution.py:507
  40.3 0.9 copy-start.10
  41.2 0.9 copy-start.12
  42.1 50.5 %copy-start.14 = (bf16[128,2048]{1,0:T(8,128)(2,1)S(1)}, bf16[128,2048]{1,0:T(8,128)(2,1)}, u32[]{:S(2)}) copy-start(bf16[128,2048]{1,0:T(8,128)(2,1)} %heads.1) | copy-start | bytes 1572868
  43.2 11.4 %collective-permute-start.7 = (bf16[2,128,384]{2,1,0:T(8,128)(2,1)S(1)}, bf16[2,128,384]{2,1,0:T(8,128)(2,1)S(1)}, u32[]{:S(2)}, u32[]{:S(2)}) collective-permute-start(bf16[2,128,384]{2,1,0:T(8,128)(2,1)S(1)} %get-tuple-element.46), channel_id=1, source_target_pairs={{0,1},{1,0},{2,3},{3,2},{4,5},{5,4},{6,7},{7,6},{8,9},{9,8},{10,11... | collective-permute-start | bytes 589832 | tf_op jit(solution)/shard_map/ppermute | solution.py:507
  43.4 12.3 %collective-permute-start.3 = (bf16[144,384]{1,0:T(8,128)(2,1)S(1)}, bf16[144,384]{1,0:T(8,128)(2,1)S(1)}, u32[]{:S(2)}, u32[]{:S(2)}) collective-permute-start(bf16[144,384]{1,0:T(8,128)(2,1)S(1)} %get-tuple-element.36), channel_id=1, source_target_pairs={{0,2},{1,3},{2,0},{3,1},{4,6},{5,7},{6,4},{7,5},{8,10},{9,11},{10,... | collective-permute-start | bytes 331784 | tf_op jit(solution)/shard_map/ppermute | solution.py:507
  45.7 9.9 %collective-permute-start.5 = (bf16[128,384]{1,0:T(8,128)(2,1)S(1)}, bf16[128,384]{1,0:T(8,128)(2,1)S(1)}, u32[]{:S(2)}, u32[]{:S(2)}) collective-permute-start(bf16[128,384]{1,0:T(8,128)(2,1)S(1)} %get-tuple-element.41), channel_id=1, source_target_pairs={{0,2},{1,3},{2,0},{3,1},{4,6},{5,7},{6,4},{7,5},{8,10},{9,11},{10,... | collective-permute-start | bytes 294920 | tf_op jit(solution)/shard_map/ppermute | solution.py:507
  45.8 0.9 copy-start.6
  46.8 19.3 %collective-permute-start.11 = (bf16[144,384]{1,0:T(8,128)(2,1)S(1)}, bf16[144,384]{1,0:T(8,128)(2,1)S(1)}, u32[]{:S(2)}, u32[]{:S(2)}) collective-permute-start(bf16[144,384]{1,0:T(8,128)(2,1)S(1)} %get-tuple-element.44.refs_5_), channel_id=1, source_target_pairs={{0,2},{1,3},{2,0},{3,1},{4,6},{5,7},{6,4},{7,5},{8,10},{9,11},{10,... | collective-permute-start | bytes 331784 | tf_op jit(solution)/shard_map/ppermute | solution.py:507
  54.6 0.9 copy-start.8
  55.6 10.5 %collective-permute-start.12 = (bf16[128,384]{1,0:T(8,128)(2,1)S(1)}, bf16[128,384]{1,0:T(8,128)(2,1)S(1)}, u32[]{:S(2)}, u32[]{:S(2)}) collective-permute-start(bf16[128,384]{1,0:T(8,128)(2,1)S(1)} %get-tuple-element.47.refs_6_), channel_id=1, source_target_pairs={{0,2},{1,3},{2,0},{3,1},{4,6},{5,7},{6,4},{7,5},{8,10},{9,11},{10,... | collective-permute-start | bytes 294920 | tf_op jit(solution)/shard_map/ppermute | solution.py:507
  56.5 12.2 %collective-permute-start.10 = (bf16[2,128,128]{2,1,0:T(8,128)(2,1)S(1)}, bf16[2,128,128]{2,1,0:T(8,128)(2,1)S(1)}, u32[]{:S(2)}, u32[]{:S(2)}) collective-permute-start(bf16[2,128,128]{2,1,0:T(8,128)(2,1)S(1)} %attend_part.2.refs_0_), channel_id=1, source_target_pairs={{0,3},{1,2},{2,1},{3,0},{4,7},{5,6},{6,5},{7,4},{8,11},{9,10},{10,... | collective-permute-start | bytes 196616 | tf_op jit(solution)/shard_map/ppermute | solution.py:507
  57.8 12.6 %collective-permute-start.9 = (bf16[2,128,128]{2,1,0:T(8,128)(2,1)S(1)}, bf16[2,128,128]{2,1,0:T(8,128)(2,1)S(1)}, u32[]{:S(2)}, u32[]{:S(2)}) collective-permute-start(bf16[2,128,128]{2,1,0:T(8,128)(2,1)S(1)} %attend_part.2.refs_0_), channel_id=1, source_target_pairs={{0,2},{1,3},{2,0},{3,1},{4,6},{5,7},{6,4},{7,5},{8,10},{9,11},{10,... | collective-permute-start | bytes 196616 | tf_op jit(solution)/shard_map/ppermute | solution.py:507
  59.3 11.2 %collective-permute-start.8 = (bf16[2,128,128]{2,1,0:T(8,128)(2,1)S(1)}, bf16[2,128,128]{2,1,0:T(8,128)(2,1)S(1)}, u32[]{:S(2)}, u32[]{:S(2)}) collective-permute-start(bf16[2,128,128]{2,1,0:T(8,128)(2,1)S(1)} %attend_part.2.refs_0_), channel_id=1, source_target_pairs={{0,1},{1,0},{2,3},{3,2},{4,5},{5,4},{6,7},{7,6},{8,9},{9,8},{10,11... | collective-permute-start | bytes 196616 | tf_op jit(solution)/shard_map/ppermute | solution.py:507
  66.8 5.3 %collective-permute-start.15 = (bf16[2,128,128]{2,1,0:T(8,128)(2,1)S(1)}, bf16[2,128,128]{2,1,0:T(8,128)(2,1)S(1)}, u32[]{:S(2)}, u32[]{:S(2)}) collective-permute-start(bf16[2,128,128]{2,1,0:T(8,128)(2,1)S(1)} %attend_part.3.refs_4_), channel_id=1, source_target_pairs={{0,3},{1,2},{2,1},{3,0},{4,7},{5,6},{6,5},{7,4},{8,11},{9,10},{10,... | collective-permute-start | bytes 196616 | tf_op jit(solution)/shard_map/ppermute | solution.py:507
  68.7 5.7 %collective-permute-start.14 = (bf16[2,128,128]{2,1,0:T(8,128)(2,1)S(1)}, bf16[2,128,128]{2,1,0:T(8,128)(2,1)S(1)}, u32[]{:S(2)}, u32[]{:S(2)}) collective-permute-start(bf16[2,128,128]{2,1,0:T(8,128)(2,1)S(1)} %attend_part.3.refs_4_), channel_id=1, source_target_pairs={{0,2},{1,3},{2,0},{3,1},{4,6},{5,7},{6,4},{7,5},{8,10},{9,11},{10,... | collective-permute-start | bytes 196616 | tf_op jit(solution)/shard_map/ppermute | solution.py:507
  68.7 6.2 %collective-permute-start.13 = (bf16[2,128,128]{2,1,0:T(8,128)(2,1)S(1)}, bf16[2,128,128]{2,1,0:T(8,128)(2,1)S(1)}, u32[]{:S(2)}, u32[]{:S(2)}) collective-permute-start(bf16[2,128,128]{2,1,0:T(8,128)(2,1)S(1)} %attend_part.3.refs_4_), channel_id=1, source_target_pairs={{0,1},{1,0},{2,3},{3,2},{4,5},{5,4},{6,7},{7,6},{8,9},{9,8},{10,11... | collective-permute-start | bytes 196616 | tf_op jit(solution)/shard_map/ppermute | solution.py:507
  75.9 5.4 %collective-permute-start.16 = (bf16[128,640]{1,0:T(8,128)(2,1)S(1)}, bf16[128,640]{1,0:T(8,128)(2,1)S(1)}, u32[]{:S(2)}, u32[]{:S(2)}) collective-permute-start(bf16[128,640]{1,0:T(8,128)(2,1)S(1)} %get-tuple-element.51), channel_id=1, source_target_pairs={{0,8},{8,0},{16,24},{24,16},{1,9},{9,1},{17,25},{25,17},{2,10},{10... | collective-permute-start | bytes 491528 | tf_op jit(solution)/shard_map/ppermute | solution.py:507
  81.4 6.4 %collective-permute-start.19 = (bf16[128,640]{1,0:T(8,128)(2,1)S(1)}, bf16[128,640]{1,0:T(8,128)(2,1)S(1)}, u32[]{:S(2)}, u32[]{:S(2)}) collective-permute-start(bf16[128,640]{1,0:T(8,128)(2,1)S(1)} %add_convert_fusion), channel_id=1, source_target_pairs={{0,20},{4,16},{8,28},{12,24},{16,4},{20,0},{24,12},{28,8},{1,21},{... | collective-permute-start | bytes 491528 | tf_op jit(solution)/shard_map/ppermute | solution.py:572
  83.5 8.4 %collective-permute-start.18 = (bf16[128,640]{1,0:T(8,128)(2,1)S(1)}, bf16[128,640]{1,0:T(8,128)(2,1)S(1)}, u32[]{:S(2)}, u32[]{:S(2)}) collective-permute-start(bf16[128,640]{1,0:T(8,128)(2,1)S(1)} %add_convert_fusion), channel_id=1, source_target_pairs={{0,16},{8,24},{16,0},{24,8},{1,17},{9,25},{17,1},{25,9},{2,18},{10... | collective-permute-start | bytes 491528 | tf_op jit(solution)/shard_map/ppermute | solution.py:507
  83.8 8.2 %collective-permute-start.17 = (bf16[128,640]{1,0:T(8,128)(2,1)S(1)}, bf16[128,640]{1,0:T(8,128)(2,1)S(1)}, u32[]{:S(2)}, u32[]{:S(2)}) collective-permute-start(bf16[128,640]{1,0:T(8,128)(2,1)S(1)} %add_convert_fusion), channel_id=1, source_target_pairs={{0,4},{4,0},{1,5},{5,1},{2,6},{6,2},{3,7},{7,3},{8,12},{12,8},{9,1... | collective-permute-start | bytes 491528 | tf_op jit(solution)/shard_map/ppermute | solution.py:507
  92.1 2.9 %collective-permute-start.20 = (bf16[128,640]{1,0:T(8,128)(2,1)S(1)}, bf16[128,640]{1,0:T(8,128)(2,1)S(1)}, u32[]{:S(2)}, u32[]{:S(2)}) collective-permute-start(bf16[128,640]{1,0:T(8,128)(2,1)S(1)} %multiply_convert_fusion.rows), channel_id=1, source_target_pairs={{0,8},{8,0},{16,24},{24,16},{1,9},{9,1},{17,25},{25,17},{2,10},{10... | collective-permute-start | bytes 491528 | tf_op jit(solution)/shard_map/ppermute | solution.py:507

commit v5 on v3

--- a/solution.py
+++ b/solution.py
@@ -160,7 +160,7 @@
     return pl.CostEstimate(flops=flops, bytes_accessed=moved, transcendentals=0)
 
 
-GEN_CUTS = 4
+GEN_CUTS = 8
 
 
 def gen_kernel(seq, core, embed, heads, weight, time_w, resid, noise, full, sent, heads_v, weight_v, time_v, resid_v, sems):
@@ -241,7 +241,7 @@
     )(embed, time_a, time_b, time_w, after)
 
 
-def join_kernel(full, arrived, after, joined):
+def join_kernel(full, arrived, after_a, after_b, after_c, joined):
     length = full.shape[0]
     own = arrived.shape[0] - length
     top = full[...] + arrived[pl.ds(0, length), :].astype(jnp.float32)
@@ -249,18 +249,18 @@
     joined[pl.ds(length, own), :] = arrived[pl.ds(length, own), :]
 
 
-def join_part(full, arrived, after):
+def join_part(full, arrived, *after):
     return pl.pallas_call(
         join_kernel,
-        in_specs=[vmem_spec(), vmem_spec(), any_spec()],
+        in_specs=[vmem_spec(), vmem_spec()] + [any_spec()] * 3,
         out_specs=vmem_spec(),
         out_shape=jax.ShapeDtypeStruct(arrived.shape, jnp.bfloat16),
         compiler_params=params(8),
         name="join_part",
-    )(full, arrived, after)
-
-
-def project(index, mine, noisy, squares, mods, weight, copies, kept, sent, result):
+    )(full, arrived, *after)
+
+
+def project(index, mine, noisy, squares, mods, weight, kept, sent, result):
     tokens = noisy.shape[0]
     length = tokens // 2
     unit = squares.shape[1] // 2
@@ -274,7 +274,6 @@
     rows = jnp.concatenate([top, low, extra], axis=0).astype(jnp.bfloat16)
     row_id = lax.broadcasted_iota(jnp.int32, (EXTRA_ROWS, unit), 0)
     for part in range(3):
-        copies[part].wait()
         result[...] = dot32(rows, weight[part])
         cols = pl.ds(part * unit, unit)
         for slot in range(groups):
@@ -290,23 +289,8 @@
             goal[0][slot // 2, pl.ds(length, EXTRA_ROWS), cols] = tail.astype(jnp.bfloat16)
 
 
-def weight_copies(role, planes, weight, sems):
-    cols = at_block(role[0], weight.shape[3])
-    copies = [
-        [
-            pltpu.make_async_copy(planes[index].at[part, :, cols], weight.at[index, part], sems.at[3 * index + part])
-            for part in range(3)
-        ]
-        for index in range(2)
-    ]
-    for copy in copies[0] + copies[1]:
-        copy.start()
-    return copies
-
-
-def qkv_kernel(role, seq, core, mine, levels, joined, swapped, noise, mods, planes_a, planes_b, latent, *refs):
-    chunks, (values, noises, result, weight, sems) = refs[:8], refs[8:]
-    copies = weight_copies(role, (planes_a, planes_b), weight, sems)
+def qkv_kernel(seq, core, mine, levels, joined, swapped, noise, mods, weight_a, weight_b, latent, *refs):
+    chunks, (values, noises, result) = refs[:8], refs[8:]
     length, cols = values.shape[0], joined.shape[1]
     own = latent.shape[0]
     tokens = 2 * length
@@ -326,9 +310,9 @@
     wide = mixed.astype(jnp.float32)
     sums = jnp.sum(wide * wide, axis=1, keepdims=True)
     sums = jnp.broadcast_to(sums, (tokens, length)).T[0:8]
-    for index in range(2):
+    for index, weight in enumerate((weight_a, weight_b)):
         kept, sent = chunks[4 * index : 4 * index + 2], chunks[4 * index + 2 : 4 * index + 4]
-        project(index, mine[0], mixed, sums, mods, weight.at[index], copies[index], kept, sent, result)
+        project(index, mine[0], mixed, sums, mods, weight, kept, sent, result)
 
 
 def chunk_shapes(length, cols):
@@ -339,49 +323,27 @@
     return shapes * 2
 
 
-def qkv_part(role, seq, core, mine, levels, joined, swapped, noise, mods, planes_a, planes_b, cols):
+def qkv_part(seq, core, mine, levels, joined, swapped, noise, mods, weight_a, weight_b):
     own, width = noise.shape
     length = joined.shape[0] - own
     tokens = 2 * length
+    cols = weight_a.shape[2]
     return pl.pallas_call(
         qkv_kernel,
-        in_specs=[smem_spec()] * 5 + [vmem_spec()] * 4 + [hbm_spec()] * 2,
+        in_specs=[smem_spec()] * 4 + [vmem_spec()] * 6,
         out_specs=[vmem_spec()] * 9,
         out_shape=[jax.ShapeDtypeStruct((own, width), jnp.bfloat16)] + chunk_shapes(length, cols) * 2,
         scratch_shapes=[
             pltpu.VMEM((length, width), jnp.bfloat16),
             pltpu.VMEM((length, width), jnp.bfloat16),
             pltpu.VMEM((tokens + EXTRA_ROWS, cols), jnp.float32),
-            pltpu.VMEM((2, 3, width, cols), jnp.bfloat16),
-            pltpu.SemaphoreType.DMA((6,)),
         ],
-        compiler_params=params(48),
+        compiler_params=params(24),
         name="qkv_part",
-    )(role, seq, core, mine, levels, joined, swapped, noise, mods, planes_a, planes_b)
-
-
-def add_kernel(mine, theirs, *refs):
-    kept, sent = refs[-3:-1] if len(refs) > 2 else refs
-    kept[...] = mine[0].astype(jnp.float32) + theirs[0].astype(jnp.float32)
-    sent[...] = (mine[1].astype(jnp.float32) + theirs[1].astype(jnp.float32)).astype(jnp.bfloat16)
-
-
-def add_part(mine, theirs, later=None):
-    rest = [] if later is None else [later]
-    shape = mine.shape[1:]
-    return pl.pallas_call(
-        add_kernel,
-        in_specs=[vmem_spec()] * 2 + [any_spec()] * len(rest),
-        out_specs=[vmem_spec()] * 2 + [any_spec()] * len(rest),
-        out_shape=[jax.ShapeDtypeStruct(shape, jnp.float32), jax.ShapeDtypeStruct(shape, jnp.bfloat16)]
-        + [jax.ShapeDtypeStruct(x.shape, x.dtype) for x in rest],
-        input_output_aliases={2: 2} if rest else {},
-        compiler_params=params(8),
-        name="add_part",
-    )(mine, theirs, *rest)
-
-
-def attend_kernel(width, kept_a, other_a, kept_b, other_b, gains, after, out):
+    )(seq, core, mine, levels, joined, swapped, noise, mods, weight_a, weight_b)
+
+
+def attend_kernel(width, kept_a, other_a, kept_b, other_b, gains, out):
     _, length, unit = out.shape
     extra = None
     for level, (kept, other) in enumerate(((kept_a, other_a), (kept_b, other_b))):
@@ -410,18 +372,18 @@
         out[level] = dot32(probs, value).astype(jnp.bfloat16)
 
 
-def attend_part(chunks, gains, after, width):
+def attend_part(chunks, gains, width):
     kept_a, kept_b = chunks[0][0], chunks[1][0]
     unit = kept_a.shape[1] // 3
     length = kept_a.shape[0] - EXTRA_ROWS
     return pl.pallas_call(
         lambda *refs: attend_kernel(width, *refs),
-        in_specs=[vmem_spec()] * 5 + [any_spec()],
+        in_specs=[vmem_spec()] * 5,
         out_specs=vmem_spec(),
         out_shape=jax.ShapeDtypeStruct((2, length, unit), jnp.bfloat16),
         compiler_params=params(8),
         name="attend_part",
-    )(kept_a, chunks[0][1], kept_b, chunks[1][1], gains, after)
+    )(kept_a, chunks[0][1], kept_b, chunks[1][1], gains)
 
 
 def out_kernel(core, mine, *refs):
@@ -523,8 +485,8 @@
     role, seq, mp = lax.axis_index("role"), lax.axis_index("seq"), lax.axis_index("mp")
     part_cols = gen_heads.shape[1] // roles
     freq = gen_time_w.shape[0]
-    role_at, seq_at, mine = [v.astype(jnp.int32).reshape(1) for v in (role, seq, mp)]
-    core = role_at % 2
+    seq_at, mine = [v.astype(jnp.int32).reshape(1) for v in (seq, mp)]
+    core = (role % 2).astype(jnp.int32).reshape(1)
     half_cols = gen_resid.shape[1] // 2
 
     embed = jax.vmap(lambda t: time_embed(t, freq))(steps)
@@ -534,25 +496,31 @@
     arrived = exchange(sent, "seq", 1)
     planes = [w.transpose(1, 0, 2) for w in (teacher_qkv, critic_qkv, teacher_time, critic_time)]
     mods, gate = mod_part(embed, planes[2], planes[3], gen_time_w, full)
-    joined = join_part(full, arrived, gate)
+    start = role * part_cols
+    later, _ = lax.optimization_barrier((start, full))
+    weight_a, weight_b = [lax.dynamic_slice_in_dim(w, later, part_cols, axis=2) for w in planes[:2]]
+    joined = join_part(full, arrived, gate, weight_a, weight_b)
     swapped = exchange(joined, "role", 1)
-    start = role * part_cols
+    unit = part_cols // groups
+
+    latent, *chunks = qkv_part(seq_at, core, mine, levels, joined, swapped, noise, mods, weight_a, weight_b)
+    first, second = chunks[:4], chunks[4:]
+    arrivals = [exchange(send, "mp", 1) for send in first[2:]]
     out_a, out_b = [lax.dynamic_slice_in_dim(w, start, part_cols, axis=0) for w in (teacher_out, critic_out)]
-    unit = part_cols // groups
     gains = [lax.dynamic_slice_in_dim(g, start + mp * unit, unit, axis=1) for g in (teacher_norm, critic_norm)]
-
-    latent, *chunks = qkv_part(
-        role_at, seq_at, core, mine, levels, joined, swapped, noise, mods, planes[0], planes[1], part_cols
-    )
-    first, second = chunks[:4], chunks[4:]
-    kept_a, send_a, third = add_part(first[0], exchange(first[2], "mp", 1), second[2])
-    kept_b, send_b, last = add_part(first[1], exchange(first[3], "mp", 1), second[3])
-    kept_c, send_c = add_part(second[0], exchange(third, "mp", 1))
-    kept_d, send_d = add_part(second[1], exchange(last, "mp", 1))
-    sums = [(kept, exchange(send, "mp", 2)) for kept, send in ((kept_a, send_a), (kept_b, send_b))]
-    head_a = attend_part(sums, gains[0], out_a, D)
-    sums = [(kept, exchange(send, "mp", 2)) for kept, send in ((kept_c, send_c), (kept_d, send_d))]
-    head_b = attend_part(sums, gains[1], out_b, D)
+    arrivals[0], out_a, out_b, *gains = lax.optimization_barrier((arrivals[0], out_a, out_b, *gains))
+    third, arrivals[0] = lax.optimization_barrier((second[2], arrivals[0]))
+    last, arrivals[1] = lax.optimization_barrier((second[3], arrivals[1]))
+    arrivals += [exchange(third, "mp", 1), exchange(last, "mp", 1)]
+    kept, sends = [], []
+    for mine_rows, theirs in zip(first[:2] + second[:2], arrivals):
+        summed = both(mine_rows, theirs)
+        kept.append(summed[0])
+        sends.append(summed[1].astype(jnp.bfloat16))
+    pieces = [(rows, exchange(send, "mp", 2)) for rows, send in zip(kept, sends)]
+    kept_b, _, _ = lax.optimization_barrier((pieces[1][0], sends[2], sends[3]))
+    head_a = attend_part((pieces[0], (kept_b, pieces[1][1])), gains[0], D)
+    head_b = attend_part(pieces[2:], gains[1], D)
     gathered = [[head] + [exchange(head, "mp", bits) for bits in range(1, groups)] for head in (head_a, head_b)]
 
     kept, sent = out_part(core, mine, *gathered, out_a, out_b, mods)

time: 95.6 us -> 104 us (1.088)
  local copies, waits for them, and re-layouts: 8.63 us -> 18.9 us
  waiting for transfers between devices: 37.9 us -> 34.3 us
  Pallas kernels: 19.1 us -> 17.2 us
  starting transfers between devices: 27 us -> 28.9 us
  other arithmetic: 1.74 us -> 3.63 us
    dynamic_slice x0 -> x1, local copies, waits for them, and re-layouts: none -> 8.94 us  [heads_per_role(): lax.dynamic_slice_in_dim(w, later, part_cols, axis=2)]
    ppermute x20, waiting for transfers between devices: 35 us -> 30.6 us  [exchange(): lax.ppermute(array, axis, [(i, i ^ bit) for i in range(lax.axis_size(axis...]
    unnamed x33 -> x31, local copies, waits for them, and re-layouts: 4.4 us -> 7.27 us
    ppermute x20, starting transfers between devices: 24.8 us -> 27.5 us  [exchange(): lax.ppermute(array, axis, [(i, i ^ bit) for i in range(lax.axis_size(axis...]
    pallas_call x6 -> x2, Pallas kernels: 7.59 us -> 5.23 us  [the longest x1 3.86 us: qkv_part(): pl.pallas_call(qkv_kernel, in_specs=[smem_spec()] * 4 + [vmem_spec()] * 6...]
    add x0 -> x4, other arithmetic: none -> 2.04 us  [both(): return mine.astype(jnp.float32) + theirs.astype(jnp.float32)]
    dynamic_slice x2 -> x1, local copies, waits for them, and re-layouts: 2.8 us -> 1.88 us  [heads_per_role(): lax.dynamic_slice_in_dim(w, start, part_cols, axis=0)]
  transfers between devices with their start and end apart: 21 -> 21, of which waited for: 13 -> 10; matrix products, arithmetic and copies ran while one was open for 5% -> 15% of each run, Pallas kernels for 6% -> 4%
where the time goes in v5:
time: 104 us
  waiting for transfers between devices  34.3 us (33%)
  starting transfers between devices  28.9 us (28%)
  local copies, waits for them, and re-layouts  18.9 us (18%)
  Pallas kernels  17.2 us (17%)
  other arithmetic  3.63 us (3%)
    ppermute x20, waiting for transfers between devices, exchange(): lax.ppermute(array, axis, [(i, i ^ bit) for i in range(lax.axis_size(axis...  30.6 us
    ppermute x20, starting transfers between devices, exchange(): lax.ppermute(array, axis, [(i, i ^ bit) for i in range(lax.axis_size(axis...  27.5 us
    dynamic_slice x1, local copies, waits for them, and re-layouts, heads_per_role(): lax.dynamic_slice_in_dim(w, later, part_cols, axis=2)  8.94 us
    unnamed x31, local copies, waits for them, and re-layouts  7.27 us
    pallas_call x1, Pallas kernels, gen_part(): pl.pallas_call(gen_kernel, in_specs=[smem_spec(), smem_spec(), vmem_spec(...  4.64 us
    pallas_call x2, Pallas kernels, grad_part(): pl.pallas_call(grad_kernel, grid_spec=grid_spec, out_shape=jax.ShapeDtype...  4.09 us
    pallas_call x1, Pallas kernels, qkv_part(): pl.pallas_call(qkv_kernel, in_specs=[smem_spec()] * 4 + [vmem_spec()] * 6...  3.86 us
    ppermute x1, waiting for transfers between devices, heads_per_role(): lax.ppermute(total, ('role', 'seq'), [(i, i ^ 2 * lax.axis_size('seq') +...  3.69 us
  transfers between devices with their start and end apart: 21, of which 10 were waited for; matrix products, arithmetic and copies ran while one was open for 15% of the time, Pallas kernels for 4%

profile of v5, /device:TPU:1, one launch (start us, length us, event | category | flops | bytes accessed | tf_op | source)
XLA Modules:
  0.0 103.9 jit_solution(298441746435474256)
XLA Ops:
  0.7 0.7 convert_element_type.69
  1.3 0.1 fusion.7
  1.4 0.6 fusion.6.embed
  2.0 4.6 %gen_part.1 = (f32[128,640]{1,0:T(8,128)}, bf16[192,640]{1,0:T(8,128)(2,1)}) custom-call(s32[1]{0:T(128)} %bitcast.seq, s32[1]{0:T(128)} %bitcast.1.core.half, bf16[8,256]{1,0:T(8,128)(2,1)} %fusion.6.embed, bf16[128,2048]{1,0:T(8,128)(2,1)} %heads.1, bf16[2048,1280]{1,0:T(8,128)(2,1)} %weight.1, bf16[256,1280]{1,0:T(8,128)(2,1)} %time_w.3, ...), custom_call_target="tpu_custom_call" | custom-call | tf_op jit(solution)/shard_map/gen_part/pallas_call | solution.py:200
  6.7 2.1 %collective-permute-start = (bf16[192,640]{1,0:T(8,128)(2,1)}, bf16[192,640]{1,0:T(8,128)(2,1)}, u32[]{:S(2)}, u32[]{:S(2)}) collective-permute-start(bf16[192,640]{1,0:T(8,128)(2,1)} %get-tuple-element.29), channel_id=1, source_target_pairs={{0,4},{4,0},{1,5},{5,1},{2,6},{6,2},{3,7},{7,3},{8,12},{12,8},{9,1... | collective-permute-start | bytes 737288 | tf_op jit(solution)/shard_map/ppermute | solution.py:460
  8.8 0.0 copy-start.10
  8.8 8.9 %dynamic-slice_bitcast_fusion = (bf16[3,1280,512]{2,1,0:T(8,128)(2,1)S(1)}, bf16[3,1280,512]{2,1,0:T(8,128)(2,1)S(1)}) fusion(bf16[1280,3,2048]{2,0,1:T(8,128)(2,1)} %param.24, s32[]{:T(128)S(6)} %select_n.23, bf16[1280,3,2048]{2,0,1:T(8,128)(2,1)} %param.20), kind=kLoop, calls=%fused_computation | loop fusion | bytes 15728644 | tf_op jit(solution)/shard_map/dynamic_slice | solution.py:501
  17.8 0.0 copy-start.2
  17.8 0.7 mod_part.1
  18.5 0.0 collective-permute-done.arrived
  18.6 1.4 %join_part.1.joined = bf16[192,640]{1,0:T(8,128)(2,1)S(1)} custom-call(f32[128,640]{1,0:T(8,128)S(1)} %copy-done.7, bf16[192,640]{1,0:T(8,128)(2,1)} %collective-permute-done.arrived, f32[8,1280]{1,0:T(8,128)S(1)} %get-tuple-element.30.after_a, bf16[3,1280,512]{2,1,0:T(8,128)(2,1)S(1)} %get-tuple-element.57.after_b.weight_a, ...), custom_call_target="tpu_custom_call" | custom-call | tf_op jit(solution)/shard_map/join_part/pallas_call | solution.py:253
  20.0 1.0 copy-done.2
  21.0 1.0 collective-permute-start.1
  21.9 0.1 convert_multiply_fusion.levels
  22.0 1.1 %collective-permute-done.1.swapped = bf16[192,640]{1,0:T(8,128)(2,1)S(1)} collective-permute-done((bf16[192,640]{1,0:T(8,128)(2,1)S(1)}, bf16[192,640]{1,0:T(8,128)(2,1)S(1)}, u32[]{:S(2)}, u32[]{:S(2)}) %collective-permute-start.1) | collective-permute-done | bytes 245792 | tf_op jit(solution)/shard_map/ppermute | solution.py:460
  23.1 2.1 %copy-done.1 = bf16[3,1280,512]{2,1,0:T(8,128)(2,1)S(1)} copy-done((bf16[3,1280,512]{2,1,0:T(8,128)(2,1)S(1)}, bf16[3,1280,512]{2,1,0:T(8,128)(2,1)}, u32[]{:S(2)}) %copy-start.1) | copy-done | bytes 3932184
  25.2 2.1 %copy-done.3 = bf16[3,1280,512]{2,1,0:T(8,128)(2,1)S(1)} copy-done((bf16[3,1280,512]{2,1,0:T(8,128)(2,1)S(1)}, bf16[3,1280,512]{2,1,0:T(8,128)(2,1)}, u32[]{:S(2)}) %copy-start.3) | copy-done | bytes 3932184
  27.3 3.9 %qkv_part.1 = (bf16[64,1280]{1,0:T(8,128)(2,1)}, bf16[2,144,384]{2,1,0:T(8,128)(2,1)S(1)}, bf16[2,128,384]{2,1,0:T(8,128)(2,1)S(1)}, bf16[2,144,384]{2,1,0:T(8,1...) custom-call(s32[1]{0:T(128)} %bitcast.seq, ...), custom_call_target="tpu_custom_call" | custom-call | tf_op jit(solution)/shard_map/qkv_part/pallas_call | solution.py:331
  31.2 0.7 copy-done.9
  31.8 1.3 %collective-permute-start.4 = (bf16[2,128,384]{2,1,0:T(8,128)(2,1)}, bf16[2,128,384]{2,1,0:T(8,128)(2,1)}, u32[]{:S(2)}, u32[]{:S(2)}) collective-permute-start(bf16[2,128,384]{2,1,0:T(8,128)(2,1)} %get-tuple-element.41), channel_id=1, source_target_pairs={{0,1},{1,0},{2,3},{3,2},{4,5},{5,4},{6,7},{7,6},{8,9},{9,8},{10,11... | collective-permute-start | bytes 589832 | tf_op jit(solution)/shard_map/ppermute | solution.py:460
  33.1 1.9 %constant_dynamic-slice_fusion.2 = (bf16[512,1280]{1,0:T(8,128)(2,1)S(1)}, bf16[512,1280]{1,0:T(8,128)(2,1)S(1)}) fusion(bf16[2048,1280]{1,0:T(8,128)(2,1)} %param.25, s32[]{:T(128)S(6)} %select_n.25, bf16[2048,1280]{1,0:T(8,128)(2,1)} %param.21), kind=kLoop, calls=%fused_computation.31 | loop fusion | bytes 5242884 | tf_op jit(solution)/shard_map/dynamic_slice | solution.py:509
  35.0 0.7 constant_dynamic-slice_fusion
  35.7 0.2 collective-permute-start.2
  35.9 2.3 %collective-permute-done.4 = bf16[2,128,384]{2,1,0:T(8,128)(2,1)} collective-permute-done((bf16[2,128,384]{2,1,0:T(8,128)(2,1)}, bf16[2,128,384]{2,1,0:T(8,128)(2,1)}, u32[]{:S(2)}, u32[]{:S(2)}) %collective-permute-start.4) | collective-permute-done | bytes 196640 | tf_op jit(solution)/shard_map/ppermute | solution.py:460
  38.3 1.3 %collective-permute-start.6 = (bf16[2,128,384]{2,1,0:T(8,128)(2,1)}, bf16[2,128,384]{2,1,0:T(8,128)(2,1)S(1)}, u32[]{:S(2)}, u32[]{:S(2)}) collective-permute-start(bf16[2,128,384]{2,1,0:T(8,128)(2,1)} %copy-done.13), channel_id=1, source_target_pairs={{0,1},{1,0},{2,3},{3,2},{4,5},{5,4},{6,7},{7,6},{8,9},{9,8},{10,11... | collective-permute-start | bytes 589832 | tf_op jit(solution)/shard_map/ppermute | solution.py:460
  39.5 1.0 convert_add_fusion.3
  40.5 2.4 %collective-permute-start.7 = (bf16[128,384]{1,0:T(8,128)(2,1)S(1)}, bf16[128,384]{1,0:T(8,128)(2,1)S(1)}, u32[]{:S(2)}, u32[]{:S(2)}) collective-permute-start(bf16[128,384]{1,0:T(8,128)(2,1)S(1)} %fusion.3), channel_id=1, source_target_pairs={{0,2},{1,3},{2,0},{3,1},{4,6},{5,7},{6,4},{7,5},{8,10},{9,11},{10,... | collective-permute-start | bytes 294920 | tf_op jit(solution)/shard_map/ppermute | solution.py:460
  42.9 0.0 collective-permute-done.2
  43.0 2.3 %collective-permute-start.3 = (bf16[144,384]{1,0:T(8,128)(2,1)S(1)}, bf16[144,384]{1,0:T(8,128)(2,1)S(1)}, u32[]{:S(2)}, u32[]{:S(2)}) collective-permute-start(bf16[144,384]{1,0:T(8,128)(2,1)S(1)} %fusion), channel_id=1, source_target_pairs={{0,2},{1,3},{2,0},{3,1},{4,6},{5,7},{6,4},{7,5},{8,10},{9,11},{10,... | collective-permute-start | bytes 331784 | tf_op jit(solution)/shard_map/ppermute | solution.py:460
  45.4 1.3 %collective-permute-start.5 = (bf16[2,144,384]{2,1,0:T(8,128)(2,1)}, bf16[2,144,384]{2,1,0:T(8,128)(2,1)S(1)}, u32[]{:S(2)}, u32[]{:S(2)}) collective-permute-start(bf16[2,144,384]{2,1,0:T(8,128)(2,1)} %copy-done.11), channel_id=1, source_target_pairs={{0,1},{1,0},{2,3},{3,2},{4,5},{5,4},{6,7},{7,6},{8,9},{9,8},{10,11... | collective-permute-start | bytes 663560 | tf_op jit(solution)/shard_map/ppermute | solution.py:460
  46.6 4.0 %collective-permute-done.6 = bf16[2,128,384]{2,1,0:T(8,128)(2,1)S(1)} collective-permute-done((bf16[2,128,384]{2,1,0:T(8,128)(2,1)}, bf16[2,128,384]{2,1,0:T(8,128)(2,1)S(1)}, u32[]{:S(2)}, u32[]{:S(2)}) %collective-permute-start.6) | collective-permute-done | bytes 196640 | tf_op jit(solution)/shard_map/ppermute | solution.py:460
  50.7 1.3 %collective-permute-start.12 = (bf16[128,384]{1,0:T(8,128)(2,1)S(1)}, bf16[128,384]{1,0:T(8,128)(2,1)S(1)}, u32[]{:S(2)}, u32[]{:S(2)}) collective-permute-start(bf16[128,384]{1,0:T(8,128)(2,1)S(1)} %fusion.2), channel_id=1, source_target_pairs={{0,2},{1,3},{2,0},{3,1},{4,6},{5,7},{6,4},{7,5},{8,10},{9,11},{10,... | collective-permute-start | bytes 294920 | tf_op jit(solution)/shard_map/ppermute | solution.py:460
  52.0 5.1 %collective-permute-done.5 = bf16[2,144,384]{2,1,0:T(8,128)(2,1)S(1)} collective-permute-done((bf16[2,144,384]{2,1,0:T(8,128)(2,1)}, bf16[2,144,384]{2,1,0:T(8,128)(2,1)S(1)}, u32[]{:S(2)}, u32[]{:S(2)}) %collective-permute-start.5) | collective-permute-done | bytes 221216 | tf_op jit(solution)/shard_map/ppermute | solution.py:460
  57.1 1.0 convert_add_fusion
  58.1 0.0 collective-permute-done.7.refs_3_
  58.1 0.0 collective-permute-done.3.refs_1_
  58.1 0.8 attend_part.2.refs_0_
  58.9 0.6 collective-permute-start.8
  59.5 3.6 %collective-permute-start.9 = (bf16[2,128,128]{2,1,0:T(8,128)(2,1)S(1)}, bf16[2,128,128]{2,1,0:T(8,128)(2,1)S(1)}, u32[]{:S(2)}, u32[]{:S(2)}) collective-permute-start(bf16[2,128,128]{2,1,0:T(8,128)(2,1)S(1)} %attend_part.2.refs_0_), channel_id=1, source_target_pairs={{0,2},{1,3},{2,0},{3,1},{4,6},{5,7},{6,4},{7,5},{8,10},{9,11},{10,... | collective-permute-start | bytes 196616 | tf_op jit(solution)/shard_map/ppermute | solution.py:460
  63.1 0.0 collective-permute-start.10
  63.1 1.3 %collective-permute-start.11 = (bf16[144,384]{1,0:T(8,128)(2,1)S(1)}, bf16[144,384]{1,0:T(8,128)(2,1)S(1)}, u32[]{:S(2)}, u32[]{:S(2)}) collective-permute-start(bf16[144,384]{1,0:T(8,128)(2,1)S(1)} %fusion.1), channel_id=1, source_target_pairs={{0,2},{1,3},{2,0},{3,1},{4,6},{5,7},{6,4},{7,5},{8,10},{9,11},{10,... | collective-permute-start | bytes 331784 | tf_op jit(solution)/shard_map/ppermute | solution.py:460
  64.4 0.0 collective-permute-done.12.refs_3_
  64.4 9.2 %collective-permute-done.11.refs_1_ = bf16[144,384]{1,0:T(8,128)(2,1)S(1)} collective-permute-done((bf16[144,384]{1,0:T(8,128)(2,1)S(1)}, bf16[144,384]{1,0:T(8,128)(2,1)S(1)}, u32[]{:S(2)}, u32[]{:S(2)}) %collective-permute-start.11) | collective-permute-done | bytes 110624 | tf_op jit(solution)/shard_map/ppermute | solution.py:460
  73.6 0.8 attend_part.3.refs_4_
  74.4 0.1 collective-permute-start.13
  74.4 2.0 %collective-permute-start.14 = (bf16[2,128,128]{2,1,0:T(8,128)(2,1)S(1)}, bf16[2,128,128]{2,1,0:T(8,128)(2,1)S(1)}, u32[]{:S(2)}, u32[]{:S(2)}) collective-permute-start(bf16[2,128,128]{2,1,0:T(8,128)(2,1)S(1)} %attend_part.3.refs_4_), channel_id=1, source_target_pairs={{0,2},{1,3},{2,0},{3,1},{4,6},{5,7},{6,4},{7,5},{8,10},{9,11},{10,... | collective-permute-start | bytes 196616 | tf_op jit(solution)/shard_map/ppermute | solution.py:460
  76.5 0.0 collective-permute-done.8.refs_1_
  76.5 1.5 %collective-permute-start.15 = (bf16[2,128,128]{2,1,0:T(8,128)(2,1)S(1)}, bf16[2,128,128]{2,1,0:T(8,128)(2,1)S(1)}, u32[]{:S(2)}, u32[]{:S(2)}) collective-permute-start(bf16[2,128,128]{2,1,0:T(8,128)(2,1)S(1)} %attend_part.3.refs_4_), channel_id=1, source_target_pairs={{0,3},{1,2},{2,1},{3,0},{4,7},{5,6},{6,5},{7,4},{8,11},{9,10},{10,... | collective-permute-start | bytes 196616 | tf_op jit(solution)/shard_map/ppermute | solution.py:460
  78.0 0.5 collective-permute-done.14.refs_6_
  78.5 3.2 %collective-permute-done.15.refs_7_ = bf16[2,128,128]{2,1,0:T(8,128)(2,1)S(1)} collective-permute-done((bf16[2,128,128]{2,1,0:T(8,128)(2,1)S(1)}, bf16[2,128,128]{2,1,0:T(8,128)(2,1)S(1)}, u32[]{:S(2)}, u32[]{:S(2)}) %collective-permute-start.15) | collective-permute-done | bytes 65568 | tf_op jit(solution)/shard_map/ppermute | solution.py:460
  81.7 1.0 out_part.1
  82.7 3.4 %collective-permute-start.16 = (bf16[128,640]{1,0:T(8,128)(2,1)S(1)}, bf16[128,640]{1,0:T(8,128)(2,1)S(1)}, u32[]{:S(2)}, u32[]{:S(2)}) collective-permute-start(bf16[128,640]{1,0:T(8,128)(2,1)S(1)} %get-tuple-element.53), channel_id=1, source_target_pairs={{0,8},{8,0},{16,24},{24,16},{1,9},{9,1},{17,25},{25,17},{2,10},{10... | collective-permute-start | bytes 491528 | tf_op jit(solution)/shard_map/ppermute | solution.py:460
  86.1 1.0 collective-permute-done.16
  87.2 1.4 %collective-permute-start.19 = (bf16[128,640]{1,0:T(8,128)(2,1)S(1)}, bf16[128,640]{1,0:T(8,128)(2,1)S(1)}, u32[]{:S(2)}, u32[]{:S(2)}) collective-permute-start(bf16[128,640]{1,0:T(8,128)(2,1)S(1)} %add_convert_fusion), channel_id=1, source_target_pairs={{0,20},{4,16},{8,28},{12,24},{16,4},{20,0},{24,12},{28,8},{1,21},{... | collective-permute-start | bytes 491528 | tf_op jit(solution)/shard_map/ppermute | solution.py:530
  88.5 0.2 collective-permute-start.18
  88.7 1.1 %collective-permute-start.17 = (bf16[128,640]{1,0:T(8,128)(2,1)S(1)}, bf16[128,640]{1,0:T(8,128)(2,1)S(1)}, u32[]{:S(2)}, u32[]{:S(2)}) collective-permute-start(bf16[128,640]{1,0:T(8,128)(2,1)S(1)} %add_convert_fusion), channel_id=1, source_target_pairs={{0,4},{4,0},{1,5},{5,1},{2,6},{6,2},{3,7},{7,3},{8,12},{12,8},{9,1... | collective-permute-start | bytes 491528 | tf_op jit(solution)/shard_map/ppermute | solution.py:460
  89.9 3.7 %collective-permute-done.19 = bf16[128,640]{1,0:T(8,128)(2,1)S(1)} collective-permute-done((bf16[128,640]{1,0:T(8,128)(2,1)S(1)}, bf16[128,640]{1,0:T(8,128)(2,1)S(1)}, u32[]{:S(2)}, u32[]{:S(2)}) %collective-permute-start.19) | collective-permute-done | bytes 163872 | tf_op jit(solution)/shard_map/ppermute | solution.py:530
  93.6 4.2 %collective-permute-done.18 = bf16[128,640]{1,0:T(8,128)(2,1)S(1)} collective-permute-done((bf16[128,640]{1,0:T(8,128)(2,1)S(1)}, bf16[128,640]{1,0:T(8,128)(2,1)S(1)}, u32[]{:S(2)}, u32[]{:S(2)}) %collective-permute-start.18) | collective-permute-done | bytes 163872 | tf_op jit(solution)/shard_map/ppermute | solution.py:460
  97.8 0.1 multiply_convert_fusion.rows
  97.9 0.7 collective-permute-start.20
  98.5 1.3 %copy.17 = bf16[128,2048]{0,1:T(8,128)(2,1)S(1)} copy(bf16[128,2048]{1,0:T(8,128)(2,1)} %heads.1) | data formatting | bytes 1048576 | tf_op args[0]
  99.8 2.1 %grad_part.2.refs_0_ = bf16[2048,1280]{1,0:T(8,128)(2,1)} custom-call(s32[1]{0:T(128)} %bitcast.1.core.half, bf16[2048,128]{1,0:T(8,128)(2,1)S(1)} %bitcast.26, bf16[128,640]{1,0:T(8,128)(2,1)S(1)} %multiply_convert_fusion.rows), custom_call_target="tpu_custom_call" | custom-call | tf_op jit(solution)/shard_map/grad_part/pallas_call | solution.py:449
  101.9 0.0 collective-permute-done.20.rows
  101.9 2.0 %grad_part.3 = bf16[2048,1280]{1,0:T(8,128)(2,1)} custom-call(s32[1]{0:T(128)S(6)} %sub.3.half, bf16[2048,128]{1,0:T(8,128)(2,1)S(1)} %bitcast.27, bf16[128,640]{1,0:T(8,128)(2,1)S(1)} %collective-permute-done.20.rows, bf16[2048,1280]{1,0:T(8,128)(2,1)} %grad_part.2.refs_0_), custom_call_target="tpu_custom_call", output_to_operand_aliasing={{}: (3, {})} | custom-call | tf_op jit(solution)/shard_map/grad_part/pallas_call | solution.py:449
  (41 shorter events, 0.3 us)
Async XLA Ops:
  6.7 11.9 %collective-permute-start = (bf16[192,640]{1,0:T(8,128)(2,1)}, bf16[192,640]{1,0:T(8,128)(2,1)}, u32[]{:S(2)}, u32[]{:S(2)}) collective-permute-start(bf16[192,640]{1,0:T(8,128)(2,1)} %get-tuple-element.29), channel_id=1, source_target_pairs={{0,4},{4,0},{1,5},{5,1},{2,6},{6,2},{3,7},{7,3},{8,12},{12,8},{9,1... | collective-permute-start | bytes 737288 | tf_op jit(solution)/shard_map/ppermute | solution.py:460
  8.8 9.0 %copy-start.4 = (bf16[256,1280]{1,0:T(8,128)(2,1)S(1)}, bf16[256,1280]{1,0:T(8,128)(2,1)}, u32[]{:S(2)}) copy-start(bf16[256,1280]{1,0:T(8,128)(2,1)} %time_w.3) | copy-start | bytes 1966084
  8.8 9.0 %copy-start.5 = (bf16[256,3,1280]{2,0,1:T(8,128)(2,1)S(1)}, bf16[256,3,1280]{2,0,1:T(8,128)(2,1)}, u32[]{:S(2)}) copy-start(bf16[256,3,1280]{2,0,1:T(8,128)(2,1)} %param.22) | copy-start | bytes 5898244
  8.8 9.0 %copy-start.6 = (bf16[256,3,1280]{2,0,1:T(8,128)(2,1)S(1)}, bf16[256,3,1280]{2,0,1:T(8,128)(2,1)}, u32[]{:S(2)}) copy-start(bf16[256,3,1280]{2,0,1:T(8,128)(2,1)} %param.26) | copy-start | bytes 5898244
  8.8 9.0 %copy-start.7 = (f32[128,640]{1,0:T(8,128)S(1)}, f32[128,640]{1,0:T(8,128)}, u32[]{:S(2)}) copy-start(f32[128,640]{1,0:T(8,128)} %get-tuple-element.28.after.full) | copy-start | bytes 983044
  8.8 9.0 %copy-start.10 = (bf16[8,256]{1,0:T(8,128)(2,1)S(1)}, bf16[8,256]{1,0:T(8,128)(2,1)}, u32[]{:S(2)}) copy-start(bf16[8,256]{1,0:T(8,128)(2,1)} %fusion.6.embed) | copy-start | bytes 12292
  17.8 2.2 %copy-start = (bf16[3,1280,512]{2,1,0:T(8,128)(2,1)}, bf16[3,1280,512]{2,1,0:T(8,128)(2,1)S(1)}, u32[]{:S(2)}) copy-start(bf16[3,1280,512]{2,1,0:T(8,128)(2,1)S(1)} %get-tuple-element.56.after_c.weight_b) | copy-start | bytes 11796484
  17.8 3.2 %copy-start.2 = (bf16[3,1280,512]{2,1,0:T(8,128)(2,1)}, bf16[3,1280,512]{2,1,0:T(8,128)(2,1)S(1)}, u32[]{:S(2)}) copy-start(bf16[3,1280,512]{2,1,0:T(8,128)(2,1)S(1)} %get-tuple-element.57.after_b.weight_a) | copy-start | bytes 11796484
  18.5 3.4 %copy-start.14 = (s32[3]{0:T(128)S(1)}, s32[3]{0:T(128)}, u32[]{:S(2)}) copy-start(s32[3]{0:T(128)} %param.19) | copy-start | bytes 40
  18.5 4.5 %copy-start.8 = (bf16[64,1280]{1,0:T(8,128)(2,1)S(1)}, bf16[64,1280]{1,0:T(8,128)(2,1)}, u32[]{:S(2)}) copy-start(bf16[64,1280]{1,0:T(8,128)(2,1)} %noise.3) | copy-start | bytes 491524
  21.0 2.1 %collective-permute-start.1 = (bf16[192,640]{1,0:T(8,128)(2,1)S(1)}, bf16[192,640]{1,0:T(8,128)(2,1)S(1)}, u32[]{:S(2)}, u32[]{:S(2)}) collective-permute-start(bf16[192,640]{1,0:T(8,128)(2,1)S(1)} %join_part.1.joined), channel_id=1, source_target_pairs={{0,8},{8,0},{16,24},{24,16},{1,9},{9,1},{17,25},{25,17},{2,10},{10... | collective-permute-start | bytes 737288 | tf_op jit(solution)/shard_map/ppermute | solution.py:460
  23.1 2.1 %copy-start.1 = (bf16[3,1280,512]{2,1,0:T(8,128)(2,1)S(1)}, bf16[3,1280,512]{2,1,0:T(8,128)(2,1)}, u32[]{:S(2)}) copy-start(bf16[3,1280,512]{2,1,0:T(8,128)(2,1)} %copy-done) | copy-start | bytes 11796484
  25.2 2.1 %copy-start.3 = (bf16[3,1280,512]{2,1,0:T(8,128)(2,1)S(1)}, bf16[3,1280,512]{2,1,0:T(8,128)(2,1)}, u32[]{:S(2)}) copy-start(bf16[3,1280,512]{2,1,0:T(8,128)(2,1)} %copy-done.2) | copy-start | bytes 11796484
  31.2 0.7 copy-start.9
  31.2 2.0 %copy-start.11 = (bf16[2,144,384]{2,1,0:T(8,128)(2,1)}, bf16[2,144,384]{2,1,0:T(8,128)(2,1)S(1)}, u32[]{:S(2)}) copy-start(bf16[2,144,384]{2,1,0:T(8,128)(2,1)S(1)} %get-tuple-element.44) | copy-start | bytes 663556
  31.2 2.0 %copy-start.12 = (bf16[2,144,384]{2,1,0:T(8,128)(2,1)}, bf16[2,144,384]{2,1,0:T(8,128)(2,1)S(1)}, u32[]{:S(2)}) copy-start(bf16[2,144,384]{2,1,0:T(8,128)(2,1)S(1)} %get-tuple-element.36) | copy-start | bytes 663556
  31.2 2.0 %copy-start.13 = (bf16[2,128,384]{2,1,0:T(8,128)(2,1)}, bf16[2,128,384]{2,1,0:T(8,128)(2,1)S(1)}, u32[]{:S(2)}) copy-start(bf16[2,128,384]{2,1,0:T(8,128)(2,1)S(1)} %get-tuple-element.46) | copy-start | bytes 589828
  31.8 6.4 %collective-permute-start.4 = (bf16[2,128,384]{2,1,0:T(8,128)(2,1)}, bf16[2,128,384]{2,1,0:T(8,128)(2,1)}, u32[]{:S(2)}, u32[]{:S(2)}) collective-permute-start(bf16[2,128,384]{2,1,0:T(8,128)(2,1)} %get-tuple-element.41), channel_id=1, source_target_pairs={{0,1},{1,0},{2,3},{3,2},{4,5},{5,4},{6,7},{7,6},{8,9},{9,8},{10,11... | collective-permute-start | bytes 589832 | tf_op jit(solution)/shard_map/ppermute | solution.py:460
  35.7 7.2 %collective-permute-start.2 = (bf16[2,144,384]{2,1,0:T(8,128)(2,1)}, bf16[2,144,384]{2,1,0:T(8,128)(2,1)S(1)}, u32[]{:S(2)}, u32[]{:S(2)}) collective-permute-start(bf16[2,144,384]{2,1,0:T(8,128)(2,1)} %copy-done.12), channel_id=1, source_target_pairs={{0,1},{1,0},{2,3},{3,2},{4,5},{5,4},{6,7},{7,6},{8,9},{9,8},{10,11... | collective-permute-start | bytes 663560 | tf_op jit(solution)/shard_map/ppermute | solution.py:460
  38.3 12.4 %collective-permute-start.6 = (bf16[2,128,384]{2,1,0:T(8,128)(2,1)}, bf16[2,128,384]{2,1,0:T(8,128)(2,1)S(1)}, u32[]{:S(2)}, u32[]{:S(2)}) collective-permute-start(bf16[2,128,384]{2,1,0:T(8,128)(2,1)} %copy-done.13), channel_id=1, source_target_pairs={{0,1},{1,0},{2,3},{3,2},{4,5},{5,4},{6,7},{7,6},{8,9},{9,8},{10,11... | collective-permute-start | bytes 589832 | tf_op jit(solution)/shard_map/ppermute | solution.py:460
  40.5 17.6 %collective-permute-start.7 = (bf16[128,384]{1,0:T(8,128)(2,1)S(1)}, bf16[128,384]{1,0:T(8,128)(2,1)S(1)}, u32[]{:S(2)}, u32[]{:S(2)}) collective-permute-start(bf16[128,384]{1,0:T(8,128)(2,1)S(1)} %fusion.3), channel_id=1, source_target_pairs={{0,2},{1,3},{2,0},{3,1},{4,6},{5,7},{6,4},{7,5},{8,10},{9,11},{10,... | collective-permute-start | bytes 294920 | tf_op jit(solution)/shard_map/ppermute | solution.py:460
  43.0 15.1 %collective-permute-start.3 = (bf16[144,384]{1,0:T(8,128)(2,1)S(1)}, bf16[144,384]{1,0:T(8,128)(2,1)S(1)}, u32[]{:S(2)}, u32[]{:S(2)}) collective-permute-start(bf16[144,384]{1,0:T(8,128)(2,1)S(1)} %fusion), channel_id=1, source_target_pairs={{0,2},{1,3},{2,0},{3,1},{4,6},{5,7},{6,4},{7,5},{8,10},{9,11},{10,... | collective-permute-start | bytes 331784 | tf_op jit(solution)/shard_map/ppermute | solution.py:460
  45.4 11.7 %collective-permute-start.5 = (bf16[2,144,384]{2,1,0:T(8,128)(2,1)}, bf16[2,144,384]{2,1,0:T(8,128)(2,1)S(1)}, u32[]{:S(2)}, u32[]{:S(2)}) collective-permute-start(bf16[2,144,384]{2,1,0:T(8,128)(2,1)} %copy-done.11), channel_id=1, source_target_pairs={{0,1},{1,0},{2,3},{3,2},{4,5},{5,4},{6,7},{7,6},{8,9},{9,8},{10,11... | collective-permute-start | bytes 663560 | tf_op jit(solution)/shard_map/ppermute | solution.py:460
  50.7 13.7 %collective-permute-start.12 = (bf16[128,384]{1,0:T(8,128)(2,1)S(1)}, bf16[128,384]{1,0:T(8,128)(2,1)S(1)}, u32[]{:S(2)}, u32[]{:S(2)}) collective-permute-start(bf16[128,384]{1,0:T(8,128)(2,1)S(1)} %fusion.2), channel_id=1, source_target_pairs={{0,2},{1,3},{2,0},{3,1},{4,6},{5,7},{6,4},{7,5},{8,10},{9,11},{10,... | collective-permute-start | bytes 294920 | tf_op jit(solution)/shard_map/ppermute | solution.py:460
  58.9 17.5 %collective-permute-start.8 = (bf16[2,128,128]{2,1,0:T(8,128)(2,1)S(1)}, bf16[2,128,128]{2,1,0:T(8,128)(2,1)S(1)}, u32[]{:S(2)}, u32[]{:S(2)}) collective-permute-start(bf16[2,128,128]{2,1,0:T(8,128)(2,1)S(1)} %attend_part.2.refs_0_), channel_id=1, source_target_pairs={{0,1},{1,0},{2,3},{3,2},{4,5},{5,4},{6,7},{7,6},{8,9},{9,8},{10,11... | collective-permute-start | bytes 196616 | tf_op jit(solution)/shard_map/ppermute | solution.py:460
  59.5 18.5 %collective-permute-start.9 = (bf16[2,128,128]{2,1,0:T(8,128)(2,1)S(1)}, bf16[2,128,128]{2,1,0:T(8,128)(2,1)S(1)}, u32[]{:S(2)}, u32[]{:S(2)}) collective-permute-start(bf16[2,128,128]{2,1,0:T(8,128)(2,1)S(1)} %attend_part.2.refs_0_), channel_id=1, source_target_pairs={{0,2},{1,3},{2,0},{3,1},{4,6},{5,7},{6,4},{7,5},{8,10},{9,11},{10,... | collective-permute-start | bytes 196616 | tf_op jit(solution)/shard_map/ppermute | solution.py:460
  63.1 14.9 %collective-permute-start.10 = (bf16[2,128,128]{2,1,0:T(8,128)(2,1)S(1)}, bf16[2,128,128]{2,1,0:T(8,128)(2,1)S(1)}, u32[]{:S(2)}, u32[]{:S(2)}) collective-permute-start(bf16[2,128,128]{2,1,0:T(8,128)(2,1)S(1)} %attend_part.2.refs_0_), channel_id=1, source_target_pairs={{0,3},{1,2},{2,1},{3,0},{4,7},{5,6},{6,5},{7,4},{8,11},{9,10},{10,... | collective-permute-start | bytes 196616 | tf_op jit(solution)/shard_map/ppermute | solution.py:460
  63.1 10.5 %collective-permute-start.11 = (bf16[144,384]{1,0:T(8,128)(2,1)S(1)}, bf16[144,384]{1,0:T(8,128)(2,1)S(1)}, u32[]{:S(2)}, u32[]{:S(2)}) collective-permute-start(bf16[144,384]{1,0:T(8,128)(2,1)S(1)} %fusion.1), channel_id=1, source_target_pairs={{0,2},{1,3},{2,0},{3,1},{4,6},{5,7},{6,4},{7,5},{8,10},{9,11},{10,... | collective-permute-start | bytes 331784 | tf_op jit(solution)/shard_map/ppermute | solution.py:460
  74.4 3.6 %collective-permute-start.13 = (bf16[2,128,128]{2,1,0:T(8,128)(2,1)S(1)}, bf16[2,128,128]{2,1,0:T(8,128)(2,1)S(1)}, u32[]{:S(2)}, u32[]{:S(2)}) collective-permute-start(bf16[2,128,128]{2,1,0:T(8,128)(2,1)S(1)} %attend_part.3.refs_4_), channel_id=1, source_target_pairs={{0,1},{1,0},{2,3},{3,2},{4,5},{5,4},{6,7},{7,6},{8,9},{9,8},{10,11... | collective-permute-start | bytes 196616 | tf_op jit(solution)/shard_map/ppermute | solution.py:460
  74.4 4.1 %collective-permute-start.14 = (bf16[2,128,128]{2,1,0:T(8,128)(2,1)S(1)}, bf16[2,128,128]{2,1,0:T(8,128)(2,1)S(1)}, u32[]{:S(2)}, u32[]{:S(2)}) collective-permute-start(bf16[2,128,128]{2,1,0:T(8,128)(2,1)S(1)} %attend_part.3.refs_4_), channel_id=1, source_target_pairs={{0,2},{1,3},{2,0},{3,1},{4,6},{5,7},{6,4},{7,5},{8,10},{9,11},{10,... | collective-permute-start | bytes 196616 | tf_op jit(solution)/shard_map/ppermute | solution.py:460
  76.5 5.2 %collective-permute-start.15 = (bf16[2,128,128]{2,1,0:T(8,128)(2,1)S(1)}, bf16[2,128,128]{2,1,0:T(8,128)(2,1)S(1)}, u32[]{:S(2)}, u32[]{:S(2)}) collective-permute-start(bf16[2,128,128]{2,1,0:T(8,128)(2,1)S(1)} %attend_part.3.refs_4_), channel_id=1, source_target_pairs={{0,3},{1,2},{2,1},{3,0},{4,7},{5,6},{6,5},{7,4},{8,11},{9,10},{10,... | collective-permute-start | bytes 196616 | tf_op jit(solution)/shard_map/ppermute | solution.py:460
  82.7 4.4 %collective-permute-start.16 = (bf16[128,640]{1,0:T(8,128)(2,1)S(1)}, bf16[128,640]{1,0:T(8,128)(2,1)S(1)}, u32[]{:S(2)}, u32[]{:S(2)}) collective-permute-start(bf16[128,640]{1,0:T(8,128)(2,1)S(1)} %get-tuple-element.53), channel_id=1, source_target_pairs={{0,8},{8,0},{16,24},{24,16},{1,9},{9,1},{17,25},{25,17},{2,10},{10... | collective-permute-start | bytes 491528 | tf_op jit(solution)/shard_map/ppermute | solution.py:460
  87.2 6.4 %collective-permute-start.19 = (bf16[128,640]{1,0:T(8,128)(2,1)S(1)}, bf16[128,640]{1,0:T(8,128)(2,1)S(1)}, u32[]{:S(2)}, u32[]{:S(2)}) collective-permute-start(bf16[128,640]{1,0:T(8,128)(2,1)S(1)} %add_convert_fusion), channel_id=1, source_target_pairs={{0,20},{4,16},{8,28},{12,24},{16,4},{20,0},{24,12},{28,8},{1,21},{... | collective-permute-start | bytes 491528 | tf_op jit(solution)/shard_map/ppermute | solution.py:530
  88.5 9.2 %collective-permute-start.18 = (bf16[128,640]{1,0:T(8,128)(2,1)S(1)}, bf16[128,640]{1,0:T(8,128)(2,1)S(1)}, u32[]{:S(2)}, u32[]{:S(2)}) collective-permute-start(bf16[128,640]{1,0:T(8,128)(2,1)S(1)} %add_convert_fusion), channel_id=1, source_target_pairs={{0,16},{8,24},{16,0},{24,8},{1,17},{9,25},{17,1},{25,9},{2,18},{10... | collective-permute-start | bytes 491528 | tf_op jit(solution)/shard_map/ppermute | solution.py:460
  88.7 9.0 %collective-permute-start.17 = (bf16[128,640]{1,0:T(8,128)(2,1)S(1)}, bf16[128,640]{1,0:T(8,128)(2,1)S(1)}, u32[]{:S(2)}, u32[]{:S(2)}) collective-permute-start(bf16[128,640]{1,0:T(8,128)(2,1)S(1)} %add_convert_fusion), channel_id=1, source_target_pairs={{0,4},{4,0},{1,5},{5,1},{2,6},{6,2},{3,7},{7,3},{8,12},{12,8},{9,1... | collective-permute-start | bytes 491528 | tf_op jit(solution)/shard_map/ppermute | solution.py:460
  97.9 4.0 %collective-permute-start.20 = (bf16[128,640]{1,0:T(8,128)(2,1)S(1)}, bf16[128,640]{1,0:T(8,128)(2,1)S(1)}, u32[]{:S(2)}, u32[]{:S(2)}) collective-permute-start(bf16[128,640]{1,0:T(8,128)(2,1)S(1)} %multiply_convert_fusion.rows), channel_id=1, source_target_pairs={{0,8},{8,0},{16,24},{24,16},{1,9},{9,1},{17,25},{25,17},{2,10},{10... | collective-permute-start | bytes 491528 | tf_op jit(solution)/shard_map/ppermute | solution.py:460
